TPU v7x, 32 devices: a whole 2x2x4 slice. The times are simulated.
32 devices in a mesh: groups: 2 (over y), row: 4 (over x, core), col: 4 (over z).
Axes of the slice: x: 2, y: 2, z: 4, core: 2. Of those that a mesh axis runs over, the one named last changes fastest.
Arguments:
- blocks: bfloat16 [4096, 8192], P('row', 'col'), may hold values from -0.15625 to 0.15625
- tile_map: int32 [8, 16], P('row', 'col'), may hold values from 0 to 1, as said below
- lower_bound: float32 [8192], P('col'), may hold values from -1.5 to -0.2
- upper_bound: float32 [8192], P('col'), may hold values from 0.2 to 1.5
- bound_code: int32 [8192], P('col'), may hold values from 0 to 3
- row_kind: int32 [4096], P('row'), may hold values from 0 to 1
- cost_vector: float32 [8192], P('col'), may hold values from -6 to 6
- right_side: float32 [4096, 512], P('row', 'groups'), parts along dimension 1, may hold values from -6 to 6
- primal_start: float32 [8192, 512], P('col', 'groups'), parts along dimension 1, may hold values from -6 to 6
- dual_start: float32 [4096, 512], P('row', 'groups'), parts along dimension 1, may hold values from -6 to 6
- primal_weight: float32 [512], P('groups'), parts along dimension 0, may hold values from 0.5 to 2
Outputs:
- primal_final: float32 [8192, 512], P('col', 'groups'), parts along dimension 1
- dual_final: float32 [4096, 512], P('row', 'groups'), parts along dimension 1
There are 2 independent parts, one for each index of `groups`. A program takes and returns all parts, laid end to end along the dimension named above; an argument that names none is the same for every part. Nothing has to cross between parts.
Inputs may be any that keep to these rules, and one draw needn't show every extreme that they name: `tile_map`: block row i has its block on the line j = i * 2 nonzero, the blocks one column away from that line mostly nonzero, and few nonzero blocks elsewhere.
All inputs are finite; a program needn't handle non-finite values.
Results may differ from a plain program's by a relative error of at most 0.0025.
Values may be sent and summed in bfloat16 or wider, within the bound.
No kernel may reach another device: no remote copies, remote signals or barrier semaphores. Data moves between devices by JAX's collectives and lax.ppermute only.
A program may use at most 64 MiB of HBM per device.

v0:
```python
import jax
import jax.numpy as jnp
from jax import lax
from jax.sharding import PartitionSpec as P

ITERS = 3


step_scale = 0.5


def project_primal(values, lower_bound, upper_bound, bound_code):
    low_on = ((bound_code == 1) | (bound_code == 3))[:, None]
    high_on = ((bound_code == 2) | (bound_code == 3))[:, None]
    values = jnp.where(low_on, jnp.maximum(values, lower_bound[:, None]), values)
    return jnp.where(high_on, jnp.minimum(values, upper_bound[:, None]), values)


def project_dual(values, row_kind):
    return jnp.where((row_kind == 1)[:, None], jnp.maximum(values, 0.0), values)


def transpose_product(matrix, vector):
    return lax.dot_general(
        matrix, vector, (((0,), (0,)), ((), ())), preferred_element_type=jnp.float32
    )


def local(
    blocks,
    tile_map,
    lower_bound,
    upper_bound,
    bound_code,
    row_kind,
    cost_vector,
    right_side,
    primal_start,
    dual_start,
    primal_weight,
):
    tile_rows = blocks.shape[0] // tile_map.shape[0]
    tile_cols = blocks.shape[1] // tile_map.shape[1]
    mask_full = jnp.repeat(jnp.repeat(tile_map, tile_rows, axis=0), tile_cols, axis=1)
    masked = blocks * mask_full.astype(jnp.bfloat16)
    rows_dev = blocks.shape[0]
    cols_dev = blocks.shape[1]
    total_vars = cols_dev * lax.axis_size("col")
    total_rows = rows_dev * lax.axis_size("row")
    weight_now = primal_weight
    primal = primal_start
    dual = dual_start
    for iteration in range(ITERS):
        primal_step = step_scale / weight_now
        dual_step = step_scale * weight_now
        partial_t = transpose_product(masked, dual.astype(jnp.bfloat16))
        image_t = lax.psum(partial_t, "row")
        primal_next = project_primal(
            primal - primal_step[None, :] * (cost_vector[:, None] - image_t),
            lower_bound,
            upper_bound,
            bound_code,
        )
        extrapolated = (2.0 * primal_next - primal).astype(jnp.bfloat16)
        partial_image = jnp.dot(masked, extrapolated, preferred_element_type=jnp.float32)
        image = lax.psum(partial_image, "col")
        dual_next = project_dual(dual + dual_step[None, :] * (right_side - image), row_kind)
        if iteration + 1 < ITERS:
            sum_x = lax.psum(jnp.sum((primal_next - primal) ** 2, axis=0), "col")
            sum_y = lax.psum(jnp.sum((dual_next - dual) ** 2, axis=0), "row")
            move_x = jnp.sqrt(sum_x / total_vars + 1e-06)
            move_y = jnp.sqrt(sum_y / total_rows + 1e-06)
            weight_now = jnp.sqrt(weight_now * move_y / move_x)
        primal = primal_next
        dual = dual_next
    return (primal, dual)


def solution(mesh):
    return jax.shard_map(
        local,
        mesh=mesh,
        in_specs=(
            P("row", "col"),
            P("row", "col"),
            P("col"),
            P("col"),
            P("col"),
            P("row"),
            P("col"),
            P("row", "groups"),
            P("col", "groups"),
            P("row", "groups"),
            P("groups"),
        ),
        out_specs=(P("col", "groups"), P("row", "groups")),
        check_vma=False,
    )
```

profile of v0, /device:TPU:5, one launch (start us, length us, event | category | flops | bytes accessed | tf_op | source)
XLA Modules:
  0.0 373.8 jit_solution(11418805638507890548)
XLA Ops:
  11.5 2.3 mul.76
  13.8 1.9 copy-done
  15.8 2.7 fusion.10
  18.6 52.6 %all-reduce.7.cloned.1.call-done = f32[2048,256]{1,0:T(8,128)} async-done(((f32[2048,256]{1,0:T(8,128)}), f32[2048,256]{1,0:T(8,128)}) %all-reduce.7.cloned.1.call-update) | async-done | bytes 2097168 | tf_op jit(solution)/shard_map/psum | solution.py:57
  71.2 3.8 %multiply_reduce_fusion.1 = (f32[256]{0:T(256)S(1)}, f32[2048,256]{1,0:T(8,128)S(1)}) fusion(f32[2048,256]{1,0:T(8,128)S(1)} %copy-done.9, f32[2048]{0:T(1024)S(1)} %copy-done.15, f32[2048]{0:T(1024)S(1)} %copy-done.16, f32[2048,256]{1,0:T(8,128)} %all-reduce.7.cloned.1.call-done, f32[2048]{0:T(1024)S(1)} %copy-done.17, f32[256]{0:T(256)S(1)} %get-tuple-element.17, ...), kind=kLoop, calls=%fused_computation.9 | loop fusion | flops 5242624 | bytes 6322176 | tf_op jit(solution)/shard_map/reduce_sum | solution.py:69
  76.3 2.3 fusion
  78.7 52.3 %all-reduce.9.cloned.1.call-done = f32[1024,256]{1,0:T(8,128)} async-done(((f32[1024,256]{1,0:T(8,128)}), f32[1024,256]{1,0:T(8,128)}) %all-reduce.9.cloned.1.call-update) | async-done | bytes 1048592 | tf_op jit(solution)/shard_map/psum | solution.py:66
  131.0 2.0 multiply_reduce_fusion.3
  134.0 2.7 fusion.8
  136.8 8.1 %psum.73 = f32[256]{0:T(256)S(1)} all-reduce(f32[256]{0:T(256)S(1)} %get-tuple-element.12), channel_id=1, replica_groups=mesh['groups'=2,'row'=4,'col'=4] {'col'}, use_global_device_ids=true, to_apply=%region_5.6 | all-reduce | flops 256 | bytes 2048 | tf_op jit(solution)/shard_map/psum | solution.py:69
  144.9 7.8 %psum.72 = f32[256]{0:T(256)S(1)} all-reduce(f32[256]{0:T(256)S(1)} %get-tuple-element.10), channel_id=1, replica_groups=mesh['groups'=2,'row'=4,'col'=4] {'row'}, use_global_device_ids=true, to_apply=%region_3.4 | all-reduce | flops 256 | bytes 2048 | tf_op jit(solution)/shard_map/psum | solution.py:70
  152.7 34.8 %all-reduce.11.cloned.1.call-done = f32[2048,256]{1,0:T(8,128)} async-done(((f32[2048,256]{1,0:T(8,128)}), f32[2048,256]{1,0:T(8,128)}) %all-reduce.11.cloned.1.call-update) | async-done | bytes 2097168 | tf_op jit(solution)/shard_map/psum | solution.py:57
  187.5 5.7 %multiply_reduce_fusion = (f32[256]{0:T(256)S(1)}, f32[2048,256]{1,0:T(8,128)S(1)}) fusion(f32[2048,256]{1,0:T(8,128)} %copy-done.6, f32[2048]{0:T(1024)S(1)} %copy-done.15, f32[2048]{0:T(1024)S(1)} %copy-done.16, f32[2048,256]{1,0:T(8,128)} %all-reduce.11.cloned.1.call-done, f32[2048]{0:T(1024)S(1)} %copy-done.17, f32[256]{0:T(256)S(1)} %broadcast_divide_fusion.1, ...), kind=kLoop, calls=%fused_computation.7 | loop fusion | flops 5242624 | bytes 6322176 | tf_op jit(solution)/shard_map/reduce_sum | solution.py:69
  193.2 2.3 fusion.1
  195.7 52.1 %all-reduce.13.cloned.1.call-done = f32[1024,256]{1,0:T(8,128)} async-done(((f32[1024,256]{1,0:T(8,128)}), f32[1024,256]{1,0:T(8,128)}) %all-reduce.13.cloned.1.call-update) | async-done | bytes 1048592 | tf_op jit(solution)/shard_map/psum | solution.py:66
  247.9 2.0 multiply_reduce_fusion.2
  250.9 2.7 fusion.6
  253.6 8.1 %psum.77 = f32[256]{0:T(256)S(1)} all-reduce(f32[256]{0:T(256)S(1)} %get-tuple-element.6), channel_id=1, replica_groups=mesh['groups'=2,'row'=4,'col'=4] {'col'}, use_global_device_ids=true, to_apply=%region_11.12 | all-reduce | flops 256 | bytes 2048 | tf_op jit(solution)/shard_map/psum | solution.py:69
  261.7 7.8 %psum.76 = f32[256]{0:T(256)S(1)} all-reduce(f32[256]{0:T(256)S(1)} %get-tuple-element.4), channel_id=1, replica_groups=mesh['groups'=2,'row'=4,'col'=4] {'row'}, use_global_device_ids=true, to_apply=%region_9.10 | all-reduce | flops 256 | bytes 2048 | tf_op jit(solution)/shard_map/psum | solution.py:70
  269.6 34.8 %all-reduce.15.cloned.1.call-done = f32[2048,256]{1,0:T(8,128)} async-done(((f32[2048,256]{1,0:T(8,128)}), f32[2048,256]{1,0:T(8,128)}) %all-reduce.15.cloned.1.call-update) | async-done | bytes 2097168 | tf_op jit(solution)/shard_map/psum | solution.py:57
  304.4 3.8 %minimum_select_fusion = f32[2048,256]{1,0:T(8,128)S(1)} fusion(f32[2048,256]{1,0:T(8,128)S(1)} %get-tuple-element.7, f32[2048,256]{1,0:T(8,128)} %all-reduce.15.cloned.1.call-done, f32[256]{0:T(256)S(1)} %broadcast_divide_fusion, f32[2048]{0:T(1024)S(1)} %copy-done.15, f32[2048]{0:T(1024)S(1)} %copy-done.16, f32[2048]{0:T(1024)S(1)} %copy-done.17, ...), kind=kLoop, calls=%fused_computation | loop fusion | flops 3670016 | bytes 6321152 | tf_op jit(solution)/shard_map/jit(_where)/select_n | solution.py:16
  309.5 2.3 fusion.2
  311.8 52.3 %all-reduce.17.cloned.1.call-done = f32[1024,256]{1,0:T(8,128)} async-done(((f32[1024,256]{1,0:T(8,128)}), f32[1024,256]{1,0:T(8,128)}) %all-reduce.17.cloned.1.call-update) | async-done | bytes 1048592 | tf_op jit(solution)/shard_map/psum | solution.py:66
  364.2 2.8 maximum_select_fusion.3
  (64 shorter events, 9.5 us)
Async XLA Ops:
  7.2 64.0 %all-reduce.7.cloned.1.call-start = ((), (), s32[]{:S(2)}) async-start(), calls=%async_computation | async-start | bytes 4194304 | tf_op jit(solution)/shard_map/psum | solution.py:57
  9.3 2.2 copy-start.11
  11.5 4.2 %copy-start.14 = (f32[1024,256]{1,0:T(8,128)S(1)}, f32[1024,256]{1,0:T(8,128)}, u32[]{:S(2)}) copy-start(f32[1024,256]{1,0:T(8,128)} %param.20) | copy-start | bytes 3145732
  13.8 1.9 copy-start
  15.8 2.8 copy-start.19
  15.8 2.8 copy-start.18
  18.5 52.7 %copy-start.9 = (f32[2048,256]{1,0:T(8,128)S(1)}, f32[2048,256]{1,0:T(8,128)}, u32[]{:S(2)}) copy-start(f32[2048,256]{1,0:T(8,128)} %param.19) | copy-start | bytes 6291460
  18.5 52.7 %copy-start.15 = (f32[2048]{0:T(1024)S(1)}, f32[2048]{0:T(1024)}, u32[]{:S(2)}) copy-start(f32[2048]{0:T(1024)} %param.14) | copy-start | bytes 24580
  18.5 52.7 %copy-start.16 = (f32[2048]{0:T(1024)S(1)}, f32[2048]{0:T(1024)}, u32[]{:S(2)}) copy-start(f32[2048]{0:T(1024)} %param.13) | copy-start | bytes 24580
  18.5 52.7 %copy-start.17 = (f32[2048]{0:T(1024)S(1)}, f32[2048]{0:T(1024)}, u32[]{:S(2)}) copy-start(f32[2048]{0:T(1024)} %param.17) | copy-start | bytes 24580
  18.5 112.5 %all-reduce.9.cloned.1.call-start = ((), (), s32[]{:S(2)}) async-start(), calls=%async_computation.1 | async-start | bytes 2097152 | tf_op jit(solution)/shard_map/psum | solution.py:66
  71.2 5.1 %copy-start.1 = (bf16[1024,2048]{1,0:T(8,128)(2,1)S(1)}, bf16[1024,2048]{1,0:T(8,128)(2,1)}, u32[]{:S(2)}) copy-start(bf16[1024,2048]{1,0:T(8,128)(2,1)} %copy-done) | copy-start | bytes 12582916
  75.0 1.3 copy-start.6
  76.3 2.4 copy-start.20
  76.3 54.7 %copy-start.8 = (f32[1024,256]{1,0:T(8,128)S(1)}, f32[1024,256]{1,0:T(8,128)}, u32[]{:S(2)}) copy-start(f32[1024,256]{1,0:T(8,128)} %param.18) | copy-start | bytes 3145732
  78.6 108.9 %all-reduce.11.cloned.1.call-start = ((), (), s32[]{:S(2)}) async-start(), calls=%async_computation.2 | async-start | bytes 4194304 | tf_op jit(solution)/shard_map/psum | solution.py:57
  131.0 3.0 copy-start.2
  136.7 111.1 %all-reduce.13.cloned.1.call-start = ((), (), s32[]{:S(2)}) async-start(), calls=%async_computation.3 | async-start | bytes 2097152 | tf_op jit(solution)/shard_map/psum | solution.py:66
  187.5 5.7 %copy-start.3 = (bf16[1024,2048]{1,0:T(8,128)(2,1)S(1)}, bf16[1024,2048]{1,0:T(8,128)(2,1)}, u32[]{:S(2)}) copy-start(bf16[1024,2048]{1,0:T(8,128)(2,1)} %copy-done) | copy-start | bytes 12582916
  187.5 5.7 %copy-start.7 = (f32[2048,256]{1,0:T(8,128)S(1)}, f32[2048,256]{1,0:T(8,128)}, u32[]{:S(2)}) copy-start(f32[2048,256]{1,0:T(8,128)} %copy-done.6) | copy-start | bytes 6291460
  195.5 108.8 %all-reduce.15.cloned.1.call-start = ((), (), s32[]{:S(2)}) async-start(), calls=%async_computation.4 | async-start | bytes 4194304 | tf_op jit(solution)/shard_map/psum | solution.py:57
  247.9 3.0 copy-start.4
  253.6 110.6 %all-reduce.17.cloned.1.call-start = ((), (), s32[]{:S(2)}) async-start(), calls=%async_computation.5 | async-start | bytes 2097152 | tf_op jit(solution)/shard_map/psum | solution.py:66
  304.4 5.1 %copy-start.5 = (bf16[1024,2048]{1,0:T(8,128)(2,1)S(1)}, bf16[1024,2048]{1,0:T(8,128)(2,1)}, u32[]{:S(2)}) copy-start(bf16[1024,2048]{1,0:T(8,128)(2,1)} %copy-done) | copy-start | bytes 12582916
  (3 other events, 3.3 us)
Sparse Core Ops, SparseCore 0:
  18.6 52.4 all-reduce.6
  78.8 52.1 all-reduce.8
  136.9 50.5 all-reduce.10
  195.6 52.1 all-reduce.12
  253.7 50.5 all-reduce.14
  312.0 52.1 all-reduce.16
where the time goes:
time: 375 us; the launch traced here: 374 us
  waiting for transfers between devices  279 us (74%)
  blocking collectives  31.8 us (8%)
  other arithmetic  23.1 us (6%)
  matrix products  15 us (4%)
  between operations  14.3 us (4%)
  local copies, waits for them, and re-layouts  10.2 us (3%)
    psum x3, waiting for transfers between devices, local(): image = lax.psum(partial_image, 'col')  157 us
    psum x3, waiting for transfers between devices, local(): image_t = lax.psum(partial_t, 'row')  122 us
    psum x2, blocking collectives, local(): sum_x = lax.psum(jnp.sum((primal_next - primal) ** 2, axis=0), 'col')  16.2 us
    psum x2, blocking collectives, local(): sum_y = lax.psum(jnp.sum((dual_next - dual) ** 2, axis=0), 'row')  15.6 us
    reduce_sum x2, other arithmetic, local(): sum_x = lax.psum(jnp.sum((primal_next - primal) ** 2, axis=0), 'col')  9.47 us
    unnamed x43, local copies, waits for them, and re-layouts  8.72 us
    dot_general x3, matrix products, transpose_product(): lax.dot_general(matrix, vector, (((0,), (0,)), ((), ())), preferred_eleme...  8.15 us
  transfers between devices with their start and end apart: 6, of which 6 were waited for; matrix products, arithmetic and copies ran while one was open for 0% of the time, Pallas kernels for 0%

commit v1 on v0

v1 whole, which is shorter than its diff:
```python
import functools

import jax
import jax.numpy as jnp
from jax import lax
from jax.experimental import pallas as pl
from jax.experimental.pallas import tpu as pltpu
from jax.sharding import PartitionSpec as P

ITERS = 3
STEP_SCALE = 0.5
LANES = 128
HALF = LANES // 2
TAIL = 16

bf16 = jnp.bfloat16
f32 = jnp.float32

SMEM = pl.BlockSpec(memory_space=pltpu.SMEM)
VMEM = pl.BlockSpec(memory_space=pltpu.VMEM)
ANY = pl.BlockSpec(memory_space=pl.ANY)


def swap_halves(values):
    return pltpu.roll(values, HALF, 1)


def low_lanes(shape):
    return lax.broadcasted_iota(jnp.int32, shape, 1) < HALF


def pack(upper, lower):
    return jnp.where(low_lanes(upper.shape), upper, swap_halves(lower))


def split_sum(total):
    first = total.astype(bf16).astype(f32)
    rest = total - first
    second = rest.astype(bf16).astype(f32)
    third = rest - second
    row = lax.broadcasted_iota(jnp.int32, (TAIL, LANES), 0)
    tile = jnp.where(row == 0, first, jnp.where(row == 1, second, jnp.where(row == 2, third, 0.0)))
    return tile.astype(bf16)


def join_sum(tile):
    return jnp.sum(tile.astype(f32), axis=0, keepdims=True)


def tree_sum(terms):
    terms = list(terms)
    while len(terms) > 1:
        terms = [terms[k] + terms[k + 1] for k in range(0, len(terms), 2)]
    return terms[0]


def column_total(squares):
    total = jnp.sum(squares, axis=0, keepdims=True)
    return total + swap_halves(jnp.broadcast_to(total, (8, LANES)))[0:1]


class Tiles:
    def __init__(self, tile_map, sources, slots, sems):
        self.tile_map, self.sources, self.slots, self.sems = tile_map, sources, slots, sems
        self.rows, self.cols = tile_map.shape
        self.size_r, self.size_c = slots.shape[1:]
        self.rows_each = self.rows // len(sources)

    def copy(self, source, i, j):
        spot = i * self.cols + j
        inner = i % self.rows_each
        return pltpu.make_async_copy(
            source.at[pl.ds(inner * self.size_r, self.size_r), pl.ds(j * self.size_c, self.size_c)],
            self.slots.at[spot],
            self.sems.at[spot],
        )

    def start(self):
        for i in range(self.rows):
            for j in range(self.cols):
                @pl.when(self.tile_map[i, j] != 0)
                def _():
                    self.copy(self.sources[i // self.rows_each], i, j).start()

    def each(self, body):
        def step(t, carry):
            i, j = t // self.cols, t % self.cols

            @pl.when(self.tile_map[i, j] != 0)
            def _():
                pltpu.make_async_copy(self.slots.at[t], self.slots.at[t], self.sems.at[t]).wait()
                body(i, j, self.slots[t])

            return carry

        lax.fori_loop(0, self.rows * self.cols, step, 0)


def product_back(tiles, vector, acc):
    acc[...] = jnp.zeros_like(acc)

    def body(i, j, tile):
        rows = vector[pl.ds(pl.multiple_of(i * tiles.size_r, tiles.size_r), tiles.size_r)]
        where = pl.ds(pl.multiple_of(j * tiles.size_c, tiles.size_c), tiles.size_c)
        acc[where] += lax.dot_general(
            tile, rows, (((0,), (0,)), ((), ())), preferred_element_type=f32
        )

    tiles.each(body)


def product_forward(tiles, vector, acc):
    acc[...] = jnp.zeros_like(acc)

    def body(i, j, tile):
        rows = vector[pl.ds(pl.multiple_of(j * tiles.size_c, tiles.size_c), tiles.size_c)]
        where = pl.ds(pl.multiple_of(i * tiles.size_r, tiles.size_r), tiles.size_r)
        acc[where] += jnp.dot(tile, rows, preferred_element_type=f32)

    tiles.each(body)


def first_kernel(tile_map, place, blocks, dual, mine, other, slots, sems, acc, vector):
    tiles = Tiles(tile_map, [blocks], slots, sems)
    tiles.start()
    vector[...] = dual[...].astype(bf16)
    product_back(tiles, vector, acc)

    @pl.when(place[1] == 0)
    def _():
        mine[...] = acc[:, :LANES]
        other[...] = acc[:, LANES:]

    @pl.when(place[1] != 0)
    def _():
        mine[...] = acc[:, LANES:]
        other[...] = acc[:, :LANES]


def first_pack_kernel(mine, other, msg_a, msg_b):
    half = msg_a.shape[0] - TAIL
    upper = mine[:half] + other[:half]
    lower = mine[half:] + other[half:]
    msg_a[:half] = pack(upper, lower).astype(bf16)
    msg_b[:half] = pack(swap_halves(upper), swap_halves(lower)).astype(bf16)
    msg_a[half:] = jnp.zeros((TAIL, LANES), bf16)
    msg_b[half:] = jnp.zeros((TAIL, LANES), bf16)


def back_kernel(count, tile_map, place, *refs):
    pieces = refs[:count]
    own, partner, msg, slots, sems, vector, acc = refs[count:]
    tiles = Tiles(tile_map, [own, partner], slots, sems)
    tiles.start()
    piece = pieces[0].shape[0] - TAIL
    half = vector.shape[0] // 2
    for k in range(count):
        start = pl.multiple_of((place[0] ^ k) * piece, piece)
        values = pieces[k][:piece]
        vector[pl.ds(start, piece)] = values
        vector[pl.ds(half + start, piece)] = swap_halves(values.astype(f32)).astype(bf16)
    product_back(tiles, vector, acc)
    out = msg.shape[0] - TAIL
    msg[:out] = pack(acc[:out], acc[out:]).astype(bf16)
    total = sum(join_sum(ref[piece:]) for ref in pieces)
    msg[out:] = split_sum(total)


def forward_kernel(
    near, count, first, last, total_rows, total_cols, tile_map, place, *refs
):
    msgs = refs[:near]
    primal, cost, lower, upper, state, own, partner = refs[near : near + 7]
    outs = refs[near + 7 :]
    primal_next, image_own = outs[:2]
    image_msgs = outs[2 : 1 + count]
    state_out, slots, sems, vector, acc = outs[1 + count :]
    tiles = Tiles(tile_map, [own, partner], slots, sems)
    tiles.start()
    size = primal.shape[0]
    weight = state[0:1]
    if not first:
        sum_y = tree_sum([join_sum(ref[size:]) for ref in msgs])
        move_y = jnp.sqrt(sum_y / total_rows + 1e-06)
        move_x = jnp.sqrt(state[1:2] / total_cols + 1e-06)
        weight = jnp.sqrt(weight * move_y / move_x)
    state_out[...] = jnp.broadcast_to(weight, state_out.shape)
    step = STEP_SCALE / weight
    image_t = tree_sum([ref[:size].astype(f32) for ref in msgs])
    before = primal[...]
    after = before - step * (cost[...] - image_t)
    after = jnp.minimum(jnp.maximum(after, lower[...]), upper[...])
    primal_next[...] = after
    extrapolated = 2.0 * after - before
    vector[:size] = extrapolated.astype(bf16)
    vector[size:] = swap_halves(extrapolated).astype(bf16)
    tail = None
    if not last:
        tail = split_sum(column_total((after - before) ** 2))
    product_forward(tiles, vector, acc)
    half = acc.shape[0] // 2
    piece = image_own.shape[0]
    for k in range(count):
        start = pl.multiple_of((place[0] ^ k) * piece, piece)
        part = pack(acc[pl.ds(start, piece)], acc[pl.ds(half + start, piece)])
        if k == 0:
            image_own[...] = part
        else:
            image_msgs[k - 1][:piece] = part.astype(bf16)
            image_msgs[k - 1][piece:] = jnp.zeros((TAIL, LANES), bf16) if last else tail
    if not last:
        state_out[1:2] = join_sum(tail)


def dual_kernel(count, last, *refs):
    image_own, state = refs[:2]
    msgs = refs[2 : 1 + count]
    dual, right, floor, dual_next = refs[1 + count : 5 + count]
    piece = image_own.shape[0]
    image = image_own[...]
    for ref in msgs:
        image = image + ref[:piece].astype(f32)
    before = dual[...]
    after = before + STEP_SCALE * state[0:1] * (right[...] - image)
    after = jnp.maximum(after, floor[...])
    dual_next[...] = after
    if not last:
        msg, state_out = refs[5 + count :]
        msg[:piece] = after.astype(bf16)
        msg[piece:] = split_sum(column_total((after - before) ** 2))
        sum_x = state[1:2]
        for ref in msgs:
            sum_x = sum_x + join_sum(ref[piece:])
        state_out[...] = state[...]
        state_out[1:2] = sum_x


def unpack_kernel(count, place, *refs):
    pieces_a, pieces_b = refs[:count], refs[count : 2 * count]
    upper, lower = refs[2 * count :]
    piece = pieces_a[0].shape[0]
    for k in range(count):
        start = pl.multiple_of((place[0] ^ k) * piece, piece) if count > 1 else 0
        a, b = pieces_a[k][...], pieces_b[k][...]
        low = low_lanes(a.shape)
        upper[pl.ds(start, piece)] = jnp.where(low, a, swap_halves(b))
        lower[pl.ds(start, piece)] = jnp.where(low, swap_halves(a), b)


def call(kernel, out_shape, in_specs, scratch=(), flops=0, name=None):
    return pl.pallas_call(
        kernel,
        out_shape=out_shape,
        in_specs=in_specs,
        out_specs=jax.tree.map(lambda _: VMEM, out_shape),
        scratch_shapes=list(scratch),
        compiler_params=pltpu.CompilerParams(vmem_limit_bytes=32 * 1024 * 1024),
        cost_estimate=pl.CostEstimate(flops=flops, bytes_accessed=4 << 20, transcendentals=0),
        name=name,
    )


def shape(rows, kind=f32, cols=LANES):
    return jax.ShapeDtypeStruct((rows, cols), kind)


def local(
    blocks,
    tile_map,
    lower_bound,
    upper_bound,
    bound_code,
    row_kind,
    cost_vector,
    right_side,
    primal_start,
    dual_start,
    primal_weight,
):
    rows, cols = blocks.shape
    size_r = rows // tile_map.shape[0]
    size_c = cols // tile_map.shape[1]
    count = lax.axis_size("col")
    near = lax.axis_size("row") // 2
    total_rows = rows * near * 2
    total_cols = cols * count
    piece = rows // count
    half = cols // 2
    z = lax.axis_index("col")
    core = lax.axis_index("row") % 2
    place = jnp.stack([z, core]).astype(jnp.int32)

    def to_core(value):
        return lax.ppermute(value, "row", [(i, i ^ 1) for i in range(2 * near)])

    def to_x(value, k):
        return lax.ppermute(value, "row", [(i, i ^ (2 * k)) for i in range(2 * near)])

    def to_z(value, k):
        return lax.ppermute(value, "col", [(i, i ^ k) for i in range(count)])

    def scratch(n_tiles):
        return [
            pltpu.VMEM((n_tiles, size_r, size_c), bf16),
            pltpu.SemaphoreType.DMA((n_tiles,)),
        ]

    n_own = tile_map.size

    with jax.named_scope("first_product"):
        mine, other = call(
            first_kernel,
            (shape(cols), shape(cols)),
            [SMEM, SMEM, ANY, VMEM],
            scratch(n_own) + [pltpu.VMEM((cols, 2 * LANES), f32), pltpu.VMEM((rows, 2 * LANES), bf16)],
            flops=2 * rows * cols * 256,
            name="first_product",
        )(tile_map, place, blocks, dual_start)
    other = to_core(other)
    messages = call(
        first_pack_kernel, (shape(half + TAIL, bf16),) * 2, [VMEM, VMEM], name="first_pack"
    )(mine, other)
    messages, blocks = lax.optimization_barrier((messages, blocks))
    partner = to_core(blocks)
    chip_map = jnp.concatenate([tile_map, to_core(tile_map)], axis=0)

    def my_half(value):
        return lax.dynamic_slice_in_dim(value, core * LANES, LANES, 1)

    def other_half(value):
        return lax.dynamic_slice_in_dim(value, (1 - core) * LANES, LANES, 1)

    def batches(upper, lower):
        return [
            jnp.concatenate([upper[:, b * HALF : (b + 1) * HALF], lower[:, b * HALF : (b + 1) * HALF]], axis=1)
            for b in range(2)
        ]

    def spread(vector):
        wide = jnp.broadcast_to(vector[:, None], (cols, HALF))
        return jnp.concatenate([wide[:half], wide[half:]], axis=1)

    start = my_half(primal_start)
    primal = batches(start[:half], start[half:])
    low_on = (bound_code == 1) | (bound_code == 3)
    high_on = (bound_code == 2) | (bound_code == 3)
    lower = spread(jnp.where(low_on, lower_bound, -jnp.inf))
    upper = spread(jnp.where(high_on, upper_bound, jnp.inf))
    cost = spread(cost_vector)

    def own_rows(value):
        return lax.dynamic_slice_in_dim(value, z * piece, piece, 0)

    floor = jnp.broadcast_to(jnp.where(own_rows(row_kind) == 1, 0.0, -jnp.inf)[:, None], (piece, LANES))
    dual_rows, right_rows = own_rows(dual_start), own_rows(right_side)
    received = to_core(jnp.concatenate([other_half(dual_rows), other_half(right_rows), floor], axis=0))
    dual = batches(my_half(dual_rows), received[:piece])
    right = batches(my_half(right_rows), received[piece : 2 * piece])
    floors = batches(floor, received[2 * piece :])

    weight = lax.dynamic_slice_in_dim(primal_weight, core * LANES, LANES, 0)
    state = [
        jnp.broadcast_to(jnp.tile(weight[b * HALF : (b + 1) * HALF], 2)[None, :], (8, LANES)) for b in range(2)
    ]

    n_chip = 2 * n_own
    flops = 2 * (2 * rows) * cols * LANES
    gathered = [None, None]
    for iteration in range(ITERS):
        first, last = iteration == 0, iteration + 1 == ITERS
        for b in range(2):
            if not first:
                messages = list(messages)
                messages[b] = call(
                    functools.partial(back_kernel, count),
                    shape(half + TAIL, bf16),
                    [SMEM, SMEM] + [VMEM] * count + [ANY, ANY],
                    scratch(n_chip) + [pltpu.VMEM((2 * rows, LANES), bf16), pltpu.VMEM((cols, LANES), f32)],
                    flops=flops,
                    name="back_product",
                )(chip_map, place, *gathered[b], blocks, partner)
            x_msgs = [messages[b]] + [to_x(messages[b], k) for k in range(1, near)]
            outs = call(
                functools.partial(forward_kernel, near, count, first, last, total_rows, total_cols),
                (shape(half), shape(piece)) + (shape(piece + TAIL, bf16),) * (count - 1) + (shape(8),),
                [SMEM, SMEM] + [VMEM] * (near + 5) + [ANY, ANY],
                scratch(n_chip) + [pltpu.VMEM((cols, LANES), bf16), pltpu.VMEM((2 * rows, LANES), f32)],
                flops=flops,
                name="forward_product",
            )(chip_map, place, *x_msgs, primal[b], cost, lower, upper, state[b], blocks, partner)
            primal[b], image_own, image_msgs, state_b = outs[0], outs[1], outs[2:-1], outs[-1]
            image_msgs = [to_z(image_msgs[k - 1], k) for k in range(1, count)]
            out_shape = (shape(piece),)
            if not last:
                out_shape += (shape(piece + TAIL, bf16), shape(8))
            outs = call(
                functools.partial(dual_kernel, count, last),
                out_shape,
                [VMEM] * (count + 4),
                name="dual_update",
            )(image_own, state_b, *image_msgs, dual[b], right[b], floors[b])
            dual[b] = outs[0]
            if last:
                gathered[b] = [dual[b]] + [to_z(dual[b], k) for k in range(1, count)]
            else:
                state[b] = outs[2]
                gathered[b] = [outs[1]] + [to_z(outs[1], k) for k in range(1, count)]

    def both(mine, theirs):
        return lax.cond(
            core == 0,
            lambda a, b: jnp.concatenate([a, b], axis=1),
            lambda a, b: jnp.concatenate([b, a], axis=1),
            mine,
            theirs,
        )

    upper, lower = call(
        functools.partial(unpack_kernel, 1), (shape(half), shape(half)), [SMEM, VMEM, VMEM], name="unpack_primal"
    )(place, *primal)
    primal_mine = jnp.concatenate([upper, lower], axis=0)
    primal_final = both(primal_mine, to_core(primal_mine))
    own, theirs = call(
        functools.partial(unpack_kernel, count),
        (shape(rows), shape(rows)),
        [SMEM] + [VMEM] * (2 * count),
        name="unpack_dual",
    )(place, *gathered[0], *gathered[1])
    dual_final = both(own, to_core(theirs))
    return primal_final, dual_final


def solution(mesh):
    return jax.shard_map(
        local,
        mesh=mesh,
        in_specs=(
            P("row", "col"),
            P("row", "col"),
            P("col"),
            P("col"),
            P("col"),
            P("row"),
            P("col"),
            P("row", "groups"),
            P("col", "groups"),
            P("row", "groups"),
            P("groups"),
        ),
        out_specs=(P("col", "groups"), P("row", "groups")),
        check_vma=False,
    )
```

time: 375 us -> 188 us (0.50)
  waiting for transfers between devices: 279 us -> 49.8 us
  starting transfers between devices: 0.43 us -> 67.1 us
  Pallas kernels: 0 us -> 41 us
  blocking collectives: 31.8 us -> 0 us
  matrix products: 15 us -> 0 us
  other arithmetic: 23.1 us -> 8.91 us
  between operations: 14.3 us -> 1.14 us
  local copies, waits for them, and re-layouts: 10.2 us -> 17.4 us
    psum x6 -> x0, waiting for transfers between devices: 279 us -> none  [the longest x3 157 us: local(): image = lax.psum(partial_image, 'col')]
    ppermute x0 -> x48, starting transfers between devices: none -> 67.1 us  [the longest x36 51.4 us: to_z(): return lax.ppermute(value, 'col', [(i, i ^ k) for i in range(count)])]
    ppermute x0 -> x48, waiting for transfers between devices: none -> 49.8 us  [the longest x36 37.8 us: to_z(): return lax.ppermute(value, 'col', [(i, i ^ k) for i in range(count)])]
    pallas_call x0 -> x20, Pallas kernels: none -> 41 us  [the longest x6 21.6 us: local(): call(functools.partial(forward_kernel, near, count, first, last, total_ro...]
    psum x4 -> x0, blocking collectives: 31.8 us -> none  [the longest x2 16.2 us: local(): sum_x = lax.psum(jnp.sum((primal_next - primal) ** 2, axis=0), 'col')]
    dot_general x6 -> x0, matrix products: 15 us -> none  [the longest x3 8.15 us: transpose_product(): lax.dot_general(matrix, vector, (((0,), (0,)), ((), ())), preferred_eleme...]
    reduce_sum x4 -> x0, other arithmetic: 13.5 us -> none  [the longest x2 9.47 us: local(): sum_x = lax.psum(jnp.sum((primal_next - primal) ** 2, axis=0), 'col')]
    concatenate x0 -> x14, other arithmetic: none -> 8.06 us  [the longest x2 3.67 us: both(): jnp.concatenate([b, a], axis=1)]
  transfers between devices with their start and end apart: 6 -> 48, of which waited for: 6 -> 19; matrix products, arithmetic and copies ran while one was open for 0% -> 11% of each run, Pallas kernels for 0% -> 18%
where the time goes in v1:
time: 188 us; the launch traced here: 185 us
  starting transfers between devices  67.1 us (36%)
  waiting for transfers between devices  49.8 us (26%)
  Pallas kernels  41 us (22%)
  local copies, waits for them, and re-layouts  17.4 us (9%)
  other arithmetic  8.91 us (5%)
    ppermute x36, starting transfers between devices, to_z(): return lax.ppermute(value, 'col', [(i, i ^ k) for i in range(count)])  51.4 us
    ppermute x36, waiting for transfers between devices, to_z(): return lax.ppermute(value, 'col', [(i, i ^ k) for i in range(count)])  37.8 us
    pallas_call x6, Pallas kernels, local(): call(functools.partial(forward_kernel, near, count, first, last, total_ro...  21.6 us
    pallas_call x4, Pallas kernels, local(): call(functools.partial(back_kernel, count), shape(half + TAIL, bf16), [SM...  14.2 us
    ppermute x6, starting transfers between devices, to_core(): return lax.ppermute(value, 'row', [(i, i ^ 1) for i in range(2 * near)])  12.1 us
    ppermute x6, waiting for transfers between devices, to_x(): return lax.ppermute(value, 'row', [(i, i ^ 2 * k) for i in range(2 * near)])  8.03 us
    slice x4, local copies, waits for them, and re-layouts, batches(): upper[:, b * HALF:(b + 1) * HALF]  5.35 us
    ppermute x6, waiting for transfers between devices, to_core(): return lax.ppermute(value, 'row', [(i, i ^ 1) for i in range(2 * near)])  3.97 us
  transfers between devices with their start and end apart: 48, of which 19 were waited for; matrix products, arithmetic and copies ran while one was open for 11% of the time, Pallas kernels for 18%

profile of v1, /device:TPU:5, one launch (start us, length us, event | category | flops | bytes accessed | tf_op | source)
XLA Modules:
  0.0 185.3 jit_solution(7295274377896274318)
XLA Ops:
  6.4 2.3 %collective-permute-done.1.other = f32[2048,128]{1,0:T(8,128)S(1)} collective-permute-done((f32[2048,128]{1,0:T(8,128)S(1)}, f32[2048,128]{1,0:T(8,128)S(1)}, u32[]{:S(2)}, u32[]{:S(2)}) %collective-permute-start.1) | collective-permute-done | bytes 1048608 | tf_op jit(solution)/shard_map/ppermute | solution.py:294
  32.0 5.6 %collective-permute-done.19.refs_1_ = bf16[1040,128]{1,0:T(8,128)(2,1)S(1)} collective-permute-done((bf16[1040,128]{1,0:T(8,128)(2,1)S(1)}, bf16[1040,128]{1,0:T(8,128)(2,1)S(1)}, u32[]{:S(2)}, u32[]{:S(2)}) %collective-permute-start.19) | collective-permute-done | bytes 266272 | tf_op jit(solution)/shard_map/ppermute | solution.py:297
  37.6 3.6 %forward_product.9 = (f32[1024,128]{1,0:T(8,128)S(1)}, f32[256,128]{1,0:T(8,128)S(1)}, bf16[272,128]{1,0:T(8,128)(2,1)S(1)}, bf16[272,128]{1,0:T(8,128)(2,1)S(1)...) custom-call(s32[4,4]{1,0:T(4,128)S(1)} %pad_add_fusion.tile_map, s32[2]{0:T(128)S(1)} %pad_add_fusion.1.place, ...), custom_call_target="tpu_custom_call" | custom-call | flops 1073741824 | bytes 4194304 | tf_op jit(solution)/shard_map/forward_product/pallas_call | solution.py:383
  43.3 3.6 %forward_product.6 = (f32[1024,128]{1,0:T(8,128)S(1)}, f32[256,128]{1,0:T(8,128)S(1)}, bf16[272,128]{1,0:T(8,128)(2,1)S(1)}, bf16[272,128]{1,0:T(8,128)(2,1)S(1)...) custom-call(s32[4,4]{1,0:T(4,128)S(1)} %pad_add_fusion.tile_map, s32[2]{0:T(128)S(1)} %pad_add_fusion.1.place, ...), custom_call_target="tpu_custom_call" | custom-call | flops 1073741824 | bytes 4194304 | tf_op jit(solution)/shard_map/forward_product/pallas_call | solution.py:383
  54.5 2.3 %collective-permute-start.10 = (bf16[272,128]{1,0:T(8,128)(2,1)S(1)}, bf16[272,128]{1,0:T(8,128)(2,1)S(1)}, u32[]{:S(2)}, u32[]{:S(2)}) collective-permute-start(bf16[272,128]{1,0:T(8,128)(2,1)S(1)} %get-tuple-element.102.refs_0_), channel_id=1, source_target_pairs={{0,3},{1,2},{2,1},{3,0},{4,7},{5,6},{6,5},{7,4},{8,11},{9,10},{10,... | collective-permute-start | bytes 208904 | tf_op jit(solution)/shard_map/ppermute | solution.py:300
  56.8 4.9 %collective-permute-start.9 = (bf16[272,128]{1,0:T(8,128)(2,1)S(1)}, bf16[272,128]{1,0:T(8,128)(2,1)S(1)}, u32[]{:S(2)}, u32[]{:S(2)}) collective-permute-start(bf16[272,128]{1,0:T(8,128)(2,1)S(1)} %get-tuple-element.102.refs_0_), channel_id=1, source_target_pairs={{0,2},{1,3},{2,0},{3,1},{4,6},{5,7},{6,4},{7,5},{8,10},{9,11},{10,... | collective-permute-start | bytes 208904 | tf_op jit(solution)/shard_map/ppermute | solution.py:300
  63.8 2.3 %collective-permute-start.24 = (bf16[272,128]{1,0:T(8,128)(2,1)S(1)}, bf16[272,128]{1,0:T(8,128)(2,1)S(1)}, u32[]{:S(2)}, u32[]{:S(2)}) collective-permute-start(bf16[272,128]{1,0:T(8,128)(2,1)S(1)} %get-tuple-element.121.refs_0_), channel_id=1, source_target_pairs={{0,2},{1,3},{2,0},{3,1},{4,6},{5,7},{6,4},{7,5},{8,10},{9,11},{10,... | collective-permute-start | bytes 208904 | tf_op jit(solution)/shard_map/ppermute | solution.py:300
  68.1 2.4 %collective-permute-done.9.refs_2_ = bf16[272,128]{1,0:T(8,128)(2,1)S(1)} collective-permute-done((bf16[272,128]{1,0:T(8,128)(2,1)S(1)}, bf16[272,128]{1,0:T(8,128)(2,1)S(1)}, u32[]{:S(2)}, u32[]{:S(2)}) %collective-permute-start.9) | collective-permute-done | bytes 69664 | tf_op jit(solution)/shard_map/ppermute | solution.py:300
  70.5 3.6 %back_product.4.refs_0_ = bf16[1040,128]{1,0:T(8,128)(2,1)S(1)} custom-call(s32[4,4]{1,0:T(4,128)S(1)} %pad_add_fusion.tile_map, s32[2]{0:T(128)S(1)} %pad_add_fusion.1.place, bf16[272,128]{1,0:T(8,128)(2,1)S(1)} %get-tuple-element.102.refs_0_, bf16[272,128]{1,0:T(8,128)(2,1)S(1)} %collective-permute-done.8.refs_1_, ...), custom_call_target="tpu_custom_call" | custom-call | flops 1073741824 | bytes 4194304 | tf_op jit(solution)/shard_map/back_product/pallas_call | solution.py:374
  75.0 3.6 %back_product.6.refs_0_ = bf16[1040,128]{1,0:T(8,128)(2,1)S(1)} custom-call(s32[4,4]{1,0:T(4,128)S(1)} %pad_add_fusion.tile_map, s32[2]{0:T(128)S(1)} %pad_add_fusion.1.place, bf16[272,128]{1,0:T(8,128)(2,1)S(1)} %get-tuple-element.121.refs_0_, bf16[272,128]{1,0:T(8,128)(2,1)S(1)} %collective-permute-done.23.refs_1_, ...), custom_call_target="tpu_custom_call" | custom-call | flops 1073741824 | bytes 4194304 | tf_op jit(solution)/shard_map/back_product/pallas_call | solution.py:374
  79.4 3.6 %forward_product.7 = (f32[1024,128]{1,0:T(8,128)S(1)}, f32[256,128]{1,0:T(8,128)S(1)}, bf16[272,128]{1,0:T(8,128)(2,1)S(1)}, bf16[272,128]{1,0:T(8,128)(2,1)S(1)...) custom-call(s32[4,4]{1,0:T(4,128)S(1)} %pad_add_fusion.tile_map, s32[2]{0:T(128)S(1)} %pad_add_fusion.1.place, ...), custom_call_target="tpu_custom_call" | custom-call | flops 1073741824 | bytes 4194304 | tf_op jit(solution)/shard_map/forward_product/pallas_call | solution.py:383
  87.0 3.6 %forward_product.10 = (f32[1024,128]{1,0:T(8,128)S(1)}, f32[256,128]{1,0:T(8,128)S(1)}, bf16[272,128]{1,0:T(8,128)(2,1)S(1)}, bf16[272,128]{1,0:T(8,128)(2,1)S(1...) custom-call(s32[4,4]{1,0:T(4,128)S(1)} %pad_add_fusion.tile_map, s32[2]{0:T(128)S(1)} %pad_add_fusion.1.place, ...), custom_call_target="tpu_custom_call" | custom-call | flops 1073741824 | bytes 4194304 | tf_op jit(solution)/shard_map/forward_product/pallas_call | solution.py:383
  99.8 3.1 %collective-permute-start.31 = (bf16[272,128]{1,0:T(8,128)(2,1)S(1)}, bf16[272,128]{1,0:T(8,128)(2,1)S(1)}, u32[]{:S(2)}, u32[]{:S(2)}) collective-permute-start(bf16[272,128]{1,0:T(8,128)(2,1)S(1)} %get-tuple-element.130.refs_0_), channel_id=1, source_target_pairs={{0,2},{1,3},{2,0},{3,1},{4,6},{5,7},{6,4},{7,5},{8,10},{9,11},{10,... | collective-permute-start | bytes 208904 | tf_op jit(solution)/shard_map/ppermute | solution.py:300
  104.5 3.6 %back_product.5.refs_0_ = bf16[1040,128]{1,0:T(8,128)(2,1)S(1)} custom-call(s32[4,4]{1,0:T(4,128)S(1)} %pad_add_fusion.tile_map, s32[2]{0:T(128)S(1)} %pad_add_fusion.1.place, bf16[272,128]{1,0:T(8,128)(2,1)S(1)} %get-tuple-element.111.refs_0_, bf16[272,128]{1,0:T(8,128)(2,1)S(1)} %collective-permute-done.15.refs_1_, ...), custom_call_target="tpu_custom_call" | custom-call | flops 1073741824 | bytes 4194304 | tf_op jit(solution)/shard_map/back_product/pallas_call | solution.py:374
  110.9 3.6 %back_product.7.refs_0_ = bf16[1040,128]{1,0:T(8,128)(2,1)S(1)} custom-call(s32[4,4]{1,0:T(4,128)S(1)} %pad_add_fusion.tile_map, s32[2]{0:T(128)S(1)} %pad_add_fusion.1.place, bf16[272,128]{1,0:T(8,128)(2,1)S(1)} %get-tuple-element.130.refs_0_, bf16[272,128]{1,0:T(8,128)(2,1)S(1)} %collective-permute-done.30.refs_1_, ...), custom_call_target="tpu_custom_call" | custom-call | flops 1073741824 | bytes 4194304 | tf_op jit(solution)/shard_map/back_product/pallas_call | solution.py:374
  114.8 3.6 %forward_product.8 = (f32[1024,128]{1,0:T(8,128)S(1)}, f32[256,128]{1,0:T(8,128)S(1)}, bf16[272,128]{1,0:T(8,128)(2,1)S(1)}, bf16[272,128]{1,0:T(8,128)(2,1)S(1)...) custom-call(s32[4,4]{1,0:T(4,128)S(1)} %pad_add_fusion.tile_map, s32[2]{0:T(128)S(1)} %pad_add_fusion.1.place, ...), custom_call_target="tpu_custom_call" | custom-call | flops 1073741824 | bytes 4194304 | tf_op jit(solution)/shard_map/forward_product/pallas_call | solution.py:383
  119.8 3.6 %forward_product.11 = (f32[1024,128]{1,0:T(8,128)S(1)}, f32[256,128]{1,0:T(8,128)S(1)}, bf16[272,128]{1,0:T(8,128)(2,1)S(1)}, bf16[272,128]{1,0:T(8,128)(2,1)S(1...) custom-call(s32[4,4]{1,0:T(4,128)S(1)} %pad_add_fusion.tile_map, s32[2]{0:T(128)S(1)} %pad_add_fusion.1.place, ...), custom_call_target="tpu_custom_call" | custom-call | flops 1073741824 | bytes 4194304 | tf_op jit(solution)/shard_map/forward_product/pallas_call | solution.py:383
  124.3 8.3 %collective-permute-start.34 = (f32[2048,128]{1,0:T(8,128)S(1)}, f32[2048,128]{1,0:T(8,128)S(1)}, u32[]{:S(2)}, u32[]{:S(2)}) collective-permute-start(f32[2048,128]{1,0:T(8,128)S(1)} %constant_dynamic-update-slice_fusion), channel_id=1, source_target_pairs={{0,4},{4,0},{8,12},{12,8},{1,5},{5,1},{9,13},{13,9},{2,6},{6,2},{1... | collective-permute-start | bytes 3145736 | tf_op jit(solution)/shard_map/ppermute | solution.py:294
  132.6 2.9 %collective-permute-start.35 = (bf16[272,128]{1,0:T(8,128)(2,1)S(1)}, bf16[272,128]{1,0:T(8,128)(2,1)S(1)}, u32[]{:S(2)}, u32[]{:S(2)}) collective-permute-start(bf16[272,128]{1,0:T(8,128)(2,1)S(1)} %get-tuple-element.138), channel_id=1, source_target_pairs={{0,1},{1,0},{2,3},{3,2},{4,5},{5,4},{6,7},{7,6},{8,9},{9,8},{10,11... | collective-permute-start | bytes 208904 | tf_op jit(solution)/shard_map/ppermute | solution.py:300
  138.2 5.2 %collective-permute-done.36.refs_3_ = bf16[272,128]{1,0:T(8,128)(2,1)S(1)} collective-permute-done((bf16[272,128]{1,0:T(8,128)(2,1)S(1)}, bf16[272,128]{1,0:T(8,128)(2,1)S(1)}, u32[]{:S(2)}, u32[]{:S(2)}) %collective-permute-start.36) | collective-permute-done | bytes 69664 | tf_op jit(solution)/shard_map/ppermute | solution.py:300
  146.6 2.6 %collective-permute-start.43 = (bf16[272,128]{1,0:T(8,128)(2,1)S(1)}, bf16[272,128]{1,0:T(8,128)(2,1)S(1)}, u32[]{:S(2)}, u32[]{:S(2)}) collective-permute-start(bf16[272,128]{1,0:T(8,128)(2,1)S(1)} %get-tuple-element.146), channel_id=1, source_target_pairs={{0,3},{1,2},{2,1},{3,0},{4,7},{5,6},{6,5},{7,4},{8,11},{9,10},{10,... | collective-permute-start | bytes 208904 | tf_op jit(solution)/shard_map/ppermute | solution.py:300
  149.1 13.9 %collective-permute-done.42.refs_3_ = bf16[272,128]{1,0:T(8,128)(2,1)S(1)} collective-permute-done((bf16[272,128]{1,0:T(8,128)(2,1)S(1)}, bf16[272,128]{1,0:T(8,128)(2,1)S(1)}, u32[]{:S(2)}, u32[]{:S(2)}) %collective-permute-start.42) | collective-permute-done | bytes 69664 | tf_op jit(solution)/shard_map/ppermute | solution.py:300
  166.8 3.0 %collective-permute-done.46.refs_7_ = f32[256,128]{1,0:T(8,128)S(1)} collective-permute-done((f32[256,128]{1,0:T(8,128)S(1)}, f32[256,128]{1,0:T(8,128)S(1)}, u32[]{:S(2)}, u32[]{:S(2)}) %collective-permute-start.46) | collective-permute-done | bytes 131104 | tf_op jit(solution)/shard_map/ppermute | solution.py:300
  169.8 7.8 %collective-permute-done.45.refs_6_ = f32[256,128]{1,0:T(8,128)S(1)} collective-permute-done((f32[256,128]{1,0:T(8,128)S(1)}, f32[256,128]{1,0:T(8,128)S(1)}, u32[]{:S(2)}, u32[]{:S(2)}) %collective-permute-start.45) | collective-permute-done | bytes 131104 | tf_op jit(solution)/shard_map/ppermute | solution.py:300
  (171 shorter events, 85.6 us)
Async XLA Ops:
  9.0 28.6 %collective-permute-start.3 = (bf16[1024,2048]{1,0:T(8,128)(2,1)}, bf16[1024,2048]{1,0:T(8,128)(2,1)}, u32[]{:S(2)}, u32[]{:S(2)}) collective-permute-start(bf16[1024,2048]{1,0:T(8,128)(2,1)} %refs_7_.5), channel_id=1, source_target_pairs={{0,4},{4,0},{8,12},{12,8},{1,5},{5,1},{9,13},{13,9},{2,6},{6,2},{1... | collective-permute-start | bytes 12582920 | tf_op jit(solution)/shard_map/ppermute | solution.py:294
  9.5 19.6 %collective-permute-start = (s32[2,4]{1,0:T(2,128)S(1)}, s32[2,4]{1,0:T(2,128)}, u32[]{:S(2)}, u32[]{:S(2)}) collective-permute-start(s32[2,4]{1,0:T(2,128)S(1)} %copy-done.2), channel_id=1, source_target_pairs={{0,4},{4,0},{8,12},{12,8},{1,5},{5,1},{9,13},{13,9},{2,6},{6,2},{1... | collective-permute-start | bytes 104 | tf_op jit(solution)/shard_map/ppermute | solution.py:294
  14.0 15.8 %collective-permute-start.7 = (f32[768,128]{1,0:T(8,128)}, f32[768,128]{1,0:T(8,128)S(1)}, u32[]{:S(2)}, u32[]{:S(2)}) collective-permute-start(f32[768,128]{1,0:T(8,128)} %maximum_maximum_fusion), channel_id=1, source_target_pairs={{0,4},{4,0},{8,12},{12,8},{1,5},{5,1},{9,13},{13,9},{2,6},{6,2},{1... | collective-permute-start | bytes 1179656 | tf_op jit(solution)/shard_map/ppermute | solution.py:294
  30.2 13.1 %collective-permute-start.2 = (bf16[1040,128]{1,0:T(8,128)(2,1)S(1)}, bf16[1040,128]{1,0:T(8,128)(2,1)S(1)}, u32[]{:S(2)}, u32[]{:S(2)}) collective-permute-start(bf16[1040,128]{1,0:T(8,128)(2,1)S(1)} %get-tuple-element.95.refs_0_), channel_id=1, source_target_pairs={{0,8},{4,12},{8,0},{12,4},{1,9},{5,13},{9,1},{13,5},{2,10},{6,14},... | collective-permute-start | bytes 798728 | tf_op jit(solution)/shard_map/ppermute | solution.py:297
  41.3 20.4 %collective-permute-start.20 = (bf16[272,128]{1,0:T(8,128)(2,1)S(1)}, bf16[272,128]{1,0:T(8,128)(2,1)S(1)}, u32[]{:S(2)}, u32[]{:S(2)}) collective-permute-start(bf16[272,128]{1,0:T(8,128)(2,1)S(1)} %get-tuple-element.118), channel_id=1, source_target_pairs={{0,1},{1,0},{2,3},{3,2},{4,5},{5,4},{6,7},{7,6},{8,9},{9,8},{10,11... | collective-permute-start | bytes 208904 | tf_op jit(solution)/shard_map/ppermute | solution.py:300
  51.1 11.1 %collective-permute-start.21 = (bf16[272,128]{1,0:T(8,128)(2,1)S(1)}, bf16[272,128]{1,0:T(8,128)(2,1)S(1)}, u32[]{:S(2)}, u32[]{:S(2)}) collective-permute-start(bf16[272,128]{1,0:T(8,128)(2,1)S(1)} %get-tuple-element.119), channel_id=1, source_target_pairs={{0,2},{1,3},{2,0},{3,1},{4,6},{5,7},{6,4},{7,5},{8,10},{9,11},{10,... | collective-permute-start | bytes 208904 | tf_op jit(solution)/shard_map/ppermute | solution.py:300
  51.8 10.4 %collective-permute-start.22 = (bf16[272,128]{1,0:T(8,128)(2,1)S(1)}, bf16[272,128]{1,0:T(8,128)(2,1)S(1)}, u32[]{:S(2)}, u32[]{:S(2)}) collective-permute-start(bf16[272,128]{1,0:T(8,128)(2,1)S(1)} %get-tuple-element.120), channel_id=1, source_target_pairs={{0,3},{1,2},{2,1},{3,0},{4,7},{5,6},{6,5},{7,4},{8,11},{9,10},{10,... | collective-permute-start | bytes 208904 | tf_op jit(solution)/shard_map/ppermute | solution.py:300
  54.5 11.6 %collective-permute-start.10 = (bf16[272,128]{1,0:T(8,128)(2,1)S(1)}, bf16[272,128]{1,0:T(8,128)(2,1)S(1)}, u32[]{:S(2)}, u32[]{:S(2)}) collective-permute-start(bf16[272,128]{1,0:T(8,128)(2,1)S(1)} %get-tuple-element.102.refs_0_), channel_id=1, source_target_pairs={{0,3},{1,2},{2,1},{3,0},{4,7},{5,6},{6,5},{7,4},{8,11},{9,10},{10,... | collective-permute-start | bytes 208904 | tf_op jit(solution)/shard_map/ppermute | solution.py:300
  56.8 13.7 %collective-permute-start.9 = (bf16[272,128]{1,0:T(8,128)(2,1)S(1)}, bf16[272,128]{1,0:T(8,128)(2,1)S(1)}, u32[]{:S(2)}, u32[]{:S(2)}) collective-permute-start(bf16[272,128]{1,0:T(8,128)(2,1)S(1)} %get-tuple-element.102.refs_0_), channel_id=1, source_target_pairs={{0,2},{1,3},{2,0},{3,1},{4,6},{5,7},{6,4},{7,5},{8,10},{9,11},{10,... | collective-permute-start | bytes 208904 | tf_op jit(solution)/shard_map/ppermute | solution.py:300
  62.4 11.9 %collective-permute-start.25 = (bf16[272,128]{1,0:T(8,128)(2,1)S(1)}, bf16[272,128]{1,0:T(8,128)(2,1)S(1)}, u32[]{:S(2)}, u32[]{:S(2)}) collective-permute-start(bf16[272,128]{1,0:T(8,128)(2,1)S(1)} %get-tuple-element.121.refs_0_), channel_id=1, source_target_pairs={{0,3},{1,2},{2,1},{3,0},{4,7},{5,6},{6,5},{7,4},{8,11},{9,10},{10,... | collective-permute-start | bytes 208904 | tf_op jit(solution)/shard_map/ppermute | solution.py:300
  63.8 11.1 %collective-permute-start.24 = (bf16[272,128]{1,0:T(8,128)(2,1)S(1)}, bf16[272,128]{1,0:T(8,128)(2,1)S(1)}, u32[]{:S(2)}, u32[]{:S(2)}) collective-permute-start(bf16[272,128]{1,0:T(8,128)(2,1)S(1)} %get-tuple-element.121.refs_0_), channel_id=1, source_target_pairs={{0,2},{1,3},{2,0},{3,1},{4,6},{5,7},{6,4},{7,5},{8,10},{9,11},{10,... | collective-permute-start | bytes 208904 | tf_op jit(solution)/shard_map/ppermute | solution.py:300
  66.1 8.8 %collective-permute-start.23 = (bf16[272,128]{1,0:T(8,128)(2,1)S(1)}, bf16[272,128]{1,0:T(8,128)(2,1)S(1)}, u32[]{:S(2)}, u32[]{:S(2)}) collective-permute-start(bf16[272,128]{1,0:T(8,128)(2,1)S(1)} %get-tuple-element.121.refs_0_), channel_id=1, source_target_pairs={{0,1},{1,0},{2,3},{3,2},{4,5},{5,4},{6,7},{7,6},{8,9},{9,8},{10,11... | collective-permute-start | bytes 208904 | tf_op jit(solution)/shard_map/ppermute | solution.py:300
  83.0 9.7 %collective-permute-start.12 = (bf16[272,128]{1,0:T(8,128)(2,1)S(1)}, bf16[272,128]{1,0:T(8,128)(2,1)S(1)}, u32[]{:S(2)}, u32[]{:S(2)}) collective-permute-start(bf16[272,128]{1,0:T(8,128)(2,1)S(1)} %get-tuple-element.107), channel_id=1, source_target_pairs={{0,1},{1,0},{2,3},{3,2},{4,5},{5,4},{6,7},{7,6},{8,9},{9,8},{10,11... | collective-permute-start | bytes 208904 | tf_op jit(solution)/shard_map/ppermute | solution.py:300
  84.0 10.3 %collective-permute-start.13 = (bf16[272,128]{1,0:T(8,128)(2,1)S(1)}, bf16[272,128]{1,0:T(8,128)(2,1)S(1)}, u32[]{:S(2)}, u32[]{:S(2)}) collective-permute-start(bf16[272,128]{1,0:T(8,128)(2,1)S(1)} %get-tuple-element.108), channel_id=1, source_target_pairs={{0,2},{1,3},{2,0},{3,1},{4,6},{5,7},{6,4},{7,5},{8,10},{9,11},{10,... | collective-permute-start | bytes 208904 | tf_op jit(solution)/shard_map/ppermute | solution.py:300
  98.7 10.4 %collective-permute-start.32 = (bf16[272,128]{1,0:T(8,128)(2,1)S(1)}, bf16[272,128]{1,0:T(8,128)(2,1)S(1)}, u32[]{:S(2)}, u32[]{:S(2)}) collective-permute-start(bf16[272,128]{1,0:T(8,128)(2,1)S(1)} %get-tuple-element.130.refs_0_), channel_id=1, source_target_pairs={{0,3},{1,2},{2,1},{3,0},{4,7},{5,6},{6,5},{7,4},{8,11},{9,10},{10,... | collective-permute-start | bytes 208904 | tf_op jit(solution)/shard_map/ppermute | solution.py:300
  99.8 11.0 %collective-permute-start.31 = (bf16[272,128]{1,0:T(8,128)(2,1)S(1)}, bf16[272,128]{1,0:T(8,128)(2,1)S(1)}, u32[]{:S(2)}, u32[]{:S(2)}) collective-permute-start(bf16[272,128]{1,0:T(8,128)(2,1)S(1)} %get-tuple-element.130.refs_0_), channel_id=1, source_target_pairs={{0,2},{1,3},{2,0},{3,1},{4,6},{5,7},{6,4},{7,5},{8,10},{9,11},{10,... | collective-permute-start | bytes 208904 | tf_op jit(solution)/shard_map/ppermute | solution.py:300
  124.3 59.4 %collective-permute-start.34 = (f32[2048,128]{1,0:T(8,128)S(1)}, f32[2048,128]{1,0:T(8,128)S(1)}, u32[]{:S(2)}, u32[]{:S(2)}) collective-permute-start(f32[2048,128]{1,0:T(8,128)S(1)} %constant_dynamic-update-slice_fusion), channel_id=1, source_target_pairs={{0,4},{4,0},{8,12},{12,8},{1,5},{5,1},{9,13},{13,9},{2,6},{6,2},{1... | collective-permute-start | bytes 3145736 | tf_op jit(solution)/shard_map/ppermute | solution.py:294
  137.6 9.0 %collective-permute-start.41 = (bf16[272,128]{1,0:T(8,128)(2,1)S(1)}, bf16[272,128]{1,0:T(8,128)(2,1)S(1)}, u32[]{:S(2)}, u32[]{:S(2)}) collective-permute-start(bf16[272,128]{1,0:T(8,128)(2,1)S(1)} %get-tuple-element.144), channel_id=1, source_target_pairs={{0,1},{1,0},{2,3},{3,2},{4,5},{5,4},{6,7},{7,6},{8,9},{9,8},{10,11... | collective-permute-start | bytes 208904 | tf_op jit(solution)/shard_map/ppermute | solution.py:300
  143.4 20.8 %collective-permute-start.40 = (f32[256,128]{1,0:T(8,128)S(1)}, f32[256,128]{1,0:T(8,128)S(1)}, u32[]{:S(2)}, u32[]{:S(2)}) collective-permute-start(f32[256,128]{1,0:T(8,128)S(1)} %dual_update.10.refs_0_), channel_id=1, source_target_pairs={{0,3},{1,2},{2,1},{3,0},{4,7},{5,6},{6,5},{7,4},{8,11},{9,10},{10,... | collective-permute-start | bytes 393224 | tf_op jit(solution)/shard_map/ppermute | solution.py:300
  144.2 21.9 %collective-permute-start.39 = (f32[256,128]{1,0:T(8,128)S(1)}, f32[256,128]{1,0:T(8,128)S(1)}, u32[]{:S(2)}, u32[]{:S(2)}) collective-permute-start(f32[256,128]{1,0:T(8,128)S(1)} %dual_update.10.refs_0_), channel_id=1, source_target_pairs={{0,2},{1,3},{2,0},{3,1},{4,6},{5,7},{6,4},{7,5},{8,10},{9,11},{10,... | collective-permute-start | bytes 393224 | tf_op jit(solution)/shard_map/ppermute | solution.py:300
  146.5 16.6 %collective-permute-start.42 = (bf16[272,128]{1,0:T(8,128)(2,1)S(1)}, bf16[272,128]{1,0:T(8,128)(2,1)S(1)}, u32[]{:S(2)}, u32[]{:S(2)}) collective-permute-start(bf16[272,128]{1,0:T(8,128)(2,1)S(1)} %get-tuple-element.145), channel_id=1, source_target_pairs={{0,2},{1,3},{2,0},{3,1},{4,6},{5,7},{6,4},{7,5},{8,10},{9,11},{10,... | collective-permute-start | bytes 208904 | tf_op jit(solution)/shard_map/ppermute | solution.py:300
  146.6 16.4 %collective-permute-start.43 = (bf16[272,128]{1,0:T(8,128)(2,1)S(1)}, bf16[272,128]{1,0:T(8,128)(2,1)S(1)}, u32[]{:S(2)}, u32[]{:S(2)}) collective-permute-start(bf16[272,128]{1,0:T(8,128)(2,1)S(1)} %get-tuple-element.146), channel_id=1, source_target_pairs={{0,3},{1,2},{2,1},{3,0},{4,7},{5,6},{6,5},{7,4},{8,11},{9,10},{10,... | collective-permute-start | bytes 208904 | tf_op jit(solution)/shard_map/ppermute | solution.py:300
  164.3 13.3 %collective-permute-start.45 = (f32[256,128]{1,0:T(8,128)S(1)}, f32[256,128]{1,0:T(8,128)S(1)}, u32[]{:S(2)}, u32[]{:S(2)}) collective-permute-start(f32[256,128]{1,0:T(8,128)S(1)} %dual_update.11.refs_4_), channel_id=1, source_target_pairs={{0,2},{1,3},{2,0},{3,1},{4,6},{5,7},{6,4},{7,5},{8,10},{9,11},{10,... | collective-permute-start | bytes 393224 | tf_op jit(solution)/shard_map/ppermute | solution.py:300
  166.1 11.5 %collective-permute-start.44 = (f32[256,128]{1,0:T(8,128)S(1)}, f32[256,128]{1,0:T(8,128)S(1)}, u32[]{:S(2)}, u32[]{:S(2)}) collective-permute-start(f32[256,128]{1,0:T(8,128)S(1)} %dual_update.11.refs_4_), channel_id=1, source_target_pairs={{0,1},{1,0},{2,3},{3,2},{4,5},{5,4},{6,7},{7,6},{8,9},{9,8},{10,11... | collective-permute-start | bytes 393224 | tf_op jit(solution)/shard_map/ppermute | solution.py:300
  (41 other events, 257.8 us)

commit v2 on v0

v2 whole, which is shorter than its diff:
```python
import functools

import jax
import jax.numpy as jnp
from jax import lax
from jax.experimental import pallas as pl
from jax.experimental.pallas import tpu as pltpu
from jax.sharding import PartitionSpec as P

ITERS = 3
STEP_SCALE = 0.5
BATCHES = 2
TAIL = 128

bf16 = jnp.bfloat16
f32 = jnp.float32

SMEM = pl.BlockSpec(memory_space=pltpu.SMEM)
VMEM = pl.BlockSpec(memory_space=pltpu.VMEM)
ANY = pl.BlockSpec(memory_space=pl.ANY)


def split_sum(total):
    first = total.astype(bf16).astype(f32)
    rest = total - first
    second = rest.astype(bf16).astype(f32)
    third = rest - second
    lane = lax.broadcasted_iota(jnp.int32, (total.shape[0], TAIL), 1)
    block = jnp.where(lane == 0, first, jnp.where(lane == 1, second, jnp.where(lane == 2, third, 0.0)))
    return block.astype(bf16)


def join_sum(block):
    return jnp.sum(block.astype(f32), axis=1, keepdims=True)


def tree_sum(terms):
    terms = list(terms)
    while len(terms) > 1:
        terms = [terms[k] + terms[k + 1] for k in range(0, len(terms), 2)]
    return terms[0]


def set_state(weight, total):
    lane = lax.broadcasted_iota(jnp.int32, (weight.shape[0], TAIL), 1)
    return jnp.where(lane == 0, weight, jnp.where(lane == 1, total, 0.0))


class Tiles:
    def __init__(self, tile_map, sources, slots, sems, order):
        self.tile_map, self.sources, self.slots, self.sems, self.order = tile_map, sources, slots, sems, order
        self.rows, self.cols = tile_map.shape
        self.size_r, self.size_c = slots.shape[1:]

    def start(self):
        each = self.rows // len(self.sources)
        self.n = jnp.int32(0)
        for i in range(self.rows):
            for j in range(self.cols):
                spot = i * self.cols + j
                nonzero = self.tile_map[i, j] != 0

                @pl.when(nonzero)
                def _():
                    pltpu.make_async_copy(
                        self.sources[i // each].at[
                            pl.ds(i % each * self.size_r, self.size_r), pl.ds(j * self.size_c, self.size_c)
                        ],
                        self.slots.at[spot],
                        self.sems.at[spot],
                    ).start()
                    self.order[self.n] = spot

                self.n = self.n + nonzero.astype(jnp.int32)

    def run(self, body):
        def several(first, width):
            spots = [self.order[first + q] for q in range(width)]
            for spot in spots:
                pltpu.make_async_copy(self.slots.at[spot], self.slots.at[spot], self.sems.at[spot]).wait()
            for spot in spots:
                body(spot // self.cols, spot % self.cols, self.slots[spot])

        def four(u, carry):
            several(u * 4, 4)
            return carry

        lax.fori_loop(0, self.n // 4, four, 0)
        pl.when(self.n % 4 >= 2)(lambda: several(self.n // 4 * 4, 2))
        pl.when(self.n % 2 == 1)(lambda: several(self.n - 1, 1))

    def back(self, vector, acc):
        acc[...] = jnp.zeros_like(acc)

        def body(i, j, tile):
            rows = vector[:, pl.ds(pl.multiple_of(i * self.size_r, self.size_r), self.size_r)]
            acc[:, pl.ds(pl.multiple_of(j * self.size_c, self.size_c), self.size_c)] += jnp.dot(
                rows, tile, preferred_element_type=f32
            )

        self.run(body)

    def forward(self, vector, acc):
        acc[...] = jnp.zeros_like(acc)

        def body(i, j, tile):
            cols = vector[:, pl.ds(pl.multiple_of(j * self.size_c, self.size_c), self.size_c)]
            acc[:, pl.ds(pl.multiple_of(i * self.size_r, self.size_r), self.size_r)] += lax.dot_general(
                cols, tile, (((1,), (1,)), ((), ())), preferred_element_type=f32
            )

        self.run(body)


def first_kernel(tile_map, place, blocks, dual, mine, other, slots, sems, order, vector, acc):
    tiles = Tiles(tile_map, [blocks], slots, sems, order)
    tiles.start()
    vector[...] = dual[...].T.astype(bf16)
    tiles.back(vector, acc)
    size = mine.shape[0]
    mine[...] = acc[pl.ds(pl.multiple_of(place[1] * size, size), size)]
    other[...] = acc[pl.ds(pl.multiple_of((1 - place[1]) * size, size), size)]


def first_pack_kernel(mine, other, *msgs):
    size, width = msgs[0].shape[0], mine.shape[1]
    for b, msg in enumerate(msgs):
        here = pl.ds(b * size, size)
        msg[:, :width] = (mine[here] + other[here]).astype(bf16)
        msg[:, width:] = jnp.zeros((size, TAIL), bf16)


def back_kernel(tile_map, place, own_half, got_half, own, partner, msg, slots, sems, order, vector, acc):
    tiles = Tiles(tile_map, [own, partner], slots, sems, order)
    tiles.start()
    half = vector.shape[1] // 2
    side = place[0] % 2
    vector[:, pl.ds(pl.multiple_of(side * half, half), half)] = own_half[:, :half]
    vector[:, pl.ds(pl.multiple_of((1 - side) * half, half), half)] = got_half[:, :half]
    tiles.back(vector, acc)
    width = acc.shape[1]
    msg[:, :width] = acc[...].astype(bf16)
    msg[:, width:] = split_sum(join_sum(own_half[:, half:]) + join_sum(got_half[:, half:]))


def forward_kernel(near, first, last, total_rows, total_cols, tile_map, place, *refs):
    msgs = refs[:near]
    primal, vectors, state, own, partner = refs[near : near + 5]
    primal_next, kept, sent, state_out, slots, sems, order, vector, acc = refs[near + 5 :]
    tiles = Tiles(tile_map, [own, partner], slots, sems, order)
    tiles.start()
    width = primal.shape[1]
    weight = state[:, 0:1]
    if not first:
        sum_y = tree_sum([join_sum(ref[:, width:]) for ref in msgs])
        move_y = jnp.sqrt(sum_y / total_rows + 1e-06)
        move_x = jnp.sqrt(state[:, 1:2] / total_cols + 1e-06)
        weight = jnp.sqrt(weight * move_y / move_x)
    step = STEP_SCALE / weight
    image_t = tree_sum([ref[:, :width].astype(f32) for ref in msgs])
    before = primal[...]
    after = before - step * (vectors[0:1] - image_t)
    after = jnp.minimum(jnp.maximum(after, vectors[1:2]), vectors[2:3])
    primal_next[...] = after
    vector[...] = (2.0 * after - before).astype(bf16)
    sum_x = jnp.zeros_like(weight) if last else jnp.sum((after - before) ** 2, axis=1, keepdims=True)
    state_out[...] = set_state(weight, sum_x)
    tiles.forward(vector, acc)
    half = acc.shape[1] // 2
    side = place[0] % 2
    kept[...] = acc[:, pl.ds(pl.multiple_of(side * half, half), half)]
    sent[:, :half] = acc[:, pl.ds(pl.multiple_of((1 - side) * half, half), half)].astype(bf16)
    sent[:, half:] = split_sum(sum_x)


def pair_kernel(kept, state, got, msg):
    half = kept.shape[1]
    msg[:, :half] = (kept[...] + got[:, :half].astype(f32)).astype(bf16)
    msg[:, half:] = split_sum(state[:, 1:2] + join_sum(got[:, half:]))


def cross_kernel(own, got, msg):
    half = own.shape[1] - TAIL
    msg[:, :half] = (own[:, :half].astype(f32) + got[:, :half].astype(f32)).astype(bf16)
    msg[:, half:] = split_sum(join_sum(own[:, half:]) + join_sum(got[:, half:]))


def dual_kernel(last, own, got, state, dual, right, floor, dual_next, *outs):
    half = dual.shape[1]
    image = own[:, :half].astype(f32) + got[:, :half].astype(f32)
    before = dual[...]
    weight = state[:, 0:1]
    after = before + STEP_SCALE * weight * (right[...] - image)
    after = jnp.maximum(after, floor[0:1])
    dual_next[...] = after
    if not last:
        msg, state_out = outs
        msg[:, :half] = after.astype(bf16)
        msg[:, half:] = split_sum(jnp.sum((after - before) ** 2, axis=1, keepdims=True))
        state_out[...] = set_state(weight, join_sum(own[:, half:]) + join_sum(got[:, half:]))


def turn_kernel(place, value, *outs):
    size = outs[0].shape[0]
    width = size * len(outs)
    turned = value[:, pl.ds(pl.multiple_of(place[1] * width, width), width)].T
    for b, out in enumerate(outs):
        out[...] = turned[b * size : (b + 1) * size]


def rows_kernel(place, dual, right, got, *outs):
    size = outs[0].shape[0]
    width = size * BATCHES
    rows = dual.shape[0]
    here = pl.ds(pl.multiple_of(place[1] * width, width), width)

    def put(values, outs):
        turned = values.T
        for b, out in enumerate(outs):
            out[...] = turned[b * size : (b + 1) * size]

    @pl.when(place[0] % 2 == 0)
    def _():
        put(dual[:, here], outs[:BATCHES])
        put(right[:, here], outs[BATCHES:])

    @pl.when(place[0] % 2 == 1)
    def _():
        put(got[:rows], outs[:BATCHES])
        put(got[rows:], outs[BATCHES:])


def primal_out_kernel(place, *refs):
    mine, theirs, out = refs[:BATCHES], refs[BATCHES:-1], refs[-1]
    width = out.shape[1] // 2
    out[:, pl.ds(pl.multiple_of(place[1] * width, width), width)] = jnp.concatenate([r[...] for r in mine], axis=0).T
    out[:, pl.ds(pl.multiple_of((1 - place[1]) * width, width), width)] = jnp.concatenate(
        [r[...] for r in theirs], axis=0
    ).T


def choose_kernel(place, own, got, mine, other):
    @pl.when(place[0] % 2 == 0)
    def _():
        mine[...] = own[...]
        other[...] = got[...]

    @pl.when(place[0] % 2 == 1)
    def _():
        mine[...] = got[...]
        other[...] = own[...]


def call(kernel, out_shape, in_specs, scratch=(), flops=0, name=None):
    return pl.pallas_call(
        kernel,
        out_shape=out_shape,
        in_specs=in_specs,
        out_specs=jax.tree.map(lambda _: VMEM, out_shape),
        scratch_shapes=list(scratch),
        compiler_params=pltpu.CompilerParams(vmem_limit_bytes=32 * 1024 * 1024),
        cost_estimate=pl.CostEstimate(flops=flops, bytes_accessed=4 << 20, transcendentals=0),
        name=name,
    )


def shape(rows, cols, kind=f32):
    return jax.ShapeDtypeStruct((rows, cols), kind)


def local(
    blocks,
    tile_map,
    lower_bound,
    upper_bound,
    bound_code,
    row_kind,
    cost_vector,
    right_side,
    primal_start,
    dual_start,
    primal_weight,
):
    rows, cols = blocks.shape
    size_r = rows // tile_map.shape[0]
    size_c = cols // tile_map.shape[1]
    profiles = dual_start.shape[1]
    width = profiles // 2
    size = width // BATCHES
    count = lax.axis_size("col")
    near = lax.axis_size("row") // 2
    total_rows = rows * near * 2
    total_cols = cols * count
    z = lax.axis_index("col")
    core = lax.axis_index("row") % 2
    place = jnp.stack([z, core]).astype(jnp.int32)

    def to_core(value):
        return lax.ppermute(value, "row", [(i, i ^ 1) for i in range(2 * near)])

    def to_x(value, k):
        return lax.ppermute(value, "row", [(i, i ^ (2 * k)) for i in range(2 * near)])

    def to_z(value, k):
        return lax.ppermute(value, "col", [(i, i ^ k) for i in range(count)])

    def scratch(n_tiles, batch, depth, out):
        return [
            pltpu.VMEM((n_tiles, size_r, size_c), bf16),
            pltpu.SemaphoreType.DMA((n_tiles,)),
            pltpu.SMEM((n_tiles,), jnp.int32),
            pltpu.VMEM((batch, depth), bf16),
            pltpu.VMEM((batch, out), f32),
        ]

    n_own = tile_map.size
    n_chip = 2 * n_own

    with jax.named_scope("first_product"):
        mine, other = call(
            first_kernel,
            (shape(width, cols),) * 2,
            [SMEM, SMEM, ANY, VMEM],
            scratch(n_own, profiles, rows, cols),
            flops=2 * rows * cols * profiles,
            name="first_product",
        )(tile_map, place, blocks, dual_start)
    other = to_core(other)
    messages = list(
        call(first_pack_kernel, (shape(size, cols + TAIL, bf16),) * BATCHES, [VMEM] * 2, name="first_pack")(
            mine, other
        )
    )
    partner = to_core(blocks)
    chip_map = jnp.concatenate([tile_map, to_core(tile_map)], axis=0)

    primal = list(call(turn_kernel, (shape(size, cols),) * BATCHES, [SMEM, VMEM], name="turn_primal")(place, primal_start))
    low_on = (bound_code == 1) | (bound_code == 3)
    high_on = (bound_code == 2) | (bound_code == 3)
    vectors = jnp.stack(
        [cost_vector, jnp.where(low_on, lower_bound, -jnp.inf), jnp.where(high_on, upper_bound, jnp.inf)]
    )

    def other_half(value):
        return lax.dynamic_slice_in_dim(value, (1 - core) * width, width, 1)

    received = to_core(jnp.concatenate([other_half(dual_start), other_half(right_side)], axis=0))
    kind = jnp.where(z % 2 == 0, row_kind, to_core(row_kind))
    floor = jnp.where(kind == 1, 0.0, -jnp.inf).astype(f32)[None, :]
    held = call(
        rows_kernel, (shape(size, rows),) * (2 * BATCHES), [SMEM] + [VMEM] * 3, name="turn_rows"
    )(place, dual_start, right_side, received)
    dual, right = list(held[:BATCHES]), held[BATCHES:]

    weight = lax.dynamic_slice_in_dim(primal_weight, core * width, width, 0)
    state = [jnp.broadcast_to(weight[b * size : (b + 1) * size, None], (size, TAIL)) for b in range(BATCHES)]

    flops = 2 * (2 * rows) * cols * size
    half_msg = shape(size, rows + TAIL, bf16)
    halves = [None] * BATCHES
    for iteration in range(ITERS):
        first, last = iteration == 0, iteration + 1 == ITERS
        for b in range(BATCHES):
            if not first:
                messages[b] = call(
                    back_kernel,
                    shape(size, cols + TAIL, bf16),
                    [SMEM, SMEM, VMEM, VMEM, ANY, ANY],
                    scratch(n_chip, size, 2 * rows, cols),
                    flops=flops,
                    name="back_product",
                )(chip_map, place, *halves[b], blocks, partner)
            x_msgs = [messages[b]] + [to_x(messages[b], k) for k in range(1, near)]
            primal[b], kept, sent, state[b] = call(
                functools.partial(forward_kernel, near, first, last, total_rows, total_cols),
                (shape(size, cols), shape(size, rows), half_msg, shape(size, TAIL)),
                [SMEM, SMEM] + [VMEM] * (near + 3) + [ANY, ANY],
                scratch(n_chip, size, cols, 2 * rows),
                flops=flops,
                name="forward_product",
            )(chip_map, place, *x_msgs, primal[b], vectors, state[b], blocks, partner)
            own = call(pair_kernel, half_msg, [VMEM] * 3, name="pair_sum")(kept, state[b], to_z(sent, 1))
            mask = 2
            while mask * 2 < count:
                own = call(cross_kernel, half_msg, [VMEM] * 2, name="cross_sum")(own, to_z(own, mask))
                mask *= 2
            got = to_z(own, mask)
            out_shape = (shape(size, rows),)
            if not last:
                out_shape += (half_msg, shape(size, TAIL))
            outs = call(functools.partial(dual_kernel, last), out_shape, [VMEM] * 6, name="dual_update")(
                own, got, state[b], dual[b], right[b], floor
            )
            dual[b] = outs[0]
            if not last:
                state[b] = outs[2]
                halves[b] = (outs[1], to_z(outs[1], 1))

    primal_final = call(
        primal_out_kernel, shape(cols, profiles), [SMEM] + [VMEM] * (2 * BATCHES), name="primal_out"
    )(place, *primal, *[to_core(p) for p in primal])
    mine, theirs = [], []
    for b in range(BATCHES):
        own, other = call(choose_kernel, (shape(size, rows),) * 2, [SMEM, VMEM, VMEM], name="choose_rows")(
            place, dual[b], to_z(dual[b], 1)
        )
        mine.append(own)
        theirs.append(to_core(other))
    dual_final = call(
        primal_out_kernel, shape(rows, profiles), [SMEM] + [VMEM] * (2 * BATCHES), name="dual_out"
    )(place, *mine, *theirs)
    return primal_final, dual_final


def solution(mesh):
    return jax.shard_map(
        local,
        mesh=mesh,
        in_specs=(
            P("row", "col"),
            P("row", "col"),
            P("col"),
            P("col"),
            P("col"),
            P("row"),
            P("col"),
            P("row", "groups"),
            P("col", "groups"),
            P("row", "groups"),
            P("groups"),
        ),
        out_specs=(P("col", "groups"), P("row", "groups")),
        check_vma=False,
    )
```

time: 375 us -> 157 us (0.42)
  waiting for transfers between devices: 279 us -> 56.3 us
  Pallas kernels: 0 us -> 56.4 us
  blocking collectives: 31.8 us -> 0 us
  starting transfers between devices: 0.43 us -> 23.9 us
  other arithmetic: 23.1 us -> 1.86 us
  matrix products: 15 us -> 0 us
  between operations: 14.3 us -> 1.16 us
  local copies, waits for them, and re-layouts: 10.2 us -> 15.7 us
    psum x6 -> x0, waiting for transfers between devices: 279 us -> none  [the longest x3 157 us: local(): image = lax.psum(partial_image, 'col')]
    pallas_call x0 -> x30, Pallas kernels: none -> 56.4 us  [the longest x6 26.2 us: local(): call(functools.partial(forward_kernel, near, first, last, total_rows, tot...]
    ppermute x0 -> x33, waiting for transfers between devices: none -> 56.3 us  [the longest x18 42 us: to_z(): return lax.ppermute(value, 'col', [(i, i ^ k) for i in range(count)])]
    psum x4 -> x0, blocking collectives: 31.8 us -> none  [the longest x2 16.2 us: local(): sum_x = lax.psum(jnp.sum((primal_next - primal) ** 2, axis=0), 'col')]
    ppermute x0 -> x33, starting transfers between devices: none -> 23.9 us  [the longest x9 17 us: to_core(): return lax.ppermute(value, 'row', [(i, i ^ 1) for i in range(2 * near)])]
    dot_general x6 -> x0, matrix products: 15 us -> none  [the longest x3 8.15 us: transpose_product(): lax.dot_general(matrix, vector, (((0,), (0,)), ((), ())), preferred_eleme...]
    reduce_sum x4 -> x0, other arithmetic: 13.5 us -> none  [the longest x2 9.47 us: local(): sum_x = lax.psum(jnp.sum((primal_next - primal) ** 2, axis=0), 'col')]
    unnamed x43 -> x50, local copies, waits for them, and re-layouts: 8.72 us -> 15.3 us
  transfers between devices with their start and end apart: 6 -> 33, of which waited for: 6 -> 14; matrix products, arithmetic and copies ran while one was open for 0% -> 1% of each run, Pallas kernels for 0% -> 35%
where the time goes in v2:
time: 157 us; the launch traced here: 155 us
  Pallas kernels  56.4 us (36%)
  waiting for transfers between devices  56.3 us (36%)
  starting transfers between devices  23.9 us (15%)
  local copies, waits for them, and re-layouts  15.7 us (10%)
  other arithmetic  1.86 us (1%)
    ppermute x18, waiting for transfers between devices, to_z(): return lax.ppermute(value, 'col', [(i, i ^ k) for i in range(count)])  42 us
    pallas_call x6, Pallas kernels, local(): call(functools.partial(forward_kernel, near, first, last, total_rows, tot...  26.2 us
    ppermute x9, starting transfers between devices, to_core(): return lax.ppermute(value, 'row', [(i, i ^ 1) for i in range(2 * near)])  17 us
    unnamed x50, local copies, waits for them, and re-layouts  15.3 us
    ppermute x6, waiting for transfers between devices, to_x(): return lax.ppermute(value, 'row', [(i, i ^ 2 * k) for i in range(2 * near)])  14.3 us
    pallas_call x4, Pallas kernels, local(): call(back_kernel, shape(size, cols + TAIL, bf16), [SMEM, SMEM, VMEM, VMEM...  14 us
    ppermute x18, starting transfers between devices, to_z(): return lax.ppermute(value, 'col', [(i, i ^ k) for i in range(count)])  4.92 us
    pallas_call x1, Pallas kernels, local(): call(first_kernel, (shape(width, cols),) * 2, [SMEM, SMEM, ANY, VMEM], sc...  3.36 us
  transfers between devices with their start and end apart: 33, of which 14 were waited for; matrix products, arithmetic and copies ran while one was open for 1% of the time, Pallas kernels for 35%

profile of v2, /device:TPU:5, one launch (start us, length us, event | category | flops | bytes accessed | tf_op | source)
XLA Modules:
  0.0 155.3 jit_solution(12083468076311352414)
XLA Ops:
  4.9 3.4 %first_product.1 = (f32[128,2048]{1,0:T(8,128)S(1)}, f32[128,2048]{1,0:T(8,128)}) custom-call(s32[2,4]{1,0:T(2,128)} %tile_map.1, s32[2]{0:T(128)S(1)} %pad_add_fusion.1.place, bf16[1024,2048]{1,0:T(8,128)(2,1)S(1)} %copy-done, f32[1024,256]{1,0:T(8,128)S(1)} %copy-done.3), custom_call_target="tpu_custom_call" | custom-call | flops 1073741824 | bytes 4194304 | tf_op jit(solution)/shard_map/first_product/first_product/pallas_call | solution.py:320
  20.7 6.0 %collective-permute-done.14.refs_1_ = bf16[64,2176]{1,0:T(8,128)(2,1)S(1)} collective-permute-done((bf16[64,2176]{1,0:T(8,128)(2,1)S(1)}, bf16[64,2176]{1,0:T(8,128)(2,1)S(1)}, u32[]{:S(2)}, u32[]{:S(2)}) %collective-permute-start.14) | collective-permute-done | bytes 278560 | tf_op jit(solution)/shard_map/ppermute | solution.py:302
  30.0 4.8 %forward_product.9 = (f32[64,2048]{1,0:T(8,128)S(1)}, f32[64,1024]{1,0:T(8,128)S(1)}, bf16[64,1152]{1,0:T(8,128)(2,1)}, f32[64,128]{1,0:T(8,128)S(1)}) custom-call(s32[4,4]{1,0:T(4,128)S(1)} %pad_add_fusion.tile_map, s32[2]{0:T(128)S(1)} %pad_add_fusion.1.place, bf16[64,2176]{1,0:T(8,128)(2,1)S(1)} %get-tuple-element.72.refs_0_, ...), custom_call_target="tpu_custom_call" | custom-call | flops 536870912 | bytes 4194304 | tf_op jit(solution)/shard_map/forward_product/pallas_call | solution.py:374
  35.7 4.8 %forward_product.6 = (f32[64,2048]{1,0:T(8,128)S(1)}, f32[64,1024]{1,0:T(8,128)S(1)}, bf16[64,1152]{1,0:T(8,128)(2,1)}, f32[64,128]{1,0:T(8,128)S(1)}) custom-call(s32[4,4]{1,0:T(4,128)S(1)} %pad_add_fusion.tile_map, s32[2]{0:T(128)S(1)} %pad_add_fusion.1.place, bf16[64,2176]{1,0:T(8,128)(2,1)S(1)} %get-tuple-element.54.refs_0_, ...), custom_call_target="tpu_custom_call" | custom-call | flops 536870912 | bytes 4194304 | tf_op jit(solution)/shard_map/forward_product/pallas_call | solution.py:374
  50.9 7.3 %collective-permute-done.16.got = bf16[64,1152]{1,0:T(8,128)(2,1)S(1)} collective-permute-done((bf16[64,1152]{1,0:T(8,128)(2,1)S(1)}, bf16[64,1152]{1,0:T(8,128)(2,1)S(1)}, u32[]{:S(2)}, u32[]{:S(2)}) %collective-permute-start.16) | collective-permute-done | bytes 147488 | tf_op jit(solution)/shard_map/ppermute | solution.py:305
  58.5 2.8 %collective-permute-done.5.got = bf16[64,1152]{1,0:T(8,128)(2,1)S(1)} collective-permute-done((bf16[64,1152]{1,0:T(8,128)(2,1)S(1)}, bf16[64,1152]{1,0:T(8,128)(2,1)S(1)}, u32[]{:S(2)}, u32[]{:S(2)}) %collective-permute-start.5) | collective-permute-done | bytes 147488 | tf_op jit(solution)/shard_map/ppermute | solution.py:305
  63.7 3.5 %back_product.6.refs_0_ = bf16[64,2176]{1,0:T(8,128)(2,1)S(1)} custom-call(s32[4,4]{1,0:T(4,128)S(1)} %pad_add_fusion.tile_map, s32[2]{0:T(128)S(1)} %pad_add_fusion.1.place, bf16[64,1152]{1,0:T(8,128)(2,1)S(1)} %get-tuple-element.79.own_half, bf16[64,1152]{1,0:T(8,128)(2,1)S(1)} %collective-permute-done.17.got_half, bf16[1024,2048]{1,0:T(8,128)(2,1)S(1)} %copy-done.2, ...), custom_call_target="tpu_custom_call" | custom-call | flops 536870912 | bytes 4194304 | tf_op jit(solution)/shard_map/back_product/pallas_call | solution.py:365
  67.4 3.5 %back_product.4.refs_0_ = bf16[64,2176]{1,0:T(8,128)(2,1)S(1)} custom-call(s32[4,4]{1,0:T(4,128)S(1)} %pad_add_fusion.tile_map, s32[2]{0:T(128)S(1)} %pad_add_fusion.1.place, bf16[64,1152]{1,0:T(8,128)(2,1)S(1)} %get-tuple-element.61.own_half, bf16[64,1152]{1,0:T(8,128)(2,1)S(1)} %collective-permute-done.8.got_half, bf16[1024,2048]{1,0:T(8,128)(2,1)S(1)} %copy-done.2, ...), custom_call_target="tpu_custom_call" | custom-call | flops 536870912 | bytes 4194304 | tf_op jit(solution)/shard_map/back_product/pallas_call | solution.py:365
  71.0 2.7 %collective-permute-done.18.refs_1_ = bf16[64,2176]{1,0:T(8,128)(2,1)S(1)} collective-permute-done((bf16[64,2176]{1,0:T(8,128)(2,1)S(1)}, bf16[64,2176]{1,0:T(8,128)(2,1)S(1)}, u32[]{:S(2)}, u32[]{:S(2)}) %collective-permute-start.18) | collective-permute-done | bytes 278560 | tf_op jit(solution)/shard_map/ppermute | solution.py:302
  73.7 4.3 %forward_product.10 = (f32[64,2048]{1,0:T(8,128)S(1)}, f32[64,1024]{1,0:T(8,128)S(1)}, bf16[64,1152]{1,0:T(8,128)(2,1)S(1)}, f32[64,128]{1,0:T(8,128)S(1)}) custom-call(s32[4,4]{1,0:T(4,128)S(1)} %pad_add_fusion.tile_map, s32[2]{0:T(128)S(1)} %pad_add_fusion.1.place, bf16[64,2176]{1,0:T(8,128)(2,1)S(1)} %back_product.6.refs_0_, ...), custom_call_target="tpu_custom_call" | custom-call | flops 536870912 | bytes 4194304 | tf_op jit(solution)/shard_map/forward_product/pallas_call | solution.py:374
  79.7 4.5 %forward_product.7 = (f32[64,2048]{1,0:T(8,128)S(1)}, f32[64,1024]{1,0:T(8,128)S(1)}, bf16[64,1152]{1,0:T(8,128)(2,1)S(1)}, f32[64,128]{1,0:T(8,128)S(1)}) custom-call(s32[4,4]{1,0:T(4,128)S(1)} %pad_add_fusion.tile_map, s32[2]{0:T(128)S(1)} %pad_add_fusion.1.place, bf16[64,2176]{1,0:T(8,128)(2,1)S(1)} %back_product.4.refs_0_, ...), custom_call_target="tpu_custom_call" | custom-call | flops 536870912 | bytes 4194304 | tf_op jit(solution)/shard_map/forward_product/pallas_call | solution.py:374
  84.7 6.0 %collective-permute-done.10.got = bf16[64,1152]{1,0:T(8,128)(2,1)S(1)} collective-permute-done((bf16[64,1152]{1,0:T(8,128)(2,1)S(1)}, bf16[64,1152]{1,0:T(8,128)(2,1)S(1)}, u32[]{:S(2)}, u32[]{:S(2)}) %collective-permute-start.10) | collective-permute-done | bytes 147488 | tf_op jit(solution)/shard_map/ppermute | solution.py:305
  92.1 8.8 %collective-permute-done.11.got = bf16[64,1152]{1,0:T(8,128)(2,1)S(1)} collective-permute-done((bf16[64,1152]{1,0:T(8,128)(2,1)S(1)}, bf16[64,1152]{1,0:T(8,128)(2,1)S(1)}, u32[]{:S(2)}, u32[]{:S(2)}) %collective-permute-start.11) | collective-permute-done | bytes 147488 | tf_op jit(solution)/shard_map/ppermute | solution.py:305
  101.3 3.5 %back_product.7.refs_0_ = bf16[64,2176]{1,0:T(8,128)(2,1)S(1)} custom-call(s32[4,4]{1,0:T(4,128)S(1)} %pad_add_fusion.tile_map, s32[2]{0:T(128)S(1)} %pad_add_fusion.1.place, bf16[64,1152]{1,0:T(8,128)(2,1)S(1)} %get-tuple-element.86.own_half, bf16[64,1152]{1,0:T(8,128)(2,1)S(1)} %collective-permute-done.21.got_half, bf16[1024,2048]{1,0:T(8,128)(2,1)S(1)} %copy-done.2, ...), custom_call_target="tpu_custom_call" | custom-call | flops 536870912 | bytes 4194304 | tf_op jit(solution)/shard_map/back_product/pallas_call | solution.py:365
  106.9 3.5 %back_product.5.refs_0_ = bf16[64,2176]{1,0:T(8,128)(2,1)S(1)} custom-call(s32[4,4]{1,0:T(4,128)S(1)} %pad_add_fusion.tile_map, s32[2]{0:T(128)S(1)} %pad_add_fusion.1.place, bf16[64,1152]{1,0:T(8,128)(2,1)S(1)} %get-tuple-element.68.own_half, bf16[64,1152]{1,0:T(8,128)(2,1)S(1)} %collective-permute-done.12.got_half, bf16[1024,2048]{1,0:T(8,128)(2,1)S(1)} %copy-done.2, ...), custom_call_target="tpu_custom_call" | custom-call | flops 536870912 | bytes 4194304 | tf_op jit(solution)/shard_map/back_product/pallas_call | solution.py:365
  110.5 3.9 %forward_product.11 = (f32[64,2048]{1,0:T(8,128)S(1)}, f32[64,1024]{1,0:T(8,128)S(1)}, bf16[64,1152]{1,0:T(8,128)(2,1)S(1)}, f32[64,128]{1,0:T(8,128)S(1)}) custom-call(s32[4,4]{1,0:T(4,128)S(1)} %pad_add_fusion.tile_map, s32[2]{0:T(128)S(1)} %pad_add_fusion.1.place, bf16[64,2176]{1,0:T(8,128)(2,1)S(1)} %back_product.7.refs_0_, ...), custom_call_target="tpu_custom_call" | custom-call | flops 536870912 | bytes 4194304 | tf_op jit(solution)/shard_map/forward_product/pallas_call | solution.py:374
  114.5 3.9 %collective-permute-done.13.refs_1_ = bf16[64,2176]{1,0:T(8,128)(2,1)S(1)} collective-permute-done((bf16[64,2176]{1,0:T(8,128)(2,1)S(1)}, bf16[64,2176]{1,0:T(8,128)(2,1)S(1)}, u32[]{:S(2)}, u32[]{:S(2)}) %collective-permute-start.13) | collective-permute-done | bytes 278560 | tf_op jit(solution)/shard_map/ppermute | solution.py:302
  118.4 3.9 %forward_product.8 = (f32[64,2048]{1,0:T(8,128)S(1)}, f32[64,1024]{1,0:T(8,128)S(1)}, bf16[64,1152]{1,0:T(8,128)(2,1)S(1)}, f32[64,128]{1,0:T(8,128)S(1)}) custom-call(s32[4,4]{1,0:T(4,128)S(1)} %pad_add_fusion.tile_map, s32[2]{0:T(128)S(1)} %pad_add_fusion.1.place, bf16[64,2176]{1,0:T(8,128)(2,1)S(1)} %back_product.5.refs_0_, ...), custom_call_target="tpu_custom_call" | custom-call | flops 536870912 | bytes 4194304 | tf_op jit(solution)/shard_map/forward_product/pallas_call | solution.py:374
  122.6 5.4 %collective-permute-done.25.got = bf16[64,1152]{1,0:T(8,128)(2,1)S(1)} collective-permute-done((bf16[64,1152]{1,0:T(8,128)(2,1)S(1)}, bf16[64,1152]{1,0:T(8,128)(2,1)S(1)}, u32[]{:S(2)}, u32[]{:S(2)}) %collective-permute-start.25) | collective-permute-done | bytes 147488 | tf_op jit(solution)/shard_map/ppermute | solution.py:305
  128.4 5.3 %collective-permute-start.24 = (f32[64,2048]{1,0:T(8,128)S(1)}, f32[64,2048]{1,0:T(8,128)S(1)}, u32[]{:S(2)}, u32[]{:S(2)}) collective-permute-start(f32[64,2048]{1,0:T(8,128)S(1)} %get-tuple-element.89.refs_1_), channel_id=1, source_target_pairs={{0,4},{4,0},{8,12},{12,8},{1,5},{5,1},{9,13},{13,9},{2,6},{6,2},{1... | collective-permute-start | bytes 1572872 | tf_op jit(solution)/shard_map/ppermute | solution.py:299
  135.8 6.2 %collective-permute-done.30.got = f32[64,1024]{1,0:T(8,128)S(1)} collective-permute-done((f32[64,1024]{1,0:T(8,128)S(1)}, f32[64,1024]{1,0:T(8,128)S(1)}, u32[]{:S(2)}, u32[]{:S(2)}) %collective-permute-start.30) | collective-permute-done | bytes 262176 | tf_op jit(solution)/shard_map/ppermute | solution.py:305
  142.6 5.1 %collective-permute-start.32 = (f32[64,1024]{1,0:T(8,128)S(1)}, f32[64,1024]{1,0:T(8,128)S(1)}, u32[]{:S(2)}, u32[]{:S(2)}) collective-permute-start(f32[64,1024]{1,0:T(8,128)S(1)} %get-tuple-element.101), channel_id=1, source_target_pairs={{0,4},{4,0},{8,12},{12,8},{1,5},{5,1},{9,13},{13,9},{2,6},{6,2},{1... | collective-permute-start | bytes 786440 | tf_op jit(solution)/shard_map/ppermute | solution.py:299
  148.3 2.7 %collective-permute-start.31 = (f32[64,1024]{1,0:T(8,128)S(1)}, f32[64,1024]{1,0:T(8,128)S(1)}, u32[]{:S(2)}, u32[]{:S(2)}) collective-permute-start(f32[64,1024]{1,0:T(8,128)S(1)} %get-tuple-element.100), channel_id=1, source_target_pairs={{0,4},{4,0},{8,12},{12,8},{1,5},{5,1},{9,13},{13,9},{2,6},{6,2},{1... | collective-permute-start | bytes 786440 | tf_op jit(solution)/shard_map/ppermute | solution.py:299
  151.0 2.5 %primal_out.1 = f32[2048,256]{1,0:T(8,128)} custom-call(s32[2]{0:T(128)S(1)} %pad_add_fusion.1.place, f32[64,2048]{1,0:T(8,128)S(1)} %get-tuple-element.71.refs_0_, f32[64,2048]{1,0:T(8,128)S(1)} %get-tuple-element.89.refs_1_, f32[64,2048]{1,0:T(8,128)S(1)} %collective-permute-done.23.refs_2_, f32[64,2048]{1,0:T(8,128)S(1)} %collective-permute-done.24.refs_3_), custom_call_target="tpu_custom_call" | custom-call | bytes 4194304 | tf_op jit(solution)/shard_map/primal_out/pallas_call | solution.py:399
  (134 shorter events, 45.9 us)
Async XLA Ops:
  0.6 26.1 %collective-permute-start.3 = (bf16[1024,2048]{1,0:T(8,128)(2,1)}, bf16[1024,2048]{1,0:T(8,128)(2,1)}, u32[]{:S(2)}, u32[]{:S(2)}) collective-permute-start(bf16[1024,2048]{1,0:T(8,128)(2,1)} %refs_5_.11), channel_id=1, source_target_pairs={{0,4},{4,0},{8,12},{12,8},{1,5},{5,1},{9,13},{13,9},{2,6},{6,2},{1... | collective-permute-start | bytes 12582920 | tf_op jit(solution)/shard_map/ppermute | solution.py:299
  9.2 6.6 %collective-permute-start.1 = (f32[128,2048]{1,0:T(8,128)}, f32[128,2048]{1,0:T(8,128)}, u32[]{:S(2)}, u32[]{:S(2)}) collective-permute-start(f32[128,2048]{1,0:T(8,128)} %get-tuple-element.53), channel_id=1, source_target_pairs={{0,4},{4,0},{8,12},{12,8},{1,5},{5,1},{9,13},{13,9},{2,6},{6,2},{1... | collective-permute-start | bytes 3145736 | tf_op jit(solution)/shard_map/ppermute | solution.py:299
  9.9 10.1 %collective-permute-start = (s32[2,4]{1,0:T(2,128)}, s32[2,4]{1,0:T(2,128)S(1)}, u32[]{:S(2)}, u32[]{:S(2)}) collective-permute-start(s32[2,4]{1,0:T(2,128)} %tile_map.1), channel_id=1, source_target_pairs={{0,4},{4,0},{8,12},{12,8},{1,5},{5,1},{9,13},{13,9},{2,6},{6,2},{1... | collective-permute-start | bytes 104 | tf_op jit(solution)/shard_map/ppermute | solution.py:299
  11.1 38.9 %collective-permute-start.6 = (f32[2048,128]{1,0:T(8,128)}, f32[2048,128]{1,0:T(8,128)S(1)}, u32[]{:S(2)}, u32[]{:S(2)}) collective-permute-start(f32[2048,128]{1,0:T(8,128)} %pad_maximum_fusion), channel_id=1, source_target_pairs={{0,4},{4,0},{8,12},{12,8},{1,5},{5,1},{9,13},{13,9},{2,6},{6,2},{1... | collective-permute-start | bytes 3145736 | tf_op jit(solution)/shard_map/ppermute | solution.py:299
  18.4 8.3 %collective-permute-start.14 = (bf16[64,2176]{1,0:T(8,128)(2,1)S(1)}, bf16[64,2176]{1,0:T(8,128)(2,1)S(1)}, u32[]{:S(2)}, u32[]{:S(2)}) collective-permute-start(bf16[64,2176]{1,0:T(8,128)(2,1)S(1)} %get-tuple-element.72.refs_0_), channel_id=1, source_target_pairs={{0,8},{4,12},{8,0},{12,4},{1,9},{5,13},{9,1},{13,5},{2,10},{6,14},... | collective-permute-start | bytes 835592 | tf_op jit(solution)/shard_map/ppermute | solution.py:302
  18.5 17.2 %collective-permute-start.2 = (bf16[64,2176]{1,0:T(8,128)(2,1)S(1)}, bf16[64,2176]{1,0:T(8,128)(2,1)S(1)}, u32[]{:S(2)}, u32[]{:S(2)}) collective-permute-start(bf16[64,2176]{1,0:T(8,128)(2,1)S(1)} %get-tuple-element.54.refs_0_), channel_id=1, source_target_pairs={{0,8},{4,12},{8,0},{12,4},{1,9},{5,13},{9,1},{13,5},{2,10},{6,14},... | collective-permute-start | bytes 835592 | tf_op jit(solution)/shard_map/ppermute | solution.py:302
  35.6 8.5 %collective-permute-start.15 = (bf16[64,1152]{1,0:T(8,128)(2,1)}, bf16[64,1152]{1,0:T(8,128)(2,1)}, u32[]{:S(2)}, u32[]{:S(2)}) collective-permute-start(bf16[64,1152]{1,0:T(8,128)(2,1)} %get-tuple-element.76), channel_id=1, source_target_pairs={{0,1},{1,0},{2,3},{3,2},{4,5},{5,4},{6,7},{7,6},{8,9},{9,8},{10,11... | collective-permute-start | bytes 442376 | tf_op jit(solution)/shard_map/ppermute | solution.py:305
  42.0 7.9 %collective-permute-start.7 = (s32[1024]{0:T(1024)S(1)}, s32[1024]{0:T(1024)S(1)}, u32[]{:S(2)}, u32[]{:S(2)}) collective-permute-start(s32[1024]{0:T(1024)S(1)} %copy-done.23), channel_id=1, source_target_pairs={{0,4},{4,0},{8,12},{12,8},{1,5},{5,1},{9,13},{13,9},{2,6},{6,2},{1... | collective-permute-start | bytes 12296 | tf_op jit(solution)/shard_map/ppermute | solution.py:299
  45.4 12.8 %collective-permute-start.16 = (bf16[64,1152]{1,0:T(8,128)(2,1)S(1)}, bf16[64,1152]{1,0:T(8,128)(2,1)S(1)}, u32[]{:S(2)}, u32[]{:S(2)}) collective-permute-start(bf16[64,1152]{1,0:T(8,128)(2,1)S(1)} %pair_sum.8.own), channel_id=1, source_target_pairs={{0,2},{1,3},{2,0},{3,1},{4,6},{5,7},{6,4},{7,5},{8,10},{9,11},{10,... | collective-permute-start | bytes 442376 | tf_op jit(solution)/shard_map/ppermute | solution.py:305
  48.4 12.9 %collective-permute-start.5 = (bf16[64,1152]{1,0:T(8,128)(2,1)S(1)}, bf16[64,1152]{1,0:T(8,128)(2,1)S(1)}, u32[]{:S(2)}, u32[]{:S(2)}) collective-permute-start(bf16[64,1152]{1,0:T(8,128)(2,1)S(1)} %pair_sum.6.own), channel_id=1, source_target_pairs={{0,2},{1,3},{2,0},{3,1},{4,6},{5,7},{6,4},{7,5},{8,10},{9,11},{10,... | collective-permute-start | bytes 442376 | tf_op jit(solution)/shard_map/ppermute | solution.py:305
  70.9 8.8 %collective-permute-start.9 = (bf16[64,2176]{1,0:T(8,128)(2,1)S(1)}, bf16[64,2176]{1,0:T(8,128)(2,1)S(1)}, u32[]{:S(2)}, u32[]{:S(2)}) collective-permute-start(bf16[64,2176]{1,0:T(8,128)(2,1)S(1)} %back_product.4.refs_0_), channel_id=1, source_target_pairs={{0,8},{4,12},{8,0},{12,4},{1,9},{5,13},{9,1},{13,5},{2,10},{6,14},... | collective-permute-start | bytes 835592 | tf_op jit(solution)/shard_map/ppermute | solution.py:302
  84.2 6.6 %collective-permute-start.10 = (bf16[64,1152]{1,0:T(8,128)(2,1)S(1)}, bf16[64,1152]{1,0:T(8,128)(2,1)S(1)}, u32[]{:S(2)}, u32[]{:S(2)}) collective-permute-start(bf16[64,1152]{1,0:T(8,128)(2,1)S(1)} %get-tuple-element.66), channel_id=1, source_target_pairs={{0,1},{1,0},{2,3},{3,2},{4,5},{5,4},{6,7},{7,6},{8,9},{9,8},{10,11... | collective-permute-start | bytes 442376 | tf_op jit(solution)/shard_map/ppermute | solution.py:305
  84.5 6.6 %collective-permute-start.20 = (bf16[64,1152]{1,0:T(8,128)(2,1)S(1)}, bf16[64,1152]{1,0:T(8,128)(2,1)S(1)}, u32[]{:S(2)}, u32[]{:S(2)}) collective-permute-start(bf16[64,1152]{1,0:T(8,128)(2,1)S(1)} %pair_sum.9.own), channel_id=1, source_target_pairs={{0,2},{1,3},{2,0},{3,1},{4,6},{5,7},{6,4},{7,5},{8,10},{9,11},{10,... | collective-permute-start | bytes 442376 | tf_op jit(solution)/shard_map/ppermute | solution.py:305
  91.0 10.0 %collective-permute-start.11 = (bf16[64,1152]{1,0:T(8,128)(2,1)S(1)}, bf16[64,1152]{1,0:T(8,128)(2,1)S(1)}, u32[]{:S(2)}, u32[]{:S(2)}) collective-permute-start(bf16[64,1152]{1,0:T(8,128)(2,1)S(1)} %pair_sum.7.own), channel_id=1, source_target_pairs={{0,2},{1,3},{2,0},{3,1},{4,6},{5,7},{6,4},{7,5},{8,10},{9,11},{10,... | collective-permute-start | bytes 442376 | tf_op jit(solution)/shard_map/ppermute | solution.py:305
  91.3 10.0 %collective-permute-start.21 = (bf16[64,1152]{1,0:T(8,128)(2,1)S(1)}, bf16[64,1152]{1,0:T(8,128)(2,1)S(1)}, u32[]{:S(2)}, u32[]{:S(2)}) collective-permute-start(bf16[64,1152]{1,0:T(8,128)(2,1)S(1)} %get-tuple-element.86.own_half), channel_id=1, source_target_pairs={{0,1},{1,0},{2,3},{3,2},{4,5},{5,4},{6,7},{7,6},{8,9},{9,8},{10,11... | collective-permute-start | bytes 442376 | tf_op jit(solution)/shard_map/ppermute | solution.py:305
  110.4 8.0 %collective-permute-start.13 = (bf16[64,2176]{1,0:T(8,128)(2,1)S(1)}, bf16[64,2176]{1,0:T(8,128)(2,1)S(1)}, u32[]{:S(2)}, u32[]{:S(2)}) collective-permute-start(bf16[64,2176]{1,0:T(8,128)(2,1)S(1)} %back_product.5.refs_0_), channel_id=1, source_target_pairs={{0,8},{4,12},{8,0},{12,4},{1,9},{5,13},{9,1},{13,5},{2,10},{6,14},... | collective-permute-start | bytes 835592 | tf_op jit(solution)/shard_map/ppermute | solution.py:302
  114.4 7.9 %collective-permute-start.28 = (bf16[64,1152]{1,0:T(8,128)(2,1)S(1)}, bf16[64,1152]{1,0:T(8,128)(2,1)S(1)}, u32[]{:S(2)}, u32[]{:S(2)}) collective-permute-start(bf16[64,1152]{1,0:T(8,128)(2,1)S(1)} %get-tuple-element.97), channel_id=1, source_target_pairs={{0,1},{1,0},{2,3},{3,2},{4,5},{5,4},{6,7},{7,6},{8,9},{9,8},{10,11... | collective-permute-start | bytes 442376 | tf_op jit(solution)/shard_map/ppermute | solution.py:305
  122.6 11.1 %collective-permute-start.29 = (bf16[64,1152]{1,0:T(8,128)(2,1)S(1)}, bf16[64,1152]{1,0:T(8,128)(2,1)S(1)}, u32[]{:S(2)}, u32[]{:S(2)}) collective-permute-start(bf16[64,1152]{1,0:T(8,128)(2,1)S(1)} %pair_sum.11.own), channel_id=1, source_target_pairs={{0,2},{1,3},{2,0},{3,1},{4,6},{5,7},{6,4},{7,5},{8,10},{9,11},{10,... | collective-permute-start | bytes 442376 | tf_op jit(solution)/shard_map/ppermute | solution.py:305
  128.3 7.3 %collective-permute-start.26 = (bf16[64,1152]{1,0:T(8,128)(2,1)S(1)}, bf16[64,1152]{1,0:T(8,128)(2,1)S(1)}, u32[]{:S(2)}, u32[]{:S(2)}) collective-permute-start(bf16[64,1152]{1,0:T(8,128)(2,1)S(1)} %pair_sum.10.own), channel_id=1, source_target_pairs={{0,2},{1,3},{2,0},{3,1},{4,6},{5,7},{6,4},{7,5},{8,10},{9,11},{10,... | collective-permute-start | bytes 442376 | tf_op jit(solution)/shard_map/ppermute | solution.py:305
  128.4 22.6 %collective-permute-start.24 = (f32[64,2048]{1,0:T(8,128)S(1)}, f32[64,2048]{1,0:T(8,128)S(1)}, u32[]{:S(2)}, u32[]{:S(2)}) collective-permute-start(f32[64,2048]{1,0:T(8,128)S(1)} %get-tuple-element.89.refs_1_), channel_id=1, source_target_pairs={{0,4},{4,0},{8,12},{12,8},{1,5},{5,1},{9,13},{13,9},{2,6},{6,2},{1... | collective-permute-start | bytes 1572872 | tf_op jit(solution)/shard_map/ppermute | solution.py:299
  133.6 17.4 %collective-permute-start.23 = (f32[64,2048]{1,0:T(8,128)S(1)}, f32[64,2048]{1,0:T(8,128)S(1)}, u32[]{:S(2)}, u32[]{:S(2)}) collective-permute-start(f32[64,2048]{1,0:T(8,128)S(1)} %get-tuple-element.71.refs_0_), channel_id=1, source_target_pairs={{0,4},{4,0},{8,12},{12,8},{1,5},{5,1},{9,13},{13,9},{2,6},{6,2},{1... | collective-permute-start | bytes 1572872 | tf_op jit(solution)/shard_map/ppermute | solution.py:299
  133.7 8.3 %collective-permute-start.30 = (f32[64,1024]{1,0:T(8,128)S(1)}, f32[64,1024]{1,0:T(8,128)S(1)}, u32[]{:S(2)}, u32[]{:S(2)}) collective-permute-start(f32[64,1024]{1,0:T(8,128)S(1)} %dual_update.11.own), channel_id=1, source_target_pairs={{0,1},{1,0},{2,3},{3,2},{4,5},{5,4},{6,7},{7,6},{8,9},{9,8},{10,11... | collective-permute-start | bytes 786440 | tf_op jit(solution)/shard_map/ppermute | solution.py:305
  135.7 11.9 %collective-permute-start.27 = (f32[64,1024]{1,0:T(8,128)S(1)}, f32[64,1024]{1,0:T(8,128)S(1)}, u32[]{:S(2)}, u32[]{:S(2)}) collective-permute-start(f32[64,1024]{1,0:T(8,128)S(1)} %dual_update.10.own), channel_id=1, source_target_pairs={{0,1},{1,0},{2,3},{3,2},{4,5},{5,4},{6,7},{7,6},{8,9},{9,8},{10,11... | collective-permute-start | bytes 786440 | tf_op jit(solution)/shard_map/ppermute | solution.py:305
  142.6 10.9 %collective-permute-start.32 = (f32[64,1024]{1,0:T(8,128)S(1)}, f32[64,1024]{1,0:T(8,128)S(1)}, u32[]{:S(2)}, u32[]{:S(2)}) collective-permute-start(f32[64,1024]{1,0:T(8,128)S(1)} %get-tuple-element.101), channel_id=1, source_target_pairs={{0,4},{4,0},{8,12},{12,8},{1,5},{5,1},{9,13},{13,9},{2,6},{6,2},{1... | collective-permute-start | bytes 786440 | tf_op jit(solution)/shard_map/ppermute | solution.py:299
  (34 other events, 153.5 us)

commit v3 on v2

v3 whole, which is shorter than its diff:
```python
import functools

import jax
import jax.numpy as jnp
from jax import lax
from jax.experimental import pallas as pl
from jax.experimental.pallas import tpu as pltpu
from jax.sharding import PartitionSpec as P

ITERS = 3
STEP_SCALE = 0.5
BATCHES = 2
TAIL = 128

bf16 = jnp.bfloat16
f32 = jnp.float32

SMEM = pl.BlockSpec(memory_space=pltpu.SMEM)
VMEM = pl.BlockSpec(memory_space=pltpu.VMEM)
ANY = pl.BlockSpec(memory_space=pl.ANY)
HBM = pl.BlockSpec(memory_space=pltpu.HBM)


def split_sum(total):
    first = total.astype(bf16).astype(f32)
    rest = total - first
    second = rest.astype(bf16).astype(f32)
    third = rest - second
    lane = lax.broadcasted_iota(jnp.int32, (total.shape[0], TAIL), 1)
    block = jnp.where(lane == 0, first, jnp.where(lane == 1, second, jnp.where(lane == 2, third, 0.0)))
    return block.astype(bf16)


def join_sum(block):
    return jnp.sum(block.astype(f32), axis=1, keepdims=True)


def tree_sum(terms):
    terms = list(terms)
    while len(terms) > 1:
        terms = [terms[k] + terms[k + 1] for k in range(0, len(terms), 2)]
    return terms[0]


def set_state(weight, total):
    lane = lax.broadcasted_iota(jnp.int32, (weight.shape[0], TAIL), 1)
    return jnp.where(lane == 0, weight, jnp.where(lane == 1, total, 0.0))


class Blocks:
    def __init__(self, order, slots, cols):
        self.order, self.slots, self.cols = order, slots, cols
        self.n = order[order.shape[0] - 1]

    def ready(self, spot):
        pass

    def run(self, body):
        def several(first, width):
            spots = [self.order[first + q] for q in range(width)]
            for spot in spots:
                self.ready(spot)
            for spot in spots:
                body(spot // self.cols, spot % self.cols, self.slots[spot])

        def four(u, carry):
            several(u * 4, 4)
            return carry

        lax.fori_loop(0, self.n // 4, four, 0)
        pl.when(self.n % 4 >= 2)(lambda: several(self.n // 4 * 4, 2))
        pl.when(self.n % 2 == 1)(lambda: several(self.n - 1, 1))

    def back(self, vector, acc):
        size_r, size_c = self.slots.shape[1:]
        acc[...] = jnp.zeros_like(acc)

        def body(i, j, block):
            rows = vector[:, pl.ds(pl.multiple_of(i * size_r, size_r), size_r)]
            acc[:, pl.ds(pl.multiple_of(j * size_c, size_c), size_c)] += jnp.dot(
                rows, block, preferred_element_type=f32
            )

        self.run(body)

    def forward(self, vector, acc):
        size_c, size_r = self.slots.shape[1:]
        acc[...] = jnp.zeros_like(acc)

        def body(i, j, block):
            cols = vector[:, pl.ds(pl.multiple_of(j * size_c, size_c), size_c)]
            acc[:, pl.ds(pl.multiple_of(i * size_r, size_r), size_r)] += jnp.dot(
                cols, block, preferred_element_type=f32
            )

        self.run(body)


class Incoming(Blocks):
    def __init__(self, tile_map, sources, slots, sems, order):
        rows, cols = tile_map.shape
        size_r, size_c = slots.shape[1:]
        each = rows // len(sources)
        n = jnp.int32(0)
        for i in range(rows):
            for j in range(cols):
                spot = i * cols + j
                nonzero = tile_map[i, j] != 0

                @pl.when(nonzero)
                def _():
                    pltpu.make_async_copy(
                        sources[i // each].at[pl.ds(i % each * size_r, size_r), pl.ds(j * size_c, size_c)],
                        slots.at[spot],
                        sems.at[spot],
                    ).start()
                    order[n] = spot

                n = n + nonzero.astype(jnp.int32)
        order[order.shape[0] - 1] = n
        self.sems = sems
        super().__init__(order, slots, cols)
        self.n = n

    def ready(self, spot):
        pltpu.make_async_copy(self.slots.at[spot], self.slots.at[spot], self.sems.at[spot]).wait()


def first_kernel(tile_map, place, blocks, dual, mine, other, slots, sems, order, vector, acc):
    incoming = Incoming(tile_map, [blocks], slots, sems, order)
    vector[...] = dual[...].T.astype(bf16)
    incoming.back(vector, acc)
    size = mine.shape[0]
    mine[...] = acc[pl.ds(pl.multiple_of(place[1] * size, size), size)]
    other[...] = acc[pl.ds(pl.multiple_of((1 - place[1]) * size, size), size)]


def load_kernel(tile_map, own, partner, *refs):
    slots, turned, order, sems = refs[-4:]
    incoming = Incoming(tile_map, [own, partner], slots, sems, order)

    def one(q, carry):
        spot = order[q]
        incoming.ready(spot)
        turned[spot] = slots[spot].T
        return carry

    lax.fori_loop(0, incoming.n, one, 0)


def first_pack_kernel(batch, mine, other, after, msg):
    size = msg.shape[0]
    here = pl.ds(batch * size, size)
    msg[...] = (mine[here] + other[here]).astype(bf16)


def back_kernel(grid_cols, order, place, own_half, got_half, slots, after, msg, vector, acc):
    half = vector.shape[1] // 2
    side = place[0] % 2
    vector[:, pl.ds(pl.multiple_of(side * half, half), half)] = own_half[:, :half]
    vector[:, pl.ds(pl.multiple_of((1 - side) * half, half), half)] = got_half[:, :half]
    Blocks(order, slots, grid_cols).back(vector, acc)
    width = acc.shape[1]
    msg[:, :width] = acc[...].astype(bf16)
    msg[:, width:] = split_sum(join_sum(own_half[:, half:]) + join_sum(got_half[:, half:]))


def forward_kernel(grid_cols, near, first, last, total_rows, total_cols, order, place, *refs):
    msgs = refs[:near]
    primal, vectors, state, turned, after_ref = refs[near : near + 5]
    primal_next, kept, sent, state_out, vector, acc = refs[near + 5 :]
    width = primal.shape[1]
    weight = state[:, 0:1]
    if not first:
        sum_y = tree_sum([join_sum(ref[:, width:]) for ref in msgs])
        move_y = jnp.sqrt(sum_y / total_rows + 1e-06)
        move_x = jnp.sqrt(state[:, 1:2] / total_cols + 1e-06)
        weight = jnp.sqrt(weight * move_y / move_x)
    step = STEP_SCALE / weight
    image_t = tree_sum([ref[:, :width].astype(f32) for ref in msgs])
    before = primal[...]
    after = before - step * (vectors[0:1] - image_t)
    after = jnp.minimum(jnp.maximum(after, vectors[1:2]), vectors[2:3])
    primal_next[...] = after
    vector[...] = (2.0 * after - before).astype(bf16)
    sum_x = jnp.zeros_like(weight) if last else jnp.sum((after - before) ** 2, axis=1, keepdims=True)
    state_out[...] = set_state(weight, sum_x)
    if not last:
        sent[:, sent.shape[1] - TAIL :] = split_sum(sum_x)
    Blocks(order, turned, grid_cols).forward(vector, acc)
    half = acc.shape[1] // 2
    side = place[0] % 2
    kept[...] = acc[:, pl.ds(pl.multiple_of(side * half, half), half)]
    sent[:, :half] = acc[:, pl.ds(pl.multiple_of((1 - side) * half, half), half)].astype(bf16)


def pair_kernel(kept, state, got, after, msg):
    half = kept.shape[1]
    msg[:, :half] = (kept[...] + got[:, :half].astype(f32)).astype(bf16)
    if msg.shape[1] > half:
        msg[:, half:] = split_sum(state[:, 1:2] + join_sum(got[:, half:]))


def cross_kernel(half, own, got, msg):
    msg[:, :half] = (own[:, :half].astype(f32) + got[:, :half].astype(f32)).astype(bf16)
    if msg.shape[1] > half:
        msg[:, half:] = split_sum(join_sum(own[:, half:]) + join_sum(got[:, half:]))


def dual_kernel(last, own, got, state, dual, right, floor, after_ref, dual_next, *outs):
    half = dual.shape[1]
    image = own[:, :half].astype(f32) + got[:, :half].astype(f32)
    before = dual[...]
    weight = state[:, 0:1]
    after = before + STEP_SCALE * weight * (right[...] - image)
    after = jnp.maximum(after, floor[0:1])
    dual_next[...] = after
    if not last:
        msg, state_out = outs
        msg[:, :half] = after.astype(bf16)
        msg[:, half:] = split_sum(jnp.sum((after - before) ** 2, axis=1, keepdims=True))
        state_out[...] = set_state(weight, join_sum(own[:, half:]) + join_sum(got[:, half:]))


def turn_kernel(place, value, after, *outs):
    size = outs[0].shape[0]
    width = size * len(outs)
    turned = value[:, pl.ds(pl.multiple_of(place[1] * width, width), width)].T
    for b, out in enumerate(outs):
        out[...] = turned[b * size : (b + 1) * size]


def halves_kernel(place, dual, right, after, out):
    rows, width = dual.shape[0], out.shape[1]
    there = pl.ds(pl.multiple_of((1 - place[1]) * width, width), width)
    out[:rows] = dual[:, there]
    out[rows:] = right[:, there]


def rows_kernel(place, dual, right, got, after, *outs):
    size = outs[0].shape[0]
    width = size * BATCHES
    rows = dual.shape[0]
    here = pl.ds(pl.multiple_of(place[1] * width, width), width)

    def put(values, outs):
        turned = values.T
        for b, out in enumerate(outs):
            out[...] = turned[b * size : (b + 1) * size]

    @pl.when(place[0] % 2 == 0)
    def _():
        put(dual[:, here], outs[:BATCHES])
        put(right[:, here], outs[BATCHES:])

    @pl.when(place[0] % 2 == 1)
    def _():
        put(got[:rows], outs[:BATCHES])
        put(got[rows:], outs[BATCHES:])


def put_half(out, core, parts):
    width = out.shape[1] // 2
    out[:, pl.ds(pl.multiple_of(core * width, width), width)] = jnp.concatenate([r[...] for r in parts], axis=0).T


def primal_out_kernel(place, *refs):
    mine, theirs, out = refs[:BATCHES], refs[BATCHES : 2 * BATCHES], refs[-1]
    put_half(out, place[1], mine)
    put_half(out, 1 - place[1], theirs)


def dual_out_kernel(place, *refs):
    own, got, partner = refs[:BATCHES], refs[BATCHES : 2 * BATCHES], refs[2 * BATCHES : 3 * BATCHES]
    out = refs[-1]

    @pl.when(place[0] % 2 == 0)
    def _():
        put_half(out, place[1], own)
        put_half(out, 1 - place[1], got)

    @pl.when(place[0] % 2 == 1)
    def _():
        put_half(out, place[1], got)
        put_half(out, 1 - place[1], partner)


def call(kernel, out_shape, in_specs, scratch=(), name=None, vmem=6, out_specs=None):
    return pl.pallas_call(
        kernel,
        out_shape=out_shape,
        in_specs=in_specs,
        out_specs=out_specs or jax.tree.map(lambda _: VMEM, out_shape),
        scratch_shapes=list(scratch),
        compiler_params=pltpu.CompilerParams(vmem_limit_bytes=vmem << 20),
        cost_estimate=pl.CostEstimate(flops=0, bytes_accessed=0, transcendentals=0),
        name=name,
    )


def shape(rows, cols, kind=f32):
    return jax.ShapeDtypeStruct((rows, cols), kind)


def local(
    blocks,
    tile_map,
    lower_bound,
    upper_bound,
    bound_code,
    row_kind,
    cost_vector,
    right_side,
    primal_start,
    dual_start,
    primal_weight,
):
    rows, cols = blocks.shape
    size_r = rows // tile_map.shape[0]
    size_c = cols // tile_map.shape[1]
    profiles = dual_start.shape[1]
    width = profiles // 2
    size = width // BATCHES
    count = lax.axis_size("col")
    near = lax.axis_size("row") // 2
    total_rows = rows * near * 2
    total_cols = cols * count
    z = lax.axis_index("col")
    core = lax.axis_index("row") % 2
    place = jnp.stack([z, core]).astype(jnp.int32)

    def to_core(value):
        return lax.ppermute(value, "row", [(i, i ^ 1) for i in range(2 * near)])

    def to_x(value, k):
        return lax.ppermute(value, "row", [(i, i ^ (2 * k)) for i in range(2 * near)])

    def to_z(value, k):
        return lax.ppermute(value, "col", [(i, i ^ k) for i in range(count)])

    n_own = tile_map.size
    n_chip = 2 * n_own
    grid_cols = tile_map.shape[1]

    blocks = pltpu.with_memory_space_constraint(blocks, pltpu.HBM)
    partner = to_core(blocks)
    chip_map = jnp.concatenate([tile_map, to_core(tile_map)], axis=0)
    mine, other = call(
        first_kernel,
        (shape(width, cols),) * 2,
        [SMEM, SMEM, HBM, VMEM],
        [
            pltpu.VMEM((n_own, size_r, size_c), bf16),
            pltpu.SemaphoreType.DMA((n_own,)),
            pltpu.SMEM((n_own + 1,), jnp.int32),
            pltpu.VMEM((profiles, rows), bf16),
            pltpu.VMEM((profiles, cols), f32),
        ],
        name="first_product",
        vmem=16,
    )(tile_map, place, blocks, dual_start)
    other = to_core(other)

    low_on = (bound_code == 1) | (bound_code == 3)
    high_on = (bound_code == 2) | (bound_code == 3)
    vectors = jnp.stack(
        [cost_vector, jnp.where(low_on, lower_bound, -jnp.inf), jnp.where(high_on, upper_bound, jnp.inf)]
    )
    weight = lax.dynamic_slice_in_dim(primal_weight, core * width, width, 0)
    state = [jnp.broadcast_to(weight[b * size : (b + 1) * size, None], (size, TAIL)) for b in range(BATCHES)]
    kind = jnp.where(z % 2 == 0, row_kind, to_core(row_kind))
    floor = jnp.where(kind == 1, 0.0, -jnp.inf).astype(f32)[None, :]

    def half_msg(tail):
        return shape(size, rows + (TAIL if tail else 0), bf16)

    def back(b, iteration, after):
        if iteration == 0:
            messages[b] = call(
                functools.partial(first_pack_kernel, b),
                shape(size, cols, bf16),
                [VMEM] * 2 + [ANY],
                name="first_pack",
            )(mine, other, after)
        else:
            messages[b] = call(
                functools.partial(back_kernel, grid_cols),
                shape(size, cols + TAIL, bf16),
                [SMEM, SMEM, VMEM, VMEM, VMEM, ANY],
                [pltpu.VMEM((size, 2 * rows), bf16), pltpu.VMEM((size, cols), f32)],
                name="back_product",
            )(order, place, *halves[b], slots, after)
        return messages[b]

    def forward(b, iteration, after):
        first, last = iteration == 0, iteration + 1 == ITERS
        msgs = [messages[b]] + [to_x(messages[b], k) for k in range(1, near)]
        outs = call(
            functools.partial(forward_kernel, grid_cols, near, first, last, total_rows, total_cols),
            (shape(size, cols), shape(size, rows), half_msg(not last), shape(size, TAIL)),
            [SMEM, SMEM] + [VMEM] * (near + 4) + [ANY],
            [pltpu.VMEM((size, cols), bf16), pltpu.VMEM((size, 2 * rows), f32)],
            name="forward_product",
        )(order, place, *msgs, primal[b], vectors, state[b], turned, after)
        primal[b], kept[b], sent[b], state[b] = outs
        return state[b]

    def pair(b, iteration, after):
        out = half_msg(iteration + 1 < ITERS)
        crossing[b] = call(pair_kernel, out, [VMEM] * 3 + [ANY], name="pair_sum")(
            kept[b], state[b], to_z(sent[b], 1), after
        )
        mask = 2
        while mask * 2 < count:
            crossing[b] = call(functools.partial(cross_kernel, rows), out, [VMEM] * 2, name="cross_sum")(
                crossing[b], to_z(crossing[b], mask)
            )
            mask *= 2
        return crossing[b]

    def update(b, iteration, after):
        last = iteration + 1 == ITERS
        got = to_z(crossing[b], count // 2)
        out_shape = (shape(size, rows),)
        if not last:
            out_shape += (half_msg(True), shape(size, TAIL))
        outs = call(functools.partial(dual_kernel, last), out_shape, [VMEM] * 6 + [ANY], name="dual_update")(
            crossing[b], got, state[b], dual[b], right[b], floor, after
        )
        dual[b] = outs[0]
        if last:
            return dual[b]
        state[b] = outs[2]
        halves[b] = (outs[1], to_z(outs[1], 1))
        return state[b]

    stages = [(stage, k) for k in range(ITERS) for stage in (back, forward, pair, update)]
    lag = 4 // BATCHES
    messages, halves, kept, sent, crossing = ([None] * BATCHES for _ in range(5))
    token = state[0]
    primal_final = None
    for slot in range(len(stages) + lag * (BATCHES - 1)):
        for b in range(BATCHES):
            at = slot - lag * b
            if not 0 <= at < len(stages):
                continue
            stage, iteration = stages[at]
            token = stage(b, iteration, token)
            if (b, at) == (0, 0):
                primal = list(
                    call(turn_kernel, (shape(size, cols),) * BATCHES, [SMEM, VMEM, ANY], name="turn_primal")(
                        place, primal_start, token
                    )
                )
                spare = call(halves_kernel, shape(2 * rows, width), [SMEM, VMEM, VMEM, ANY], name="partner_half")(
                    place, dual_start, right_side, token
                )
                spare = to_core(spare)
                slots, turned, order = call(
                    load_kernel,
                    (
                        pltpu.VMEM((n_chip, size_r, size_c), bf16),
                        pltpu.VMEM((n_chip, size_c, size_r), bf16),
                        jax.ShapeDtypeStruct((n_chip + 1,), jnp.int32),
                    ),
                    [SMEM, HBM, HBM] + [ANY] * (3 + BATCHES),
                    [pltpu.SemaphoreType.DMA((n_chip,))],
                    name="load_blocks",
                    vmem=4,
                    out_specs=(VMEM, VMEM, SMEM),
                )(chip_map, blocks, partner, token, floor, vectors, *state)
            if (b, at) == (0, 1):
                held = call(
                    rows_kernel,
                    (shape(size, rows),) * (2 * BATCHES),
                    [SMEM] + [VMEM] * 3 + [ANY],
                    name="turn_rows",
                )(place, dual_start, right_side, spare, token)
                dual, right = list(held[:BATCHES]), held[BATCHES:]
            if (b, at) == (BATCHES - 1, len(stages) - 2):
                token = primal_final = call(
                    primal_out_kernel,
                    shape(cols, profiles),
                    [SMEM] + [VMEM] * (2 * BATCHES) + [ANY],
                    name="primal_out",
                )(place, *primal, *[to_core(p) for p in primal], token)

    def index(row, col):
        return row * count + col

    everyone = [(row, col) for row in range(2 * near) for col in range(count)]
    to_holder = [(index(r, c), index(r ^ (c % 2), c ^ 1)) for r, c in everyone]
    to_odd = [(index(r, c), index(r ^ 1, c)) for r, c in everyone if c % 2]
    got = [lax.ppermute(d, ("row", "col"), to_holder) for d in dual]
    partner_rows = [lax.ppermute(d, ("row", "col"), to_odd) for d in dual]
    dual_final = call(
        dual_out_kernel, shape(rows, profiles), [SMEM] + [VMEM] * (3 * BATCHES), name="dual_out"
    )(place, *dual, *got, *partner_rows)
    return primal_final, dual_final


def solution(mesh):
    return jax.shard_map(
        local,
        mesh=mesh,
        in_specs=(
            P("row", "col"),
            P("row", "col"),
            P("col"),
            P("col"),
            P("col"),
            P("row"),
            P("col"),
            P("row", "groups"),
            P("col", "groups"),
            P("row", "groups"),
            P("groups"),
        ),
        out_specs=(P("col", "groups"), P("row", "groups")),
        check_vma=False,
    )
```

time: 157 us -> 134 us (0.85)
  Pallas kernels: 56.4 us -> 32.9 us
  starting transfers between devices: 23.9 us -> 39.4 us
  local copies, waits for them, and re-layouts: 15.7 us -> 4.37 us
  waiting for transfers between devices: 56.3 us -> 52.8 us
    pallas_call x28 -> x29, Pallas kernels: 53 us -> 29.6 us  [the longest x6 11.2 us: forward(): call(functools.partial(forward_kernel, grid_cols, near, first, last, tota...]
    unnamed x50 -> x24, local copies, waits for them, and re-layouts: 15.3 us -> 4.08 us
    ppermute x18 -> x16, waiting for transfers between devices: 42 us -> 33.5 us  [to_z(): return lax.ppermute(value, 'col', [(i, i ^ k) for i in range(count)])]
    ppermute x0 -> x4, waiting for transfers between devices: none -> 7.93 us  [the longest x2 7.93 us: local(): got = [lax.ppermute(d, ('row', 'col'), to_holder) for d in dual]]
    ppermute x6, starting transfers between devices: 1.92 us -> 9.66 us  [to_x(): return lax.ppermute(value, 'row', [(i, i ^ 2 * k) for i in range(2 * near)])]
    ppermute x6, waiting for transfers between devices: 14.3 us -> 9.57 us  [to_x(): return lax.ppermute(value, 'row', [(i, i ^ 2 * k) for i in range(2 * near)])]
    ppermute x18 -> x16, starting transfers between devices: 4.92 us -> 7.81 us  [to_z(): return lax.ppermute(value, 'col', [(i, i ^ k) for i in range(count)])]
    ppermute x0 -> x4, starting transfers between devices: none -> 2.69 us  [the longest x2 1.34 us: local(): got = [lax.ppermute(d, ('row', 'col'), to_holder) for d in dual]]
  transfers between devices with their start and end apart: 33 -> 33, of which waited for: 14 -> 21; matrix products, arithmetic and copies ran while one was open for 1% -> 1% of each run, Pallas kernels for 35% -> 22%
where the time goes in v3:
time: 134 us; the launch traced here: 131 us
  waiting for transfers between devices  52.8 us (39%)
  starting transfers between devices  39.4 us (29%)
  Pallas kernels  32.9 us (25%)
  local copies, waits for them, and re-layouts  4.37 us (3%)
    ppermute x16, waiting for transfers between devices, to_z(): return lax.ppermute(value, 'col', [(i, i ^ k) for i in range(count)])  33.5 us
    ppermute x7, starting transfers between devices, to_core(): return lax.ppermute(value, 'row', [(i, i ^ 1) for i in range(2 * near)])  19.2 us
    pallas_call x6, Pallas kernels, forward(): call(functools.partial(forward_kernel, grid_cols, near, first, last, tota...  11.2 us
    ppermute x6, starting transfers between devices, to_x(): return lax.ppermute(value, 'row', [(i, i ^ 2 * k) for i in range(2 * near)])  9.66 us
    ppermute x6, waiting for transfers between devices, to_x(): return lax.ppermute(value, 'row', [(i, i ^ 2 * k) for i in range(2 * near)])  9.57 us
    ppermute x2, waiting for transfers between devices, local(): got = [lax.ppermute(d, ('row', 'col'), to_holder) for d in dual]  7.93 us
    ppermute x16, starting transfers between devices, to_z(): return lax.ppermute(value, 'col', [(i, i ^ k) for i in range(count)])  7.81 us
    pallas_call x4, Pallas kernels, back(): call(functools.partial(back_kernel, grid_cols), shape(size, cols + TAIL,...  6.01 us
  transfers between devices with their start and end apart: 33, of which 21 were waited for; matrix products, arithmetic and copies ran while one was open for 1% of the time, Pallas kernels for 22%

profile of v3, /device:TPU:5, one launch (start us, length us, event | category | flops | bytes accessed | tf_op | source)
XLA Modules:
  0.0 131.4 jit_solution(14737824809654821505)
XLA Ops:
  2.7 3.5 %first_product.1 = (f32[128,2048]{1,0:T(8,128)S(1)}, f32[128,2048]{1,0:T(8,128)}) custom-call(s32[2,4]{1,0:T(2,128)} %tile_map.1, s32[2]{0:T(128)S(1)} %pad_add_fusion.1.place, bf16[1024,2048]{1,0:T(8,128)(2,1)} %own.1, f32[1024,256]{1,0:T(8,128)S(1)} %copy-done), custom_call_target="tpu_custom_call" | custom-call | tf_op jit(solution)/shard_map/first_product/pallas_call | solution.py:348
  8.2 1.8 %collective-permute-done.2.other = f32[128,2048]{1,0:T(8,128)S(1)} collective-permute-done((f32[128,2048]{1,0:T(8,128)}, f32[128,2048]{1,0:T(8,128)S(1)}, u32[]{:S(2)}, u32[]{:S(2)}) %collective-permute-start.2) | collective-permute-done | bytes 1048608 | tf_op jit(solution)/shard_map/ppermute | solution.py:333
  15.3 3.5 %load_blocks.1 = (bf16[16,512,512]{2,1,0:T(8,128)(2,1)S(1)}, bf16[16,512,512]{2,1,0:T(8,128)(2,1)S(1)}, s32[17]{0:T(128)S(1)}) custom-call(s32[4,4]{1,0:T(4,128)S(1)} %pad_add_fusion.tile_map, bf16[1024,2048]{1,0:T(8,128)(2,1)} %own.1, bf16[1024,2048]{1,0:T(8,128)(2,1)} %collective-permute-done.1.partner, ...), custom_call_target="tpu_custom_call" | custom-call | tf_op jit(solution)/shard_map/load_blocks/pallas_call | solution.py:459
  23.1 3.5 %collective-permute-done.5.got = bf16[64,1152]{1,0:T(8,128)(2,1)S(1)} collective-permute-done((bf16[64,1152]{1,0:T(8,128)(2,1)S(1)}, bf16[64,1152]{1,0:T(8,128)(2,1)S(1)}, u32[]{:S(2)}, u32[]{:S(2)}) %collective-permute-start.5) | collective-permute-done | bytes 147488 | tf_op jit(solution)/shard_map/ppermute | solution.py:339
  28.3 2.2 %collective-permute-start.9 = (bf16[64,2048]{1,0:T(8,128)(2,1)S(1)}, bf16[64,2048]{1,0:T(8,128)(2,1)S(1)}, u32[]{:S(2)}, u32[]{:S(2)}) collective-permute-start(bf16[64,2048]{1,0:T(8,128)(2,1)S(1)} %first_pack.3.after_ref.refs_0_), channel_id=1, source_target_pairs={{0,8},{4,12},{8,0},{12,4},{1,9},{5,13},{9,1},{13,5},{2,10},{6,14},... | collective-permute-start | bytes 786440 | tf_op jit(solution)/shard_map/ppermute | solution.py:336
  31.4 4.6 %collective-permute-done.6.got = bf16[64,1152]{1,0:T(8,128)(2,1)S(1)} collective-permute-done((bf16[64,1152]{1,0:T(8,128)(2,1)S(1)}, bf16[64,1152]{1,0:T(8,128)(2,1)S(1)}, u32[]{:S(2)}, u32[]{:S(2)}) %collective-permute-start.6) | collective-permute-done | bytes 147488 | tf_op jit(solution)/shard_map/ppermute | solution.py:339
  45.1 2.1 %collective-permute-done.10.refs_1_ = bf16[64,2176]{1,0:T(8,128)(2,1)S(1)} collective-permute-done((bf16[64,2176]{1,0:T(8,128)(2,1)S(1)}, bf16[64,2176]{1,0:T(8,128)(2,1)S(1)}, u32[]{:S(2)}, u32[]{:S(2)}) %collective-permute-start.10) | collective-permute-done | bytes 278560 | tf_op jit(solution)/shard_map/ppermute | solution.py:336
  47.2 1.9 %forward_product.8 = (f32[64,2048]{1,0:T(8,128)S(1)}, f32[64,1024]{1,0:T(8,128)S(1)}, bf16[64,1152]{1,0:T(8,128)(2,1)S(1)}, f32[64,128]{1,0:T(8,128)S(1)}) custom-call(s32[17]{0:T(128)S(1)} %get-tuple-element.51.order, s32[2]{0:T(128)S(1)} %pad_add_fusion.1.place, bf16[64,2176]{1,0:T(8,128)(2,1)S(1)} %back_product.4.after.refs_0_, ...), custom_call_target="tpu_custom_call" | custom-call | tf_op jit(solution)/shard_map/forward_product/pallas_call | solution.py:398
  51.0 3.3 %collective-permute-done.12.got = bf16[64,1152]{1,0:T(8,128)(2,1)S(1)} collective-permute-done((bf16[64,1152]{1,0:T(8,128)(2,1)S(1)}, bf16[64,1152]{1,0:T(8,128)(2,1)S(1)}, u32[]{:S(2)}, u32[]{:S(2)}) %collective-permute-start.12) | collective-permute-done | bytes 147488 | tf_op jit(solution)/shard_map/ppermute | solution.py:339
  57.4 3.2 %collective-permute-start.17 = (bf16[64,2176]{1,0:T(8,128)(2,1)S(1)}, bf16[64,2176]{1,0:T(8,128)(2,1)S(1)}, u32[]{:S(2)}, u32[]{:S(2)}) collective-permute-start(bf16[64,2176]{1,0:T(8,128)(2,1)S(1)} %back_product.5.after_ref.refs_0_), channel_id=1, source_target_pairs={{0,8},{4,12},{8,0},{12,4},{1,9},{5,13},{9,1},{13,5},{2,10},{6,14},... | collective-permute-start | bytes 835592 | tf_op jit(solution)/shard_map/ppermute | solution.py:336
  61.2 3.6 %collective-permute-done.17.refs_1_ = bf16[64,2176]{1,0:T(8,128)(2,1)S(1)} collective-permute-done((bf16[64,2176]{1,0:T(8,128)(2,1)S(1)}, bf16[64,2176]{1,0:T(8,128)(2,1)S(1)}, u32[]{:S(2)}, u32[]{:S(2)}) %collective-permute-start.17) | collective-permute-done | bytes 278560 | tf_op jit(solution)/shard_map/ppermute | solution.py:336
  64.8 1.9 %forward_product.9 = (f32[64,2048]{1,0:T(8,128)S(1)}, f32[64,1024]{1,0:T(8,128)S(1)}, bf16[64,1152]{1,0:T(8,128)(2,1)S(1)}, f32[64,128]{1,0:T(8,128)S(1)}) custom-call(s32[17]{0:T(128)S(1)} %get-tuple-element.51.order, s32[2]{0:T(128)S(1)} %pad_add_fusion.1.place, bf16[64,2176]{1,0:T(8,128)(2,1)S(1)} %back_product.5.after_ref.refs_0_, ...), custom_call_target="tpu_custom_call" | custom-call | tf_op jit(solution)/shard_map/forward_product/pallas_call | solution.py:398
  69.2 2.0 %collective-permute-done.19.got = bf16[64,1152]{1,0:T(8,128)(2,1)S(1)} collective-permute-done((bf16[64,1152]{1,0:T(8,128)(2,1)S(1)}, bf16[64,1152]{1,0:T(8,128)(2,1)S(1)}, u32[]{:S(2)}, u32[]{:S(2)}) %collective-permute-start.19) | collective-permute-done | bytes 147488 | tf_op jit(solution)/shard_map/ppermute | solution.py:339
  71.5 2.4 %collective-permute-done.18.refs_1_ = bf16[64,2176]{1,0:T(8,128)(2,1)S(1)} collective-permute-done((bf16[64,2176]{1,0:T(8,128)(2,1)S(1)}, bf16[64,2176]{1,0:T(8,128)(2,1)S(1)}, u32[]{:S(2)}, u32[]{:S(2)}) %collective-permute-start.18) | collective-permute-done | bytes 278560 | tf_op jit(solution)/shard_map/ppermute | solution.py:336
  73.9 2.0 %forward_product.10 = (f32[64,2048]{1,0:T(8,128)S(1)}, f32[64,1024]{1,0:T(8,128)S(1)}, bf16[64,1024]{1,0:T(8,128)(2,1)S(1)}, f32[64,128]{1,0:T(8,128)S(1)}) custom-call(s32[17]{0:T(128)S(1)} %get-tuple-element.51.order, s32[2]{0:T(128)S(1)} %pad_add_fusion.1.place, bf16[64,2176]{1,0:T(8,128)(2,1)S(1)} %back_product.6.after.refs_0_, ...), custom_call_target="tpu_custom_call" | custom-call | tf_op jit(solution)/shard_map/forward_product/pallas_call | solution.py:398
  79.3 4.2 %collective-permute-done.22.got = bf16[64,1024]{1,0:T(8,128)(2,1)S(1)} collective-permute-done((bf16[64,1024]{1,0:T(8,128)(2,1)S(1)}, bf16[64,1024]{1,0:T(8,128)(2,1)S(1)}, u32[]{:S(2)}, u32[]{:S(2)}) %collective-permute-start.22) | collective-permute-done | bytes 131104 | tf_op jit(solution)/shard_map/ppermute | solution.py:339
  86.7 11.2 %collective-permute-start.25 = (f32[64,2048]{1,0:T(8,128)S(1)}, f32[64,2048]{1,0:T(8,128)S(1)}, u32[]{:S(2)}, u32[]{:S(2)}) collective-permute-start(f32[64,2048]{1,0:T(8,128)S(1)} %get-tuple-element.82.refs_0_), channel_id=1, source_target_pairs={{0,4},{4,0},{8,12},{12,8},{1,5},{5,1},{9,13},{13,9},{2,6},{6,2},{1... | collective-permute-start | bytes 1572872 | tf_op jit(solution)/shard_map/ppermute | solution.py:333
  98.0 1.8 %forward_product.11 = (f32[64,2048]{1,0:T(8,128)S(1)}, f32[64,1024]{1,0:T(8,128)S(1)}, bf16[64,1024]{1,0:T(8,128)(2,1)S(1)}, f32[64,128]{1,0:T(8,128)S(1)}) custom-call(s32[17]{0:T(128)S(1)} %get-tuple-element.51.order, s32[2]{0:T(128)S(1)} %pad_add_fusion.1.place, bf16[64,2176]{1,0:T(8,128)(2,1)S(1)} %back_product.7.after_ref.refs_0_, ...), custom_call_target="tpu_custom_call" | custom-call | tf_op jit(solution)/shard_map/forward_product/pallas_call | solution.py:398
  99.8 5.1 %collective-permute-start.26 = (f32[64,2048]{1,0:T(8,128)S(1)}, f32[64,2048]{1,0:T(8,128)S(1)}, u32[]{:S(2)}, u32[]{:S(2)}) collective-permute-start(f32[64,2048]{1,0:T(8,128)S(1)} %get-tuple-element.91.refs_1_), channel_id=1, source_target_pairs={{0,4},{4,0},{8,12},{12,8},{1,5},{5,1},{9,13},{13,9},{2,6},{6,2},{1... | collective-permute-start | bytes 1572872 | tf_op jit(solution)/shard_map/ppermute | solution.py:333
  104.9 5.1 %collective-permute-done.27.got = bf16[64,1024]{1,0:T(8,128)(2,1)S(1)} collective-permute-done((bf16[64,1024]{1,0:T(8,128)(2,1)S(1)}, bf16[64,1024]{1,0:T(8,128)(2,1)S(1)}, u32[]{:S(2)}, u32[]{:S(2)}) %collective-permute-start.27) | collective-permute-done | bytes 131104 | tf_op jit(solution)/shard_map/ppermute | solution.py:339
  112.6 2.5 %primal_out.1.after_ref = f32[2048,256]{1,0:T(8,128)} custom-call(s32[2]{0:T(128)S(1)} %pad_add_fusion.1.place, f32[64,2048]{1,0:T(8,128)S(1)} %get-tuple-element.82.refs_0_, f32[64,2048]{1,0:T(8,128)S(1)} %get-tuple-element.91.refs_1_, f32[64,2048]{1,0:T(8,128)S(1)} %collective-permute-done.25.refs_2_, f32[64,2048]{1,0:T(8,128)S(1)} %collective-permute-done.26.refs_3_, ...), custom_call_target="tpu_custom_call" | custom-call | tf_op jit(solution)/shard_map/primal_out/pallas_call | solution.py:481
  115.1 4.1 %collective-permute-done.28.got = bf16[64,1024]{1,0:T(8,128)(2,1)S(1)} collective-permute-done((bf16[64,1024]{1,0:T(8,128)(2,1)S(1)}, bf16[64,1024]{1,0:T(8,128)(2,1)S(1)}, u32[]{:S(2)}, u32[]{:S(2)}) %collective-permute-start.28) | collective-permute-done | bytes 131104 | tf_op jit(solution)/shard_map/ppermute | solution.py:339
  122.3 7.3 %collective-permute-done.30.refs_3_ = f32[64,1024]{1,0:T(8,128)S(1)} collective-permute-done((f32[64,1024]{1,0:T(8,128)S(1)}, f32[64,1024]{1,0:T(8,128)S(1)}, u32[]{:S(2)}, u32[]{:S(2)}) %collective-permute-start.30) | collective-permute-done | bytes 262176 | tf_op jit(solution)/shard_map/ppermute | solution.py:494
  129.5 1.9 %dual_out.1 = f32[1024,256]{1,0:T(8,128)} custom-call(s32[2]{0:T(128)S(1)} %pad_add_fusion.1.place, f32[64,1024]{1,0:T(8,128)S(1)} %dual_update.10.refs_6_.refs_0_, f32[64,1024]{1,0:T(8,128)S(1)} %dual_update.11.refs_1_, f32[64,1024]{1,0:T(8,128)S(1)} %collective-permute-done.29.refs_2_, f32[64,1024]{1,0:T(8,128)S(1)} %collective-permute-done.30.refs_3_, ...), custom_call_target="tpu_custom_call" | custom-call | tf_op jit(solution)/shard_map/dual_out/pallas_call | solution.py:496
  (106 shorter events, 45.7 us)
Async XLA Ops:
  0.6 14.6 %collective-permute-start.1 = (bf16[1024,2048]{1,0:T(8,128)(2,1)}, bf16[1024,2048]{1,0:T(8,128)(2,1)}, u32[]{:S(2)}, u32[]{:S(2)}) collective-permute-start(bf16[1024,2048]{1,0:T(8,128)(2,1)} %own.1), channel_id=1, source_target_pairs={{0,4},{4,0},{8,12},{12,8},{1,5},{5,1},{9,13},{13,9},{2,6},{6,2},{1... | collective-permute-start | bytes 12582920 | tf_op jit(solution)/shard_map/ppermute | solution.py:333
  7.5 6.1 %collective-permute-start = (s32[2,4]{1,0:T(2,128)}, s32[2,4]{1,0:T(2,128)S(1)}, u32[]{:S(2)}, u32[]{:S(2)}) collective-permute-start(s32[2,4]{1,0:T(2,128)} %tile_map.1), channel_id=1, source_target_pairs={{0,4},{4,0},{8,12},{12,8},{1,5},{5,1},{9,13},{13,9},{2,6},{6,2},{1... | collective-permute-start | bytes 104 | tf_op jit(solution)/shard_map/ppermute | solution.py:333
  7.6 6.8 %collective-permute-start.3 = (s32[1024]{0:T(1024)S(1)}, s32[1024]{0:T(1024)S(1)}, u32[]{:S(2)}, u32[]{:S(2)}) collective-permute-start(s32[1024]{0:T(1024)S(1)} %copy-done.10), channel_id=1, source_target_pairs={{0,4},{4,0},{8,12},{12,8},{1,5},{5,1},{9,13},{13,9},{2,6},{6,2},{1... | collective-permute-start | bytes 12296 | tf_op jit(solution)/shard_map/ppermute | solution.py:333
  12.0 18.5 %collective-permute-start.7 = (f32[2048,128]{1,0:T(8,128)S(1)}, f32[2048,128]{1,0:T(8,128)S(1)}, u32[]{:S(2)}, u32[]{:S(2)}) collective-permute-start(f32[2048,128]{1,0:T(8,128)S(1)} %partner_half.1), channel_id=1, source_target_pairs={{0,4},{4,0},{8,12},{12,8},{1,5},{5,1},{9,13},{13,9},{2,6},{6,2},{1... | collective-permute-start | bytes 3145736 | tf_op jit(solution)/shard_map/ppermute | solution.py:333
  12.5 7.8 %collective-permute-start.4 = (bf16[64,2048]{1,0:T(8,128)(2,1)S(1)}, bf16[64,2048]{1,0:T(8,128)(2,1)S(1)}, u32[]{:S(2)}, u32[]{:S(2)}) collective-permute-start(bf16[64,2048]{1,0:T(8,128)(2,1)S(1)} %first_pack.2.refs_0_.after.refs_6_), channel_id=1, source_target_pairs={{0,8},{4,12},{8,0},{12,4},{1,9},{5,13},{9,1},{13,5},{2,10},{6,14},... | collective-permute-start | bytes 786440 | tf_op jit(solution)/shard_map/ppermute | solution.py:336
  26.8 9.2 %collective-permute-start.6 = (bf16[64,1152]{1,0:T(8,128)(2,1)S(1)}, bf16[64,1152]{1,0:T(8,128)(2,1)S(1)}, u32[]{:S(2)}, u32[]{:S(2)}) collective-permute-start(bf16[64,1152]{1,0:T(8,128)(2,1)S(1)} %pair_sum.6.after.own), channel_id=1, source_target_pairs={{0,2},{1,3},{2,0},{3,1},{4,6},{5,7},{6,4},{7,5},{8,10},{9,11},{10,... | collective-permute-start | bytes 442376 | tf_op jit(solution)/shard_map/ppermute | solution.py:339
  28.3 8.0 %collective-permute-start.9 = (bf16[64,2048]{1,0:T(8,128)(2,1)S(1)}, bf16[64,2048]{1,0:T(8,128)(2,1)S(1)}, u32[]{:S(2)}, u32[]{:S(2)}) collective-permute-start(bf16[64,2048]{1,0:T(8,128)(2,1)S(1)} %first_pack.3.after_ref.refs_0_), channel_id=1, source_target_pairs={{0,8},{4,12},{8,0},{12,4},{1,9},{5,13},{9,1},{13,5},{2,10},{6,14},... | collective-permute-start | bytes 786440 | tf_op jit(solution)/shard_map/ppermute | solution.py:336
  38.1 5.9 %collective-permute-start.11 = (bf16[64,1152]{1,0:T(8,128)(2,1)S(1)}, bf16[64,1152]{1,0:T(8,128)(2,1)S(1)}, u32[]{:S(2)}, u32[]{:S(2)}) collective-permute-start(bf16[64,1152]{1,0:T(8,128)(2,1)S(1)} %get-tuple-element.66), channel_id=1, source_target_pairs={{0,1},{1,0},{2,3},{3,2},{4,5},{5,4},{6,7},{7,6},{8,9},{9,8},{10,11... | collective-permute-start | bytes 442376 | tf_op jit(solution)/shard_map/ppermute | solution.py:339
  44.2 5.8 %collective-permute-start.13 = (bf16[64,1152]{1,0:T(8,128)(2,1)S(1)}, bf16[64,1152]{1,0:T(8,128)(2,1)S(1)}, u32[]{:S(2)}, u32[]{:S(2)}) collective-permute-start(bf16[64,1152]{1,0:T(8,128)(2,1)S(1)} %pair_sum.7.refs_6_.own), channel_id=1, source_target_pairs={{0,2},{1,3},{2,0},{3,1},{4,6},{5,7},{6,4},{7,5},{8,10},{9,11},{10,... | collective-permute-start | bytes 442376 | tf_op jit(solution)/shard_map/ppermute | solution.py:339
  54.5 6.4 %collective-permute-start.14 = (bf16[64,1152]{1,0:T(8,128)(2,1)S(1)}, bf16[64,1152]{1,0:T(8,128)(2,1)S(1)}, u32[]{:S(2)}, u32[]{:S(2)}) collective-permute-start(bf16[64,1152]{1,0:T(8,128)(2,1)S(1)} %pair_sum.8.after.own), channel_id=1, source_target_pairs={{0,2},{1,3},{2,0},{3,1},{4,6},{5,7},{6,4},{7,5},{8,10},{9,11},{10,... | collective-permute-start | bytes 442376 | tf_op jit(solution)/shard_map/ppermute | solution.py:339
  57.4 7.4 %collective-permute-start.17 = (bf16[64,2176]{1,0:T(8,128)(2,1)S(1)}, bf16[64,2176]{1,0:T(8,128)(2,1)S(1)}, u32[]{:S(2)}, u32[]{:S(2)}) collective-permute-start(bf16[64,2176]{1,0:T(8,128)(2,1)S(1)} %back_product.5.after_ref.refs_0_), channel_id=1, source_target_pairs={{0,8},{4,12},{8,0},{12,4},{1,9},{5,13},{9,1},{13,5},{2,10},{6,14},... | collective-permute-start | bytes 835592 | tf_op jit(solution)/shard_map/ppermute | solution.py:336
  61.2 5.8 %collective-permute-start.16 = (bf16[64,1152]{1,0:T(8,128)(2,1)S(1)}, bf16[64,1152]{1,0:T(8,128)(2,1)S(1)}, u32[]{:S(2)}, u32[]{:S(2)}) collective-permute-start(bf16[64,1152]{1,0:T(8,128)(2,1)S(1)} %get-tuple-element.75.own_half), channel_id=1, source_target_pairs={{0,1},{1,0},{2,3},{3,2},{4,5},{5,4},{6,7},{7,6},{8,9},{9,8},{10,11... | collective-permute-start | bytes 442376 | tf_op jit(solution)/shard_map/ppermute | solution.py:339
  71.5 6.0 %collective-permute-start.20 = (bf16[64,1152]{1,0:T(8,128)(2,1)S(1)}, bf16[64,1152]{1,0:T(8,128)(2,1)S(1)}, u32[]{:S(2)}, u32[]{:S(2)}) collective-permute-start(bf16[64,1152]{1,0:T(8,128)(2,1)S(1)} %pair_sum.9.refs_6_.own), channel_id=1, source_target_pairs={{0,2},{1,3},{2,0},{3,1},{4,6},{5,7},{6,4},{7,5},{8,10},{9,11},{10,... | collective-permute-start | bytes 442376 | tf_op jit(solution)/shard_map/ppermute | solution.py:339
  77.7 5.8 %collective-permute-start.21 = (bf16[64,1152]{1,0:T(8,128)(2,1)S(1)}, bf16[64,1152]{1,0:T(8,128)(2,1)S(1)}, u32[]{:S(2)}, u32[]{:S(2)}) collective-permute-start(bf16[64,1152]{1,0:T(8,128)(2,1)S(1)} %get-tuple-element.85.own_half), channel_id=1, source_target_pairs={{0,1},{1,0},{2,3},{3,2},{4,5},{5,4},{6,7},{7,6},{8,9},{9,8},{10,11... | collective-permute-start | bytes 442376 | tf_op jit(solution)/shard_map/ppermute | solution.py:339
  77.8 5.7 %collective-permute-start.22 = (bf16[64,1024]{1,0:T(8,128)(2,1)S(1)}, bf16[64,1024]{1,0:T(8,128)(2,1)S(1)}, u32[]{:S(2)}, u32[]{:S(2)}) collective-permute-start(bf16[64,1024]{1,0:T(8,128)(2,1)S(1)} %get-tuple-element.87), channel_id=1, source_target_pairs={{0,1},{1,0},{2,3},{3,2},{4,5},{5,4},{6,7},{7,6},{8,9},{9,8},{10,11... | collective-permute-start | bytes 393224 | tf_op jit(solution)/shard_map/ppermute | solution.py:339
  85.1 13.0 %collective-permute-start.23 = (bf16[64,2176]{1,0:T(8,128)(2,1)S(1)}, bf16[64,2176]{1,0:T(8,128)(2,1)S(1)}, u32[]{:S(2)}, u32[]{:S(2)}) collective-permute-start(bf16[64,2176]{1,0:T(8,128)(2,1)S(1)} %back_product.7.after_ref.refs_0_), channel_id=1, source_target_pairs={{0,8},{4,12},{8,0},{12,4},{1,9},{5,13},{9,1},{13,5},{2,10},{6,14},... | collective-permute-start | bytes 835592 | tf_op jit(solution)/shard_map/ppermute | solution.py:336
  86.7 11.2 %collective-permute-start.24 = (bf16[64,1024]{1,0:T(8,128)(2,1)S(1)}, bf16[64,1024]{1,0:T(8,128)(2,1)S(1)}, u32[]{:S(2)}, u32[]{:S(2)}) collective-permute-start(bf16[64,1024]{1,0:T(8,128)(2,1)S(1)} %pair_sum.10.after.own), channel_id=1, source_target_pairs={{0,2},{1,3},{2,0},{3,1},{4,6},{5,7},{6,4},{7,5},{8,10},{9,11},{10,... | collective-permute-start | bytes 393224 | tf_op jit(solution)/shard_map/ppermute | solution.py:339
  86.7 25.9 %collective-permute-start.25 = (f32[64,2048]{1,0:T(8,128)S(1)}, f32[64,2048]{1,0:T(8,128)S(1)}, u32[]{:S(2)}, u32[]{:S(2)}) collective-permute-start(f32[64,2048]{1,0:T(8,128)S(1)} %get-tuple-element.82.refs_0_), channel_id=1, source_target_pairs={{0,4},{4,0},{8,12},{12,8},{1,5},{5,1},{9,13},{13,9},{2,6},{6,2},{1... | collective-permute-start | bytes 1572872 | tf_op jit(solution)/shard_map/ppermute | solution.py:333
  99.8 12.7 %collective-permute-start.26 = (f32[64,2048]{1,0:T(8,128)S(1)}, f32[64,2048]{1,0:T(8,128)S(1)}, u32[]{:S(2)}, u32[]{:S(2)}) collective-permute-start(f32[64,2048]{1,0:T(8,128)S(1)} %get-tuple-element.91.refs_1_), channel_id=1, source_target_pairs={{0,4},{4,0},{8,12},{12,8},{1,5},{5,1},{9,13},{13,9},{2,6},{6,2},{1... | collective-permute-start | bytes 1572872 | tf_op jit(solution)/shard_map/ppermute | solution.py:333
  110.0 9.1 %collective-permute-start.28 = (bf16[64,1024]{1,0:T(8,128)(2,1)S(1)}, bf16[64,1024]{1,0:T(8,128)(2,1)S(1)}, u32[]{:S(2)}, u32[]{:S(2)}) collective-permute-start(bf16[64,1024]{1,0:T(8,128)(2,1)S(1)} %pair_sum.11.refs_4_.own), channel_id=1, source_target_pairs={{0,2},{1,3},{2,0},{3,1},{4,6},{5,7},{6,4},{7,5},{8,10},{9,11},{10,... | collective-permute-start | bytes 393224 | tf_op jit(solution)/shard_map/ppermute | solution.py:339
  110.6 11.6 %collective-permute-start.29 = (f32[64,1024]{1,0:T(8,128)S(1)}, f32[64,1024]{1,0:T(8,128)S(1)}, u32[]{:S(2)}, u32[]{:S(2)}) collective-permute-start(f32[64,1024]{1,0:T(8,128)S(1)} %dual_update.10.refs_6_.refs_0_), channel_id=1, source_target_pairs={{0,1},{1,4},{2,3},{3,6},{4,5},{5,0},{6,7},{7,2},{8,9},{9,12},{10,1... | collective-permute-start | bytes 786440 | tf_op jit(solution)/shard_map/ppermute | solution.py:494
  111.9 10.4 %collective-permute-start.31 = (f32[64,1024]{1,0:T(8,128)S(1)}, f32[64,1024]{1,0:T(8,128)S(1)}, u32[]{:S(2)}, u32[]{:S(2)}) collective-permute-start(f32[64,1024]{1,0:T(8,128)S(1)} %dual_update.10.refs_6_.refs_0_), channel_id=1, source_target_pairs={{1,5},{3,7},{5,1},{7,3},{9,13},{11,15},{13,9},{15,11},{17,21},{19,... | collective-permute-start | bytes 786440 | tf_op jit(solution)/shard_map/ppermute | solution.py:495
  120.9 8.7 %collective-permute-start.30 = (f32[64,1024]{1,0:T(8,128)S(1)}, f32[64,1024]{1,0:T(8,128)S(1)}, u32[]{:S(2)}, u32[]{:S(2)}) collective-permute-start(f32[64,1024]{1,0:T(8,128)S(1)} %dual_update.11.refs_1_), channel_id=1, source_target_pairs={{0,1},{1,4},{2,3},{3,6},{4,5},{5,0},{6,7},{7,2},{8,9},{9,12},{10,1... | collective-permute-start | bytes 786440 | tf_op jit(solution)/shard_map/ppermute | solution.py:494
  120.9 8.6 %collective-permute-start.32 = (f32[64,1024]{1,0:T(8,128)S(1)}, f32[64,1024]{1,0:T(8,128)S(1)}, u32[]{:S(2)}, u32[]{:S(2)}) collective-permute-start(f32[64,1024]{1,0:T(8,128)S(1)} %dual_update.11.refs_1_), channel_id=1, source_target_pairs={{1,5},{3,7},{5,1},{7,3},{9,13},{11,15},{13,9},{15,11},{17,21},{19,... | collective-permute-start | bytes 786440 | tf_op jit(solution)/shard_map/ppermute | solution.py:495
  (21 other events, 111.0 us)

commit v4 on v3

v4 whole, which is shorter than its diff:
```python
import functools

import jax
import jax.numpy as jnp
from jax import lax
from jax.experimental import pallas as pl
from jax.experimental.pallas import tpu as pltpu
from jax.sharding import PartitionSpec as P

ITERS = 3
STEP_SCALE = 0.5
BATCHES = 2
LAG = 1
STAGE_FLOPS = 4 * 10**9
TAIL = 128

bf16 = jnp.bfloat16
f32 = jnp.float32

SMEM = pl.BlockSpec(memory_space=pltpu.SMEM)
VMEM = pl.BlockSpec(memory_space=pltpu.VMEM)
ANY = pl.BlockSpec(memory_space=pl.ANY)
HBM = pl.BlockSpec(memory_space=pltpu.HBM)


def split_sums(*totals):
    lane = lax.broadcasted_iota(jnp.int32, (totals[0].shape[0], TAIL), 1)
    block = jnp.zeros(lane.shape, f32)
    for k, rest in enumerate(totals):
        for part in range(3):
            rounded = rest.astype(bf16).astype(f32)
            block = jnp.where(lane == 3 * k + part, rounded, block)
            rest = rest - rounded
    return block.astype(bf16)


def join_sum(block, k=0):
    lane = lax.broadcasted_iota(jnp.int32, block.shape, 1)
    mine = (lane >= 3 * k) & (lane < 3 * k + 3)
    return jnp.sum(jnp.where(mine, block.astype(f32), 0.0), axis=1, keepdims=True)


def tree_sum(terms):
    terms = list(terms)
    while len(terms) > 1:
        terms = [terms[k] + terms[k + 1] for k in range(0, len(terms), 2)]
    return terms[0]


def set_state(weight, total):
    lane = lax.broadcasted_iota(jnp.int32, (weight.shape[0], TAIL), 1)
    return jnp.where(lane == 0, weight, jnp.where(lane == 1, total, 0.0))


class Blocks:
    def __init__(self, order, slots, cols):
        self.order, self.slots, self.cols = order, slots, cols
        self.n = order[order.shape[0] - 1]

    def ready(self, spot):
        pass

    def run(self, body):
        def several(first, width):
            spots = [self.order[first + q] for q in range(width)]
            for spot in spots:
                self.ready(spot)
            for spot in spots:
                body(spot // self.cols, spot % self.cols, self.slots[spot])

        def four(u, carry):
            several(u * 4, 4)
            return carry

        lax.fori_loop(0, self.n // 4, four, 0)
        pl.when(self.n % 4 >= 2)(lambda: several(self.n // 4 * 4, 2))
        pl.when(self.n % 2 == 1)(lambda: several(self.n - 1, 1))

    def back(self, vector, acc):
        size_r, size_c = self.slots.shape[1:]
        acc[...] = jnp.zeros_like(acc)

        def body(i, j, block):
            rows = vector[:, pl.ds(pl.multiple_of(i * size_r, size_r), size_r)]
            acc[:, pl.ds(pl.multiple_of(j * size_c, size_c), size_c)] += jnp.dot(
                rows, block, preferred_element_type=f32
            )

        self.run(body)

    def forward(self, vector, acc):
        size_c, size_r = self.slots.shape[1:]
        acc[...] = jnp.zeros_like(acc)

        def body(i, j, block):
            cols = vector[:, pl.ds(pl.multiple_of(j * size_c, size_c), size_c)]
            acc[:, pl.ds(pl.multiple_of(i * size_r, size_r), size_r)] += jnp.dot(
                cols, block, preferred_element_type=f32
            )

        self.run(body)


class Incoming(Blocks):
    def __init__(self, tile_map, source, slots, sems, order, partner_flag=None):
        each, cols = tile_map.shape
        first_row = each if partner_flag else 0
        size_r, size_c = slots.shape[1:]
        n = jnp.int32(0)
        for i in range(each + first_row):
            for j in range(cols):
                spot = i * cols + j
                nonzero = tile_map[i, j] != 0 if i < each else partner_flag(spot - each * cols) != 0

                @pl.when(nonzero)
                def _():
                    order[n] = spot
                    if i >= first_row:
                        pltpu.make_async_copy(
                            source.at[pl.ds((i - first_row) * size_r, size_r), pl.ds(j * size_c, size_c)],
                            slots.at[spot],
                            sems.at[spot],
                        ).start()

                n = n + nonzero.astype(jnp.int32)
        order[order.shape[0] - 1] = n
        self.sems = sems
        super().__init__(order, slots, cols)
        self.n = n

    def ready(self, spot):
        pltpu.make_async_copy(self.slots.at[spot], self.slots.at[spot], self.sems.at[spot]).wait()


def first_kernel(tile_map, place, blocks, dual, cost, lower, upper, code, weights, *refs):
    mine, others, vectors = refs[0], refs[1 : 1 + BATCHES], refs[1 + BATCHES]
    states = refs[2 + BATCHES : 2 + 2 * BATCHES]
    slots, sems, order, vector, acc, start, sem = refs[2 + 2 * BATCHES :]
    fetch = pltpu.make_async_copy(dual, start, sem)
    fetch.start()
    incoming = Incoming(tile_map, blocks, slots, sems, order)
    width = mine.shape[0]
    size = width // BATCHES
    low_on = (code[...] == 1) | (code[...] == 3)
    high_on = (code[...] == 2) | (code[...] == 3)
    vectors[0:1] = cost[...]
    vectors[1:2] = jnp.where(low_on, lower[...], -jnp.inf)
    vectors[2:3] = jnp.where(high_on, upper[...], jnp.inf)
    here = pl.multiple_of(place[1] * width, width)
    column = jnp.broadcast_to(weights[:, pl.ds(here, width)], (TAIL, width)).T
    for b, state in enumerate(states):
        state[...] = column[b * size : (b + 1) * size]
    fetch.wait()
    vector[...] = start[...].T.astype(bf16)
    incoming.back(vector, acc)
    mine[...] = acc[pl.ds(here, width)]
    there = pl.multiple_of((1 - place[1]) * width, width)
    for b, other in enumerate(others):
        other[:size] = acc[pl.ds(there + b * size, size)]
    lane = lax.broadcasted_iota(jnp.int32, (8, vector.shape[1]), 1)
    flags = jnp.zeros(lane.shape, jnp.int32)
    for t in range(tile_map.shape[0] * tile_map.shape[1]):
        flags = jnp.where(lane == t, tile_map[t // tile_map.shape[1], t % tile_map.shape[1]], flags)
    others[0][size:, : lane.shape[1]] = flags.astype(f32)


def load_kernel(second, tile_map, source, *refs):
    slots, turned, order, sems = refs[-4:]
    partner_flag = None
    if second:
        partner_flag = lambda t: refs[0][refs[0].shape[0] - 8, t]
    incoming = Incoming(tile_map, source, slots, sems, order, partner_flag)
    first_row = tile_map.shape[0] if second else 0

    def one(q, carry):
        spot = order[q]

        @pl.when(spot >= first_row * incoming.cols)
        def _():
            incoming.ready(spot)
            turned[spot] = slots[spot].T

        return carry

    lax.fori_loop(0, incoming.n, one, 0)


def first_pack_kernel(batch, mine, other, after, msg):
    size = msg.shape[0]
    msg[...] = (mine[batch * size : (batch + 1) * size] + other[:size]).astype(bf16)


def back_kernel(grid_cols, order, place, own_half, got_half, slots, after, msg, *refs):
    vector, acc = refs[-2:]
    half = vector.shape[1] // 2
    side = place[0] % 2
    vector[:, pl.ds(pl.multiple_of(side * half, half), half)] = own_half[:, :half]
    vector[:, pl.ds(pl.multiple_of((1 - side) * half, half), half)] = got_half[:, :half]
    if len(refs) == 3:
        refs[0][...] = vector[:, half:]
    Blocks(order, slots, grid_cols).back(vector, acc)
    width = acc.shape[1]
    msg[:, :width] = acc[...].astype(bf16)
    tails = own_half[:, half:], got_half[:, half:]
    msg[:, width:] = split_sums(*[join_sum(tails[0], k) + join_sum(tails[1], k) for k in range(2)])


def forward_kernel(grid_cols, near, first, last, total_rows, total_cols, order, place, *refs):
    msgs = refs[:near]
    primal, vectors, state, turned, after_ref = refs[near : near + 5]
    primal_next, kept, sent, state_out, vector, acc = refs[near + 5 :]
    width = primal.shape[1]
    weight = state[:, 0:1]
    if not first:
        sum_y = tree_sum([join_sum(ref[:, width:]) for ref in msgs])
        move_y = jnp.sqrt(sum_y / total_rows + 1e-06)
        sum_x = join_sum(msgs[0][:, width:], 1)
        move_x = jnp.sqrt(sum_x / total_cols + 1e-06)
        weight = jnp.sqrt(weight * move_y / move_x)
    step = STEP_SCALE / weight
    image_t = tree_sum([ref[:, :width].astype(f32) for ref in msgs])
    before = primal[...]
    after = before - step * (vectors[0:1] - image_t)
    after = jnp.minimum(jnp.maximum(after, vectors[1:2]), vectors[2:3])
    primal_next[...] = after
    vector[...] = (2.0 * after - before).astype(bf16)
    sum_x = jnp.zeros_like(weight) if last else jnp.sum((after - before) ** 2, axis=1, keepdims=True)
    state_out[...] = set_state(weight, sum_x)
    Blocks(order, turned, grid_cols).forward(vector, acc)
    half = acc.shape[1] // 2
    side = place[0] % 2
    kept[...] = acc[:, pl.ds(pl.multiple_of(side * half, half), half)]
    sent[...] = acc[:, pl.ds(pl.multiple_of((1 - side) * half, half), half)].astype(bf16)


def pair_kernel(kept, state, got, after, msg):
    half = kept.shape[1]
    msg[:, :half] = (kept[...] + got[...].astype(f32)).astype(bf16)
    if msg.shape[1] > half:
        msg[:, half:] = split_sums(state[:, 1:2])


def cross_kernel(half, own, got, msg):
    msg[:, :half] = (own[:, :half].astype(f32) + got[:, :half].astype(f32)).astype(bf16)
    if msg.shape[1] > half:
        msg[:, half:] = split_sums(join_sum(own[:, half:]) + join_sum(got[:, half:]))


def dual_kernel(last, own, got, state, dual, right, floor, before_ref, after_ref, dual_next, msg):
    half = dual.shape[1]
    image = own[:, :half].astype(f32) + got[:, :half].astype(f32)
    before = dual[...]
    after = before + STEP_SCALE * state[:, 0:1] * (right[...] - image)
    after = jnp.maximum(after, floor[0:1])
    if last:
        rounded = before_ref[:, :half].astype(f32)
        step = (after - rounded).astype(bf16)
        msg[...] = step
        dual_next[...] = rounded + step.astype(f32)
    else:
        dual_next[...] = after
        msg[:, :half] = after.astype(bf16)
        sum_y = jnp.sum((after - before) ** 2, axis=1, keepdims=True)
        msg[:, half:] = split_sums(sum_y, join_sum(own[:, half:]) + join_sum(got[:, half:]))


def turn_kernel(place, value, after, *refs):
    outs, (held, sem) = refs[:BATCHES], refs[BATCHES:]
    size = outs[0].shape[0]
    width = size * BATCHES
    fetch = pltpu.make_async_copy(value.at[:, pl.ds(pl.multiple_of(place[1] * width, width), width)], held, sem)
    fetch.start()
    fetch.wait()
    turned = held[...].T
    for b, out in enumerate(outs):
        out[...] = turned[b * size : (b + 1) * size]


def rows_kernel(place, dual, right, kind, got_dual, got_right, got_kind, after, floor, *refs):
    outs, (held, sems) = refs[: 2 * BATCHES], refs[2 * BATCHES :]
    size = outs[0].shape[0]
    width = size * BATCHES
    rows = dual.shape[0]
    here = pl.ds(pl.multiple_of(place[1] * width, width), width)

    def put(dual, right, kind):
        copies = [
            pltpu.make_async_copy(dual.at[:, here], held.at[pl.ds(0, rows)], sems.at[0]),
            pltpu.make_async_copy(right.at[:, here], held.at[pl.ds(rows, rows)], sems.at[1]),
        ]
        for copy in copies:
            copy.start()
        floor[...] = jnp.where(kind[...] == 1, 0.0, -jnp.inf)
        for k, copy in enumerate(copies):
            copy.wait()
            turned = held[k * rows : (k + 1) * rows].T
            for b in range(BATCHES):
                outs[k * BATCHES + b][...] = turned[b * size : (b + 1) * size]

    pl.when(place[0] % 2 == 0)(lambda: put(dual, right, kind))
    pl.when(place[0] % 2 == 1)(lambda: put(got_dual, got_right, got_kind))


def put_half(out, core, parts):
    width = out.shape[1] // 2
    out[:, pl.ds(pl.multiple_of(core * width, width), width)] = jnp.concatenate([r[...] for r in parts], axis=0).T


def primal_out_kernel(place, *refs):
    mine, theirs, (out, token) = refs[:BATCHES], refs[BATCHES : 2 * BATCHES], refs[-2:]
    token[...] = jnp.zeros_like(token)
    put_half(out, place[1], mine)
    put_half(out, 1 - place[1], theirs)


def dual_out_kernel(place, own, got_step, partner_step, got_before, partner_before, after, *refs):
    out = refs[-1]

    def put(mine, theirs):
        rows = jnp.concatenate([mine(), theirs()], axis=0).T
        if len(refs) == 1:
            out[...] = rows
            return
        before = refs[0][...]
        width = before.shape[1]
        low = lax.broadcasted_iota(jnp.int32, before.shape, 1) < width // 2
        out[:, pl.ds(pl.multiple_of(place[1] * width, width), width)] = jnp.where(
            low, before, pltpu.roll(rows, width // 2, 1)
        )
        out[:, pl.ds(pl.multiple_of((1 - place[1]) * width, width), width)] = jnp.where(
            low, pltpu.roll(before, width // 2, 1), rows
        )

    def moved(before, step):
        return before[:, : step.shape[1]].astype(f32) + step[...].astype(f32)

    even = (lambda: own[...]), (lambda: moved(partner_before, got_step))
    odd = (lambda: moved(got_before, got_step)), (lambda: moved(partner_before, partner_step))
    pl.when(place[0] % 2 == 0)(lambda: put(*even))
    pl.when(place[0] % 2 == 1)(lambda: put(*odd))


def call(kernel, out_shape, in_specs, scratch=(), flops=0, name=None, vmem=6, out_specs=None):
    return pl.pallas_call(
        kernel,
        out_shape=out_shape,
        in_specs=in_specs,
        out_specs=out_specs or jax.tree.map(lambda _: VMEM, out_shape),
        scratch_shapes=list(scratch),
        compiler_params=pltpu.CompilerParams(vmem_limit_bytes=vmem << 20),
        cost_estimate=pl.CostEstimate(flops=flops, bytes_accessed=0, transcendentals=0),
        name=name,
    )


def shape(rows, cols, kind=f32):
    return jax.ShapeDtypeStruct((rows, cols), kind)


def local(
    blocks,
    tile_map,
    lower_bound,
    upper_bound,
    bound_code,
    row_kind,
    cost_vector,
    right_side,
    primal_start,
    dual_start,
    primal_weight,
):
    rows, cols = blocks.shape
    size_r = rows // tile_map.shape[0]
    size_c = cols // tile_map.shape[1]
    profiles = dual_start.shape[1]
    width = profiles // 2
    size = width // BATCHES
    count = lax.axis_size("col")
    near = lax.axis_size("row") // 2
    total_rows = rows * near * 2
    total_cols = cols * count
    z = lax.axis_index("col")
    core = lax.axis_index("row") % 2
    place = jnp.stack([z, core]).astype(jnp.int32)

    def to_core(value):
        return lax.ppermute(value, "row", [(i, i ^ 1) for i in range(2 * near)])

    def to_x(value, k):
        return lax.ppermute(value, "row", [(i, i ^ (2 * k)) for i in range(2 * near)])

    def to_z(value, k):
        return lax.ppermute(value, "col", [(i, i ^ k) for i in range(count)])

    to_holder = [
        (r * count + c, (r ^ (c % 2)) * count + (c ^ 1)) for r in range(2 * near) for c in range(count)
    ]

    n_own = tile_map.size
    n_chip = 2 * n_own
    grid_cols = tile_map.shape[1]

    blocks, tile_map, primal_start, dual_start, right_side = (
        pltpu.with_memory_space_constraint(value, pltpu.HBM)
        for value in (blocks, tile_map, primal_start, dual_start, right_side)
    )
    vectors = [
        pltpu.with_memory_space_constraint(value[None, :], pltpu.HBM)
        for value in (cost_vector, lower_bound, upper_bound, bound_code, primal_weight)
    ]
    partner = to_core(blocks)
    mine, *rest = call(
        first_kernel,
        (shape(width, cols),)
        + (shape(size + 8, cols),)
        + (shape(size, cols),) * (BATCHES - 1)
        + (shape(8, cols),)
        + (shape(size, TAIL),) * BATCHES,
        [SMEM, SMEM, HBM, HBM] + [VMEM] * 5,
        [
            pltpu.VMEM((n_own, size_r, size_c), bf16),
            pltpu.SemaphoreType.DMA((n_own,)),
            pltpu.SMEM((n_own + 1,), jnp.int32),
            pltpu.VMEM((profiles, rows), bf16),
            pltpu.VMEM((profiles, cols), f32),
            pltpu.VMEM((rows, profiles), f32),
            pltpu.SemaphoreType.DMA,
        ],
        name="first_product",
        vmem=20,
    )(
        tile_map,
        place,
        blocks,
        dual_start,
        *vectors,
    )
    others = [to_core(other) for other in rest[:BATCHES]]
    vectors, state = rest[BATCHES], list(rest[BATCHES + 1 :])
    sides = dual_start, right_side, row_kind[None, :]
    sides += tuple(to_core(value) for value in sides)

    def half_msg(tail):
        return shape(size, rows + (TAIL if tail else 0), bf16)

    def back(b, iteration, after):
        if iteration == 0:
            messages[b] = call(
                functools.partial(first_pack_kernel, b),
                shape(size, cols, bf16),
                [VMEM] * 2 + [ANY],
                flops=STAGE_FLOPS,
                name="first_pack",
            )(mine, others[b], after)
        else:
            last = iteration + 1 == ITERS
            outs = call(
                functools.partial(back_kernel, grid_cols),
                (shape(size, cols + TAIL, bf16),) + (half_msg(False),) * last,
                [SMEM, SMEM, VMEM, VMEM, VMEM, ANY],
                [pltpu.VMEM((size, 2 * rows), bf16), pltpu.VMEM((size, cols), f32)],
                flops=STAGE_FLOPS,
                name="back_product",
            )(order, place, *halves[b], slots, after)
            messages[b] = outs[0]
            if last:
                partner_before[b] = to_core(outs[1])
        return messages[b]

    def forward(b, iteration, after):
        first, last = iteration == 0, iteration + 1 == ITERS
        msgs = [messages[b]] + [to_x(messages[b], k) for k in range(1, near)]
        outs = call(
            functools.partial(forward_kernel, grid_cols, near, first, last, total_rows, total_cols),
            (shape(size, cols), shape(size, rows), half_msg(False), shape(size, TAIL)),
            [SMEM, SMEM] + [VMEM] * (near + 4) + [ANY],
            [pltpu.VMEM((size, cols), bf16), pltpu.VMEM((size, 2 * rows), f32)],
            flops=STAGE_FLOPS,
            name="forward_product",
        )(order, place, *msgs, primal[b], vectors, state[b], turned, after)
        primal[b], kept[b], sent[b], state[b] = outs
        return state[b]

    def pair(b, iteration, after):
        out = half_msg(iteration + 1 < ITERS)
        crossing[b] = call(pair_kernel, out, [VMEM] * 3 + [ANY], flops=STAGE_FLOPS, name="pair_sum")(
            kept[b], state[b], to_z(sent[b], 1), after
        )
        mask = 2
        while mask * 2 < count:
            crossing[b] = call(functools.partial(cross_kernel, rows), out, [VMEM] * 2, name="cross_sum")(
                crossing[b], to_z(crossing[b], mask)
            )
            mask *= 2
        return crossing[b]

    def update(b, iteration, after):
        last = iteration + 1 == ITERS
        got = to_z(crossing[b], count // 2)
        dual[b], msg = call(
            functools.partial(dual_kernel, last),
            (shape(size, rows), half_msg(not last)),
            [VMEM] * 6 + [VMEM if last else ANY, ANY],
            flops=STAGE_FLOPS,
            name="dual_update",
        )(crossing[b], got, state[b], dual[b], right[b], floor, halves[b][0] if last else after, after)
        if last:
            steps[b] = lax.ppermute(msg, ("row", "col"), to_holder), to_core(msg)
        else:
            halves[b] = msg, to_z(msg, 1)
        return msg

    plan = []
    for b in range(BATCHES):
        at = b * LAG
        for iteration in range(ITERS):
            for stage in (back, forward, pair, update):
                plan.append((at, b, iteration, stage))
                at += 1
    plan.sort(key=lambda entry: entry[:3])

    messages, halves, kept, sent, crossing, steps, partner_before = ([None] * BATCHES for _ in range(7))
    loaded = (
        pltpu.VMEM((n_chip, size_r, size_c), bf16),
        pltpu.VMEM((n_chip, size_c, size_r), bf16),
        jax.ShapeDtypeStruct((n_chip + 1,), jnp.int32),
    )

    def load(second, source, operands, in_specs, aliases):
        return pl.pallas_call(
            functools.partial(load_kernel, second),
            out_shape=loaded,
            in_specs=[SMEM, HBM] + in_specs,
            out_specs=(VMEM, VMEM, SMEM),
            scratch_shapes=[pltpu.SemaphoreType.DMA((n_chip,))],
            input_output_aliases=aliases,
            compiler_params=pltpu.CompilerParams(vmem_limit_bytes=4 << 20),
            cost_estimate=pl.CostEstimate(flops=0, bytes_accessed=0, transcendentals=0),
            name="load_blocks",
        )(tile_map, source, *operands)

    plan = [(b, iteration, stage) for _, b, iteration, stage in plan]
    primal = list(
        call(
            turn_kernel,
            (shape(size, cols),) * BATCHES,
            [SMEM, HBM, ANY],
            [pltpu.VMEM((cols, width), f32), pltpu.SemaphoreType.DMA],
            name="turn_primal",
        )(place, primal_start, state[0])
    )
    token = primal[0]
    for b, iteration, stage in plan:
        token = stage(b, iteration, token)
        if (b, iteration, stage) == (0, 0, back):
            slots, turned, order = load(False, blocks, (token,), [ANY], {})
            slots, turned, order = load(
                True, partner, (others[0], slots, turned), [VMEM, ANY, ANY], {3: 0, 4: 1}
            )
        if (b, iteration, stage) == (0, 0, forward):
            floor, *held = call(
                rows_kernel,
                (shape(1, rows),) + (shape(size, rows),) * (2 * BATCHES),
                [SMEM] + [HBM, HBM, VMEM] * 2 + [ANY],
                [pltpu.VMEM((2 * rows, width), f32), pltpu.SemaphoreType.DMA((2,))],
                name="turn_rows",
            )(place, *sides, token)
            dual, right = held[:BATCHES], held[BATCHES:]
        if (b, iteration, stage) == (BATCHES - 1, ITERS - 1, pair):
            primal_final, token = call(
                primal_out_kernel,
                (pltpu.HBM((cols, profiles), f32), shape(8, TAIL)),
                [SMEM] + [VMEM] * (2 * BATCHES) + [ANY],
                name="primal_out",
            )(place, *primal, *[to_core(p) for p in primal], token)

    def dual_out(b, out_shape, flops, name, *others):
        return call(
            dual_out_kernel, out_shape, [SMEM] + [VMEM] * 5 + [ANY] + [VMEM] * len(others), flops=flops, name=name
        )(place, dual[b], *steps[b], halves[b][1], partner_before[b], token, *others)

    first_rows = dual_out(0, shape(rows, 2 * size), STAGE_FLOPS, "dual_part")
    dual_final = dual_out(1, shape(rows, profiles), 0, "dual_out", first_rows)
    return primal_final, dual_final


def solution(mesh):
    return jax.shard_map(
        local,
        mesh=mesh,
        in_specs=(
            P("row", "col"),
            P("row", "col"),
            P("col"),
            P("col"),
            P("col"),
            P("row"),
            P("col"),
            P("row", "groups"),
            P("col", "groups"),
            P("row", "groups"),
            P("groups"),
        ),
        out_specs=(P("col", "groups"), P("row", "groups")),
        check_vma=False,
    )
```

time: 134 us -> 114 us (0.85)
  waiting for transfers between devices: 52.8 us -> 27.7 us
  starting transfers between devices: 39.4 us -> 44.2 us
  Pallas kernels: 32.9 us -> 37.5 us
  local copies, waits for them, and re-layouts: 4.37 us -> 1.93 us
    ppermute x16, waiting for transfers between devices: 33.5 us -> 19.9 us  [to_z(): return lax.ppermute(value, 'col', [(i, i ^ k) for i in range(count)])]
    ppermute x4 -> x2, waiting for transfers between devices: 7.93 us -> 1.48 us  [update(): steps[b] = (lax.ppermute(msg, ('row', 'col'), to_holder), to_core(msg))]
    ppermute x16, starting transfers between devices: 7.81 us -> 14 us  [to_z(): return lax.ppermute(value, 'col', [(i, i ^ k) for i in range(count)])]
    ppermute x6, starting transfers between devices: 9.66 us -> 3.64 us  [to_x(): return lax.ppermute(value, 'row', [(i, i ^ 2 * k) for i in range(2 * near)])]
    ppermute x7 -> x12, starting transfers between devices: 19.2 us -> 24.4 us  [to_core(): return lax.ppermute(value, 'row', [(i, i ^ 1) for i in range(2 * near)])]
    ppermute x6, waiting for transfers between devices: 9.57 us -> 4.76 us  [to_x(): return lax.ppermute(value, 'row', [(i, i ^ 2 * k) for i in range(2 * near)])]
    pallas_call x23 -> x24, Pallas kernels: 21.6 us -> 26.3 us  [the longest x4 6.09 us: back(): call(functools.partial(back_kernel, grid_cols), (shape(size, cols + TAIL,...]
    unnamed x24 -> x6, local copies, waits for them, and re-layouts: 4.08 us -> 1.93 us
  transfers between devices with their start and end apart: 33 -> 36, of which waited for: 21 -> 16; matrix products, arithmetic and copies ran while one was open for 1% -> 0% of each run, Pallas kernels for 22% -> 32%
where the time goes in v4:
time: 114 us; the launch traced here: 112 us
  starting transfers between devices  44.2 us (39%)
  Pallas kernels  37.5 us (33%)
  waiting for transfers between devices  27.7 us (24%)
  local copies, waits for them, and re-layouts  1.93 us (2%)
    ppermute x12, starting transfers between devices, to_core(): return lax.ppermute(value, 'row', [(i, i ^ 1) for i in range(2 * near)])  24.4 us
    ppermute x16, waiting for transfers between devices, to_z(): return lax.ppermute(value, 'col', [(i, i ^ k) for i in range(count)])  19.9 us
    ppermute x16, starting transfers between devices, to_z(): return lax.ppermute(value, 'col', [(i, i ^ k) for i in range(count)])  14 us
    pallas_call x6, Pallas kernels, forward(): call(functools.partial(forward_kernel, grid_cols, near, first, last, tota...  11.2 us
    pallas_call x4, Pallas kernels, back(): call(functools.partial(back_kernel, grid_cols), (shape(size, cols + TAIL,...  6.09 us
    pallas_call x2, Pallas kernels, load(): pl.pallas_call(functools.partial(load_kernel, second), out_shape=loaded,...  6.06 us
    ppermute x6, waiting for transfers between devices, to_x(): return lax.ppermute(value, 'row', [(i, i ^ 2 * k) for i in range(2 * near)])  4.76 us
    ppermute x6, starting transfers between devices, to_x(): return lax.ppermute(value, 'row', [(i, i ^ 2 * k) for i in range(2 * near)])  3.64 us
  transfers between devices with their start and end apart: 36, of which 16 were waited for; matrix products, arithmetic and copies ran while one was open for 0% of the time, Pallas kernels for 32%

profile of v4, /device:TPU:5, one launch (start us, length us, event | category | flops | bytes accessed | tf_op | source)
XLA Modules:
  0.0 112.3 jit_solution(7889958559112091180)
XLA Ops:
  1.4 3.0 %first_product.1 = (f32[128,2048]{1,0:T(8,128)S(1)}, f32[72,2048]{1,0:T(8,128)S(1)}, f32[64,2048]{1,0:T(8,128)S(1)}, f32[8,2048]{1,0:T(8,128)S(1)}, f32[64,128]{1,0:T(8,128)S(1)}, /*index=5*/f32[64,128]{1,0:T(8,128)S(1)}) custom-call(s32[2,4]{1,0:T(2,128)} %tile_map.5, s32[2]{0:T(128)S(1)} %pad_add_fusion.place, bf16[1024,2048]{1,0:T(8,128)(2,1)} %source.1, ...), custom_call_target="tpu_custom_call" | custom-call | tf_op jit(solution)/shard_map/first_product/pallas_call | solution.py:413
  6.3 2.1 %turn_primal.1 = (f32[64,2048]{1,0:T(8,128)S(1)}, f32[64,2048]{1,0:T(8,128)S(1)}) custom-call(s32[2]{0:T(128)S(1)} %pad_add_fusion.place, f32[2048,256]{1,0:T(8,128)} %value.1, f32[64,128]{1,0:T(8,128)S(1)} %get-tuple-element.64.after.refs_4_), custom_call_target="tpu_custom_call" | custom-call | tf_op jit(solution)/shard_map/turn_primal/pallas_call | solution.py:545
  11.8 2.6 %load_blocks.2 = (bf16[16,512,512]{2,1,0:T(8,128)(2,1)S(1)}, bf16[16,512,512]{2,1,0:T(8,128)(2,1)S(1)}, s32[17]{0:T(128)}) custom-call(s32[2,4]{1,0:T(2,128)} %tile_map.5, bf16[1024,2048]{1,0:T(8,128)(2,1)} %source.1, bf16[64,2048]{1,0:T(8,128)(2,1)S(1)} %first_pack.2.refs_0_.refs_6_), custom_call_target="tpu_custom_call" | custom-call | tf_op jit(solution)/shard_map/load_blocks/pallas_call | solution.py:531
  15.3 3.5 %load_blocks.3 = (bf16[16,512,512]{2,1,0:T(8,128)(2,1)S(1)}, bf16[16,512,512]{2,1,0:T(8,128)(2,1)S(1)}, s32[17]{0:T(128)S(1)}) custom-call(s32[2,4]{1,0:T(2,128)} %tile_map.5, bf16[1024,2048]{1,0:T(8,128)(2,1)} %collective-permute-done.source, f32[72,2048]{1,0:T(8,128)S(1)} %collective-permute-done.1.other.refs_0_, ...), custom_call_target="tpu_custom_call", output_to_operand_aliasing={{0}: (3, {}), {1}: (4, {})} | custom-call | tf_op jit(solution)/shard_map/load_blocks/pallas_call | solution.py:531
  23.3 2.0 %turn_rows.1 = (f32[1,1024]{1,0:T(1,128)S(1)}, f32[64,1024]{1,0:T(8,128)S(1)}, f32[64,1024]{1,0:T(8,128)S(1)}, f32[64,1024]{1,0:T(8,128)S(1)}, f32[64,1024]{1,0:T(8,128)S(1)}) custom-call(s32[2]{0:T(128)S(1)} %pad_add_fusion.place, f32[1024,256]{1,0:T(8,128)} %dual.3, f32[1024,256]{1,0:T(8,128)} %right.1, s32[1,1024]{1,0:T(1,128)S(1)} %bitcast.9, ...), custom_call_target="tpu_custom_call" | custom-call | tf_op jit(solution)/shard_map/turn_rows/pallas_call | solution.py:562
  25.4 2.7 %collective-permute-start.5 = (bf16[64,1152]{1,0:T(8,128)(2,1)S(1)}, bf16[64,1152]{1,0:T(8,128)(2,1)S(1)}, u32[]{:S(2)}, u32[]{:S(2)}) collective-permute-start(bf16[64,1152]{1,0:T(8,128)(2,1)S(1)} %pair_sum.6.refs_6_.own), channel_id=1, source_target_pairs={{0,2},{1,3},{2,0},{3,1},{4,6},{5,7},{6,4},{7,5},{8,10},{9,11},{10,... | collective-permute-start | bytes 442376 | tf_op jit(solution)/shard_map/ppermute | solution.py:394
  31.1 4.0 %collective-permute-done.5.got = bf16[64,1152]{1,0:T(8,128)(2,1)S(1)} collective-permute-done((bf16[64,1152]{1,0:T(8,128)(2,1)S(1)}, bf16[64,1152]{1,0:T(8,128)(2,1)S(1)}, u32[]{:S(2)}, u32[]{:S(2)}) %collective-permute-start.5) | collective-permute-done | bytes 147488 | tf_op jit(solution)/shard_map/ppermute | solution.py:394
  41.4 4.6 %collective-permute-done.13.got = bf16[64,1152]{1,0:T(8,128)(2,1)S(1)} collective-permute-done((bf16[64,1152]{1,0:T(8,128)(2,1)S(1)}, bf16[64,1152]{1,0:T(8,128)(2,1)S(1)}, u32[]{:S(2)}, u32[]{:S(2)}) %collective-permute-start.13) | collective-permute-done | bytes 147488 | tf_op jit(solution)/shard_map/ppermute | solution.py:394
  47.0 1.9 %forward_product.8 = (f32[64,2048]{1,0:T(8,128)S(1)}, f32[64,1024]{1,0:T(8,128)S(1)}, bf16[64,1024]{1,0:T(8,128)(2,1)S(1)}, f32[64,128]{1,0:T(8,128)S(1)}) custom-call(s32[17]{0:T(128)S(1)} %get-tuple-element.68.order, s32[2]{0:T(128)S(1)} %pad_add_fusion.place, bf16[64,2176]{1,0:T(8,128)(2,1)S(1)} %back_product.4.before_ref.after_ref.refs_0_, ...), custom_call_target="tpu_custom_call" | custom-call | flops 4000000000 | tf_op jit(solution)/shard_map/forward_product/pallas_call | solution.py:474
  53.8 2.0 %collective-permute-start.16 = (bf16[64,1152]{1,0:T(8,128)(2,1)S(1)}, bf16[64,1152]{1,0:T(8,128)(2,1)S(1)}, u32[]{:S(2)}, u32[]{:S(2)}) collective-permute-start(bf16[64,1152]{1,0:T(8,128)(2,1)S(1)} %pair_sum.8.refs_6_.own), channel_id=1, source_target_pairs={{0,2},{1,3},{2,0},{3,1},{4,6},{5,7},{6,4},{7,5},{8,10},{9,11},{10,... | collective-permute-start | bytes 442376 | tf_op jit(solution)/shard_map/ppermute | solution.py:394
  57.4 1.9 %forward_product.9 = (f32[64,2048]{1,0:T(8,128)S(1)}, f32[64,1024]{1,0:T(8,128)S(1)}, bf16[64,1024]{1,0:T(8,128)(2,1)S(1)}, f32[64,128]{1,0:T(8,128)S(1)}) custom-call(s32[17]{0:T(128)S(1)} %get-tuple-element.68.order, s32[2]{0:T(128)S(1)} %pad_add_fusion.place, bf16[64,2176]{1,0:T(8,128)(2,1)S(1)} %back_product.5.after.refs_0_, ...), custom_call_target="tpu_custom_call" | custom-call | flops 4000000000 | tf_op jit(solution)/shard_map/forward_product/pallas_call | solution.py:474
  61.1 2.6 %collective-permute-done.19.got = bf16[64,1024]{1,0:T(8,128)(2,1)S(1)} collective-permute-done((bf16[64,1024]{1,0:T(8,128)(2,1)S(1)}, bf16[64,1024]{1,0:T(8,128)(2,1)S(1)}, u32[]{:S(2)}, u32[]{:S(2)}) %collective-permute-start.19) | collective-permute-done | bytes 131104 | tf_op jit(solution)/shard_map/ppermute | solution.py:394
  63.8 1.9 %collective-permute-start.21 = (bf16[64,1152]{1,0:T(8,128)(2,1)S(1)}, bf16[64,1152]{1,0:T(8,128)(2,1)S(1)}, u32[]{:S(2)}, u32[]{:S(2)}) collective-permute-start(bf16[64,1152]{1,0:T(8,128)(2,1)S(1)} %pair_sum.9.after.own), channel_id=1, source_target_pairs={{0,2},{1,3},{2,0},{3,1},{4,6},{5,7},{6,4},{7,5},{8,10},{9,11},{10,... | collective-permute-start | bytes 442376 | tf_op jit(solution)/shard_map/ppermute | solution.py:394
  68.5 1.9 %collective-permute-done.21.got = bf16[64,1152]{1,0:T(8,128)(2,1)S(1)} collective-permute-done((bf16[64,1152]{1,0:T(8,128)(2,1)S(1)}, bf16[64,1152]{1,0:T(8,128)(2,1)S(1)}, u32[]{:S(2)}, u32[]{:S(2)}) %collective-permute-start.21) | collective-permute-done | bytes 147488 | tf_op jit(solution)/shard_map/ppermute | solution.py:394
  70.8 2.4 %collective-permute-done.20.refs_1_ = bf16[64,2176]{1,0:T(8,128)(2,1)S(1)} collective-permute-done((bf16[64,2176]{1,0:T(8,128)(2,1)S(1)}, bf16[64,2176]{1,0:T(8,128)(2,1)S(1)}, u32[]{:S(2)}, u32[]{:S(2)}) %collective-permute-start.20) | collective-permute-done | bytes 278560 | tf_op jit(solution)/shard_map/ppermute | solution.py:391
  73.2 2.0 %forward_product.10 = (f32[64,2048]{1,0:T(8,128)S(1)}, f32[64,1024]{1,0:T(8,128)S(1)}, bf16[64,1024]{1,0:T(8,128)(2,1)S(1)}, f32[64,128]{1,0:T(8,128)S(1)}) custom-call(s32[17]{0:T(128)S(1)} %get-tuple-element.68.order, s32[2]{0:T(128)S(1)} %pad_add_fusion.place, bf16[64,2176]{1,0:T(8,128)(2,1)S(1)} %get-tuple-element.98.before_ref.after_ref.refs_0_, ...), custom_call_target="tpu_custom_call" | custom-call | flops 4000000000 | tf_op jit(solution)/shard_map/forward_product/pallas_call | solution.py:474
  78.3 6.7 %collective-permute-start.25 = (f32[64,2048]{1,0:T(8,128)S(1)}, f32[64,2048]{1,0:T(8,128)S(1)}, u32[]{:S(2)}, u32[]{:S(2)}) collective-permute-start(f32[64,2048]{1,0:T(8,128)S(1)} %get-tuple-element.102.refs_0_), channel_id=1, source_target_pairs={{0,4},{4,0},{8,12},{12,8},{1,5},{5,1},{9,13},{13,9},{2,6},{6,2},{1... | collective-permute-start | bytes 1572872 | tf_op jit(solution)/shard_map/ppermute | solution.py:388
  85.0 2.4 %collective-permute-start.28 = (bf16[64,1024]{1,0:T(8,128)(2,1)S(1)}, bf16[64,1024]{1,0:T(8,128)(2,1)S(1)}, u32[]{:S(2)}, u32[]{:S(2)}) collective-permute-start(bf16[64,1024]{1,0:T(8,128)(2,1)S(1)} %pair_sum.10.refs_6_.own), channel_id=1, source_target_pairs={{0,2},{1,3},{2,0},{3,1},{4,6},{5,7},{6,4},{7,5},{8,10},{9,11},{10,... | collective-permute-start | bytes 393224 | tf_op jit(solution)/shard_map/ppermute | solution.py:394
  89.3 5.1 %collective-permute-start.26 = (f32[64,2048]{1,0:T(8,128)S(1)}, f32[64,2048]{1,0:T(8,128)S(1)}, u32[]{:S(2)}, u32[]{:S(2)}) collective-permute-start(f32[64,2048]{1,0:T(8,128)S(1)} %get-tuple-element.108.refs_1_), channel_id=1, source_target_pairs={{0,4},{4,0},{8,12},{12,8},{1,5},{5,1},{9,13},{13,9},{2,6},{6,2},{1... | collective-permute-start | bytes 1572872 | tf_op jit(solution)/shard_map/ppermute | solution.py:388
  94.6 3.9 %collective-permute-start.35 = (bf16[64,1024]{1,0:T(8,128)(2,1)S(1)}, bf16[64,1024]{1,0:T(8,128)(2,1)S(1)}, u32[]{:S(2)}, u32[]{:S(2)}) collective-permute-start(bf16[64,1024]{1,0:T(8,128)(2,1)S(1)} %get-tuple-element.121), channel_id=1, source_target_pairs={{0,4},{4,0},{8,12},{12,8},{1,5},{5,1},{9,13},{13,9},{2,6},{6,2},{1... | collective-permute-start | bytes 393224 | tf_op jit(solution)/shard_map/ppermute | solution.py:388
  98.5 2.1 %collective-permute-start.33 = (bf16[64,1024]{1,0:T(8,128)(2,1)S(1)}, bf16[64,1024]{1,0:T(8,128)(2,1)S(1)}, u32[]{:S(2)}, u32[]{:S(2)}) collective-permute-start(bf16[64,1024]{1,0:T(8,128)(2,1)S(1)} %get-tuple-element.113.after), channel_id=1, source_target_pairs={{0,1},{1,4},{2,3},{3,6},{4,5},{5,0},{6,7},{7,2},{8,9},{9,12},{10,1... | collective-permute-start | bytes 393224 | tf_op jit(solution)/shard_map/ppermute | solution.py:509
  101.3 2.5 %primal_out.1 = (f32[2048,256]{1,0:T(8,128)}, f32[8,128]{1,0:T(8,128)S(1)}) custom-call(s32[2]{0:T(128)S(1)} %pad_add_fusion.place, f32[64,2048]{1,0:T(8,128)S(1)} %get-tuple-element.102.refs_0_, f32[64,2048]{1,0:T(8,128)S(1)} %get-tuple-element.108.refs_1_, f32[64,2048]{1,0:T(8,128)S(1)} %collective-permute-done.25.refs_2_, ...), custom_call_target="tpu_custom_call" | custom-call | tf_op jit(solution)/shard_map/primal_out/pallas_call | solution.py:571
  104.0 4.0 %collective-permute-start.31 = (bf16[64,1024]{1,0:T(8,128)(2,1)S(1)}, bf16[64,1024]{1,0:T(8,128)(2,1)S(1)}, u32[]{:S(2)}, u32[]{:S(2)}) collective-permute-start(bf16[64,1024]{1,0:T(8,128)(2,1)S(1)} %get-tuple-element.118.after), channel_id=1, source_target_pairs={{0,4},{4,0},{8,12},{12,8},{1,5},{5,1},{9,13},{13,9},{2,6},{6,2},{1... | collective-permute-start | bytes 393224 | tf_op jit(solution)/shard_map/ppermute | solution.py:388
  110.3 2.0 %dual_out.1 = f32[1024,256]{1,0:T(8,128)} custom-call(s32[2]{0:T(128)S(1)} %pad_add_fusion.place, f32[64,1024]{1,0:T(8,128)S(1)} %get-tuple-element.117.own, bf16[64,1024]{1,0:T(8,128)(2,1)S(1)} %collective-permute-done.30.got_step, bf16[64,1024]{1,0:T(8,128)(2,1)S(1)} %collective-permute-done.31.partner_step, ...), custom_call_target="tpu_custom_call" | custom-call | tf_op jit(solution)/shard_map/dual_out/pallas_call | solution.py:579
  (87 shorter events, 41.8 us)
Async XLA Ops:
  0.6 13.8 %collective-permute-start = (bf16[1024,2048]{1,0:T(8,128)(2,1)}, bf16[1024,2048]{1,0:T(8,128)(2,1)}, u32[]{:S(2)}, u32[]{:S(2)}) collective-permute-start(bf16[1024,2048]{1,0:T(8,128)(2,1)} %source.1), channel_id=1, source_target_pairs={{0,4},{4,0},{8,12},{12,8},{1,5},{5,1},{9,13},{13,9},{2,6},{6,2},{1... | collective-permute-start | bytes 12582920 | tf_op jit(solution)/shard_map/ppermute | solution.py:388
  5.8 15.6 %collective-permute-start.6 = (f32[1024,256]{1,0:T(8,128)}, f32[1024,256]{1,0:T(8,128)S(1)}, u32[]{:S(2)}, u32[]{:S(2)}) collective-permute-start(f32[1024,256]{1,0:T(8,128)} %dual.3), channel_id=1, source_target_pairs={{0,4},{4,0},{8,12},{12,8},{1,5},{5,1},{9,13},{13,9},{2,6},{6,2},{1... | collective-permute-start | bytes 3145736 | tf_op jit(solution)/shard_map/ppermute | solution.py:388
  5.9 15.5 %collective-permute-start.7 = (f32[1024,256]{1,0:T(8,128)}, f32[1024,256]{1,0:T(8,128)S(1)}, u32[]{:S(2)}, u32[]{:S(2)}) collective-permute-start(f32[1024,256]{1,0:T(8,128)} %right.1), channel_id=1, source_target_pairs={{0,4},{4,0},{8,12},{12,8},{1,5},{5,1},{9,13},{13,9},{2,6},{6,2},{1... | collective-permute-start | bytes 3145736 | tf_op jit(solution)/shard_map/ppermute | solution.py:388
  9.9 8.9 %collective-permute-start.2 = (bf16[64,2048]{1,0:T(8,128)(2,1)S(1)}, bf16[64,2048]{1,0:T(8,128)(2,1)S(1)}, u32[]{:S(2)}, u32[]{:S(2)}) collective-permute-start(bf16[64,2048]{1,0:T(8,128)(2,1)S(1)} %first_pack.2.refs_0_.refs_6_), channel_id=1, source_target_pairs={{0,8},{4,12},{8,0},{12,4},{1,9},{5,13},{9,1},{13,5},{2,10},{6,14},... | collective-permute-start | bytes 786440 | tf_op jit(solution)/shard_map/ppermute | solution.py:391
  11.2 9.5 %collective-permute-start.4 = (f32[64,2048]{1,0:T(8,128)S(1)}, f32[64,2048]{1,0:T(8,128)S(1)}, u32[]{:S(2)}, u32[]{:S(2)}) collective-permute-start(f32[64,2048]{1,0:T(8,128)S(1)} %get-tuple-element.74), channel_id=1, source_target_pairs={{0,4},{4,0},{8,12},{12,8},{1,5},{5,1},{9,13},{13,9},{2,6},{6,2},{1... | collective-permute-start | bytes 1572872 | tf_op jit(solution)/shard_map/ppermute | solution.py:388
  14.4 6.9 %collective-permute-start.8 = (s32[1,1024]{1,0:T(1,128)S(1)}, s32[1,1024]{1,0:T(1,128)S(1)}, u32[]{:S(2)}, u32[]{:S(2)}) collective-permute-start(s32[1,1024]{1,0:T(1,128)S(1)} %bitcast.8), channel_id=1, source_target_pairs={{0,4},{4,0},{8,12},{12,8},{1,5},{5,1},{9,13},{13,9},{2,6},{6,2},{1... | collective-permute-start | bytes 12296 | tf_op jit(solution)/shard_map/ppermute | solution.py:388
  20.7 7.4 %collective-permute-start.9 = (bf16[64,2048]{1,0:T(8,128)(2,1)S(1)}, bf16[64,2048]{1,0:T(8,128)(2,1)S(1)}, u32[]{:S(2)}, u32[]{:S(2)}) collective-permute-start(bf16[64,2048]{1,0:T(8,128)(2,1)S(1)} %first_pack.3.after.refs_0_), channel_id=1, source_target_pairs={{0,8},{4,12},{8,0},{12,4},{1,9},{5,13},{9,1},{13,5},{2,10},{6,14},... | collective-permute-start | bytes 786440 | tf_op jit(solution)/shard_map/ppermute | solution.py:391
  25.4 9.7 %collective-permute-start.5 = (bf16[64,1152]{1,0:T(8,128)(2,1)S(1)}, bf16[64,1152]{1,0:T(8,128)(2,1)S(1)}, u32[]{:S(2)}, u32[]{:S(2)}) collective-permute-start(bf16[64,1152]{1,0:T(8,128)(2,1)S(1)} %pair_sum.6.refs_6_.own), channel_id=1, source_target_pairs={{0,2},{1,3},{2,0},{3,1},{4,6},{5,7},{6,4},{7,5},{8,10},{9,11},{10,... | collective-permute-start | bytes 442376 | tf_op jit(solution)/shard_map/ppermute | solution.py:394
  29.9 7.1 %collective-permute-start.11 = (bf16[64,1024]{1,0:T(8,128)(2,1)S(1)}, bf16[64,1024]{1,0:T(8,128)(2,1)S(1)}, u32[]{:S(2)}, u32[]{:S(2)}) collective-permute-start(bf16[64,1024]{1,0:T(8,128)(2,1)S(1)} %get-tuple-element.84), channel_id=1, source_target_pairs={{0,1},{1,0},{2,3},{3,2},{4,5},{5,4},{6,7},{7,6},{8,9},{9,8},{10,11... | collective-permute-start | bytes 393224 | tf_op jit(solution)/shard_map/ppermute | solution.py:394
  37.1 8.9 %collective-permute-start.13 = (bf16[64,1152]{1,0:T(8,128)(2,1)S(1)}, bf16[64,1152]{1,0:T(8,128)(2,1)S(1)}, u32[]{:S(2)}, u32[]{:S(2)}) collective-permute-start(bf16[64,1152]{1,0:T(8,128)(2,1)S(1)} %pair_sum.7.after.own), channel_id=1, source_target_pairs={{0,2},{1,3},{2,0},{3,1},{4,6},{5,7},{6,4},{7,5},{8,10},{9,11},{10,... | collective-permute-start | bytes 442376 | tf_op jit(solution)/shard_map/ppermute | solution.py:394
  53.8 6.5 %collective-permute-start.16 = (bf16[64,1152]{1,0:T(8,128)(2,1)S(1)}, bf16[64,1152]{1,0:T(8,128)(2,1)S(1)}, u32[]{:S(2)}, u32[]{:S(2)}) collective-permute-start(bf16[64,1152]{1,0:T(8,128)(2,1)S(1)} %pair_sum.8.refs_6_.own), channel_id=1, source_target_pairs={{0,2},{1,3},{2,0},{3,1},{4,6},{5,7},{6,4},{7,5},{8,10},{9,11},{10,... | collective-permute-start | bytes 442376 | tf_op jit(solution)/shard_map/ppermute | solution.py:394
  63.8 6.6 %collective-permute-start.21 = (bf16[64,1152]{1,0:T(8,128)(2,1)S(1)}, bf16[64,1152]{1,0:T(8,128)(2,1)S(1)}, u32[]{:S(2)}, u32[]{:S(2)}) collective-permute-start(bf16[64,1152]{1,0:T(8,128)(2,1)S(1)} %pair_sum.9.after.own), channel_id=1, source_target_pairs={{0,2},{1,3},{2,0},{3,1},{4,6},{5,7},{6,4},{7,5},{8,10},{9,11},{10,... | collective-permute-start | bytes 442376 | tf_op jit(solution)/shard_map/ppermute | solution.py:394
  75.2 9.7 %collective-permute-start.24 = (bf16[64,1024]{1,0:T(8,128)(2,1)S(1)}, bf16[64,1024]{1,0:T(8,128)(2,1)S(1)}, u32[]{:S(2)}, u32[]{:S(2)}) collective-permute-start(bf16[64,1024]{1,0:T(8,128)(2,1)S(1)} %get-tuple-element.107), channel_id=1, source_target_pairs={{0,1},{1,0},{2,3},{3,2},{4,5},{5,4},{6,7},{7,6},{8,9},{9,8},{10,11... | collective-permute-start | bytes 393224 | tf_op jit(solution)/shard_map/ppermute | solution.py:394
  77.5 9.9 %collective-permute-start.23 = (bf16[64,2176]{1,0:T(8,128)(2,1)S(1)}, bf16[64,2176]{1,0:T(8,128)(2,1)S(1)}, u32[]{:S(2)}, u32[]{:S(2)}) collective-permute-start(bf16[64,2176]{1,0:T(8,128)(2,1)S(1)} %get-tuple-element.104.after.refs_0_), channel_id=1, source_target_pairs={{0,8},{4,12},{8,0},{12,4},{1,9},{5,13},{9,1},{13,5},{2,10},{6,14},... | collective-permute-start | bytes 835592 | tf_op jit(solution)/shard_map/ppermute | solution.py:391
  78.3 20.2 %collective-permute-start.25 = (f32[64,2048]{1,0:T(8,128)S(1)}, f32[64,2048]{1,0:T(8,128)S(1)}, u32[]{:S(2)}, u32[]{:S(2)}) collective-permute-start(f32[64,2048]{1,0:T(8,128)S(1)} %get-tuple-element.102.refs_0_), channel_id=1, source_target_pairs={{0,4},{4,0},{8,12},{12,8},{1,5},{5,1},{9,13},{13,9},{2,6},{6,2},{1... | collective-permute-start | bytes 1572872 | tf_op jit(solution)/shard_map/ppermute | solution.py:388
  85.0 9.4 %collective-permute-start.28 = (bf16[64,1024]{1,0:T(8,128)(2,1)S(1)}, bf16[64,1024]{1,0:T(8,128)(2,1)S(1)}, u32[]{:S(2)}, u32[]{:S(2)}) collective-permute-start(bf16[64,1024]{1,0:T(8,128)(2,1)S(1)} %pair_sum.10.refs_6_.own), channel_id=1, source_target_pairs={{0,2},{1,3},{2,0},{3,1},{4,6},{5,7},{6,4},{7,5},{8,10},{9,11},{10,... | collective-permute-start | bytes 393224 | tf_op jit(solution)/shard_map/ppermute | solution.py:394
  89.3 11.3 %collective-permute-start.26 = (f32[64,2048]{1,0:T(8,128)S(1)}, f32[64,2048]{1,0:T(8,128)S(1)}, u32[]{:S(2)}, u32[]{:S(2)}) collective-permute-start(f32[64,2048]{1,0:T(8,128)S(1)} %get-tuple-element.108.refs_1_), channel_id=1, source_target_pairs={{0,4},{4,0},{8,12},{12,8},{1,5},{5,1},{9,13},{13,9},{2,6},{6,2},{1... | collective-permute-start | bytes 1572872 | tf_op jit(solution)/shard_map/ppermute | solution.py:388
  94.6 9.2 %collective-permute-start.29 = (bf16[64,1024]{1,0:T(8,128)(2,1)S(1)}, bf16[64,1024]{1,0:T(8,128)(2,1)S(1)}, u32[]{:S(2)}, u32[]{:S(2)}) collective-permute-start(bf16[64,1024]{1,0:T(8,128)(2,1)S(1)} %pair_sum.11.refs_4_.own), channel_id=1, source_target_pairs={{0,2},{1,3},{2,0},{3,1},{4,6},{5,7},{6,4},{7,5},{8,10},{9,11},{10,... | collective-permute-start | bytes 393224 | tf_op jit(solution)/shard_map/ppermute | solution.py:394
  94.6 9.4 %collective-permute-start.35 = (bf16[64,1024]{1,0:T(8,128)(2,1)S(1)}, bf16[64,1024]{1,0:T(8,128)(2,1)S(1)}, u32[]{:S(2)}, u32[]{:S(2)}) collective-permute-start(bf16[64,1024]{1,0:T(8,128)(2,1)S(1)} %get-tuple-element.121), channel_id=1, source_target_pairs={{0,4},{4,0},{8,12},{12,8},{1,5},{5,1},{9,13},{13,9},{2,6},{6,2},{1... | collective-permute-start | bytes 393224 | tf_op jit(solution)/shard_map/ppermute | solution.py:388
  98.5 10.3 %collective-permute-start.32 = (bf16[64,1024]{1,0:T(8,128)(2,1)S(1)}, bf16[64,1024]{1,0:T(8,128)(2,1)S(1)}, u32[]{:S(2)}, u32[]{:S(2)}) collective-permute-start(bf16[64,1024]{1,0:T(8,128)(2,1)S(1)} %get-tuple-element.119), channel_id=1, source_target_pairs={{0,4},{4,0},{8,12},{12,8},{1,5},{5,1},{9,13},{13,9},{2,6},{6,2},{1... | collective-permute-start | bytes 393224 | tf_op jit(solution)/shard_map/ppermute | solution.py:388
  98.5 9.5 %collective-permute-start.33 = (bf16[64,1024]{1,0:T(8,128)(2,1)S(1)}, bf16[64,1024]{1,0:T(8,128)(2,1)S(1)}, u32[]{:S(2)}, u32[]{:S(2)}) collective-permute-start(bf16[64,1024]{1,0:T(8,128)(2,1)S(1)} %get-tuple-element.113.after), channel_id=1, source_target_pairs={{0,1},{1,4},{2,3},{3,6},{4,5},{5,0},{6,7},{7,2},{8,9},{9,12},{10,1... | collective-permute-start | bytes 393224 | tf_op jit(solution)/shard_map/ppermute | solution.py:509
  100.6 7.4 %collective-permute-start.34 = (bf16[64,1024]{1,0:T(8,128)(2,1)S(1)}, bf16[64,1024]{1,0:T(8,128)(2,1)S(1)}, u32[]{:S(2)}, u32[]{:S(2)}) collective-permute-start(bf16[64,1024]{1,0:T(8,128)(2,1)S(1)} %get-tuple-element.113.after), channel_id=1, source_target_pairs={{0,4},{4,0},{8,12},{12,8},{1,5},{5,1},{9,13},{13,9},{2,6},{6,2},{1... | collective-permute-start | bytes 393224 | tf_op jit(solution)/shard_map/ppermute | solution.py:388
  103.9 6.3 %collective-permute-start.30 = (bf16[64,1024]{1,0:T(8,128)(2,1)S(1)}, bf16[64,1024]{1,0:T(8,128)(2,1)S(1)}, u32[]{:S(2)}, u32[]{:S(2)}) collective-permute-start(bf16[64,1024]{1,0:T(8,128)(2,1)S(1)} %get-tuple-element.118.after), channel_id=1, source_target_pairs={{0,1},{1,4},{2,3},{3,6},{4,5},{5,0},{6,7},{7,2},{8,9},{9,12},{10,1... | collective-permute-start | bytes 393224 | tf_op jit(solution)/shard_map/ppermute | solution.py:509
  104.0 6.3 %collective-permute-start.31 = (bf16[64,1024]{1,0:T(8,128)(2,1)S(1)}, bf16[64,1024]{1,0:T(8,128)(2,1)S(1)}, u32[]{:S(2)}, u32[]{:S(2)}) collective-permute-start(bf16[64,1024]{1,0:T(8,128)(2,1)S(1)} %get-tuple-element.118.after), channel_id=1, source_target_pairs={{0,4},{4,0},{8,12},{12,8},{1,5},{5,1},{9,13},{13,9},{2,6},{6,2},{1... | collective-permute-start | bytes 393224 | tf_op jit(solution)/shard_map/ppermute | solution.py:388
  (15 other events, 67.4 us)

commit v5 on v4

--- a/solution.py
+++ b/solution.py
@@ -132,7 +132,7 @@
         pltpu.make_async_copy(self.slots.at[spot], self.slots.at[spot], self.sems.at[spot]).wait()
 
 
-def first_kernel(tile_map, place, blocks, dual, cost, lower, upper, code, weights, *refs):
+def first_kernel(tile_map, place, blocks, dual, cost, lower, upper, code, weights, kind, *refs):
     mine, others, vectors = refs[0], refs[1 : 1 + BATCHES], refs[1 + BATCHES]
     states = refs[2 + BATCHES : 2 + 2 * BATCHES]
     slots, sems, order, vector, acc, start, sem = refs[2 + 2 * BATCHES :]
@@ -161,6 +161,7 @@
     flags = jnp.zeros(lane.shape, jnp.int32)
     for t in range(tile_map.shape[0] * tile_map.shape[1]):
         flags = jnp.where(lane == t, tile_map[t // tile_map.shape[1], t % tile_map.shape[1]], flags)
+    flags = jnp.where(lax.broadcasted_iota(jnp.int32, lane.shape, 0) == 1, kind[...], flags)
     others[0][size:, : lane.shape[1]] = flags.astype(f32)
 
 
@@ -276,29 +277,29 @@
         out[...] = turned[b * size : (b + 1) * size]
 
 
-def rows_kernel(place, dual, right, kind, got_dual, got_right, got_kind, after, floor, *refs):
+def rows_kernel(place, dual, right, got_dual, got_right, kind, other, after, floor, *refs):
     outs, (held, sems) = refs[: 2 * BATCHES], refs[2 * BATCHES :]
     size = outs[0].shape[0]
     width = size * BATCHES
     rows = dual.shape[0]
     here = pl.ds(pl.multiple_of(place[1] * width, width), width)
 
-    def put(dual, right, kind):
+    def put(dual, right, one_sided):
         copies = [
             pltpu.make_async_copy(dual.at[:, here], held.at[pl.ds(0, rows)], sems.at[0]),
             pltpu.make_async_copy(right.at[:, here], held.at[pl.ds(rows, rows)], sems.at[1]),
         ]
         for copy in copies:
             copy.start()
-        floor[...] = jnp.where(kind[...] == 1, 0.0, -jnp.inf)
+        floor[...] = jnp.where(one_sided, 0.0, -jnp.inf)
         for k, copy in enumerate(copies):
             copy.wait()
             turned = held[k * rows : (k + 1) * rows].T
             for b in range(BATCHES):
                 outs[k * BATCHES + b][...] = turned[b * size : (b + 1) * size]
 
-    pl.when(place[0] % 2 == 0)(lambda: put(dual, right, kind))
-    pl.when(place[0] % 2 == 1)(lambda: put(got_dual, got_right, got_kind))
+    pl.when(place[0] % 2 == 0)(lambda: put(dual, right, kind[...] == 1))
+    pl.when(place[0] % 2 == 1)(lambda: put(got_dual, got_right, other[size + 1 : size + 2, :rows] == 1.0))
 
 
 def put_half(out, core, parts):
@@ -313,31 +314,39 @@
     put_half(out, 1 - place[1], theirs)
 
 
-def dual_out_kernel(place, own, got_step, partner_step, got_before, partner_before, after, *refs):
-    out = refs[-1]
-
-    def put(mine, theirs):
-        rows = jnp.concatenate([mine(), theirs()], axis=0).T
-        if len(refs) == 1:
-            out[...] = rows
-            return
-        before = refs[0][...]
-        width = before.shape[1]
-        low = lax.broadcasted_iota(jnp.int32, before.shape, 1) < width // 2
-        out[:, pl.ds(pl.multiple_of(place[1] * width, width), width)] = jnp.where(
-            low, before, pltpu.roll(rows, width // 2, 1)
+def last_rows(place, own, got_step, partner_step, got_before, partner_before):
+    rows = own.shape[1]
+    even = place[0] % 2 == 0
+    step = got_step[...].astype(f32)
+    mine = jnp.where(even, own[...], got_before[:, :rows].astype(f32) + step)
+    return mine, partner_before[...].astype(f32) + jnp.where(even, step, partner_step[...].astype(f32))
+
+
+def dual_part_kernel(place, *refs):
+    refs[-1][...] = jnp.concatenate(last_rows(place, *refs[:5]), axis=0).T
+
+
+def dual_out_kernel(place, *refs):
+    part, out, block, sems = refs[-4:]
+    both = jnp.concatenate(last_rows(place, *refs[:5]), axis=0)
+    rows, width = part.shape
+    chunk = rows // sems.shape[0]
+    low = lax.broadcasted_iota(jnp.int32, (chunk, width), 1) < width // 2
+    copies = []
+    for k in range(sems.shape[0]):
+        here = pl.ds(k * chunk, chunk)
+        before = part[here]
+        turned = both[:, k * chunk : (k + 1) * chunk].T
+        block[here, pl.ds(pl.multiple_of(place[1] * width, width), width)] = jnp.where(
+            low, before, pltpu.roll(turned, width // 2, 1)
         )
-        out[:, pl.ds(pl.multiple_of((1 - place[1]) * width, width), width)] = jnp.where(
-            low, pltpu.roll(before, width // 2, 1), rows
+        block[here, pl.ds(pl.multiple_of((1 - place[1]) * width, width), width)] = jnp.where(
+            low, pltpu.roll(before, width // 2, 1), turned
         )
-
-    def moved(before, step):
-        return before[:, : step.shape[1]].astype(f32) + step[...].astype(f32)
-
-    even = (lambda: own[...]), (lambda: moved(partner_before, got_step))
-    odd = (lambda: moved(got_before, got_step)), (lambda: moved(partner_before, partner_step))
-    pl.when(place[0] % 2 == 0)(lambda: put(*even))
-    pl.when(place[0] % 2 == 1)(lambda: put(*odd))
+        copies.append(pltpu.make_async_copy(block.at[here], out.at[here], sems.at[k]))
+        copies[-1].start()
+    for copy in copies:
+        copy.wait()
 
 
 def call(kernel, out_shape, in_specs, scratch=(), flops=0, name=None, vmem=6, out_specs=None):
@@ -405,9 +414,9 @@
         pltpu.with_memory_space_constraint(value, pltpu.HBM)
         for value in (blocks, tile_map, primal_start, dual_start, right_side)
     )
-    vectors = [
+    vectors_in = [
         pltpu.with_memory_space_constraint(value[None, :], pltpu.HBM)
-        for value in (cost_vector, lower_bound, upper_bound, bound_code, primal_weight)
+        for value in (cost_vector, lower_bound, upper_bound, bound_code, primal_weight, row_kind)
     ]
     partner = to_core(blocks)
     mine, *rest = call(
@@ -417,7 +426,7 @@
         + (shape(size, cols),) * (BATCHES - 1)
         + (shape(8, cols),)
         + (shape(size, TAIL),) * BATCHES,
-        [SMEM, SMEM, HBM, HBM] + [VMEM] * 5,
+        [SMEM, SMEM, HBM, HBM] + [VMEM] * 6,
         [
             pltpu.VMEM((n_own, size_r, size_c), bf16),
             pltpu.SemaphoreType.DMA((n_own,)),
@@ -434,12 +443,11 @@
         place,
         blocks,
         dual_start,
-        *vectors,
+        *vectors_in,
     )
     others = [to_core(other) for other in rest[:BATCHES]]
     vectors, state = rest[BATCHES], list(rest[BATCHES + 1 :])
-    sides = dual_start, right_side, row_kind[None, :]
-    sides += tuple(to_core(value) for value in sides)
+    sides = dual_start, right_side, to_core(dual_start), to_core(right_side)
 
     def half_msg(tail):
         return shape(size, rows + (TAIL if tail else 0), bf16)
@@ -558,14 +566,14 @@
             slots, turned, order = load(
                 True, partner, (others[0], slots, turned), [VMEM, ANY, ANY], {3: 0, 4: 1}
             )
-        if (b, iteration, stage) == (0, 0, forward):
+        if (b, iteration, stage) == (1, 0, forward):
             floor, *held = call(
                 rows_kernel,
                 (shape(1, rows),) + (shape(size, rows),) * (2 * BATCHES),
-                [SMEM] + [HBM, HBM, VMEM] * 2 + [ANY],
+                [SMEM] + [HBM] * 2 + [ANY] * 2 + [VMEM] * 2 + [ANY],
                 [pltpu.VMEM((2 * rows, width), f32), pltpu.SemaphoreType.DMA((2,))],
                 name="turn_rows",
-            )(place, *sides, token)
+            )(place, *sides, vectors_in[-1], others[0], token)
             dual, right = held[:BATCHES], held[BATCHES:]
         if (b, iteration, stage) == (BATCHES - 1, ITERS - 1, pair):
             primal_final, token = call(
@@ -575,13 +583,20 @@
                 name="primal_out",
             )(place, *primal, *[to_core(p) for p in primal], token)
 
-    def dual_out(b, out_shape, flops, name, *others):
-        return call(
-            dual_out_kernel, out_shape, [SMEM] + [VMEM] * 5 + [ANY] + [VMEM] * len(others), flops=flops, name=name
-        )(place, dual[b], *steps[b], halves[b][1], partner_before[b], token, *others)
-
-    first_rows = dual_out(0, shape(rows, 2 * size), STAGE_FLOPS, "dual_part")
-    dual_final = dual_out(1, shape(rows, profiles), 0, "dual_out", first_rows)
+    def last_operands(b):
+        return place, dual[b], *steps[b], halves[b][1], partner_before[b]
+
+    part = call(
+        dual_part_kernel, shape(rows, width), [SMEM] + [VMEM] * 5 + [ANY], flops=STAGE_FLOPS, name="dual_part"
+    )(*last_operands(0), token)
+    dual_final = call(
+        dual_out_kernel,
+        pltpu.HBM((rows, profiles), f32),
+        [SMEM] + [VMEM] * 6,
+        [pltpu.VMEM((rows, profiles), f32), pltpu.SemaphoreType.DMA((4,))],
+        name="dual_out",
+        out_specs=HBM,
+    )(*last_operands(1), part)
     return primal_final, dual_final
 
 

time: 114 us -> 118 us (1.035); the launches traced: 112 us -> 119 us
  waiting for transfers between devices: 27.7 us -> 44.9 us
  starting transfers between devices: 44.2 us -> 35 us
    ppermute x16, waiting for transfers between devices: 19.9 us -> 31 us  [to_z(): return lax.ppermute(value, 'col', [(i, i ^ k) for i in range(count)])]
    ppermute x12 -> x11, starting transfers between devices: 24.4 us -> 19.6 us  [to_core(): return lax.ppermute(value, 'row', [(i, i ^ 1) for i in range(2 * near)])]
    ppermute x6, waiting for transfers between devices: 4.76 us -> 8.1 us  [to_x(): return lax.ppermute(value, 'row', [(i, i ^ 2 * k) for i in range(2 * near)])]
    ppermute x2, waiting for transfers between devices: 1.48 us -> 4.4 us  [update(): steps[b] = (lax.ppermute(msg, ('row', 'col'), to_holder), to_core(msg))]
    ppermute x6, starting transfers between devices: 3.64 us -> 1.63 us  [to_x(): return lax.ppermute(value, 'row', [(i, i ^ 2 * k) for i in range(2 * near)])]
    ppermute x2, starting transfers between devices: 2.12 us -> 0.68 us  [update(): steps[b] = (lax.ppermute(msg, ('row', 'col'), to_holder), to_core(msg))]
  transfers between devices with their start and end apart: 36 -> 35, of which waited for: 16 -> 19; matrix products, arithmetic and copies ran while one was open for 0% -> 0% of each run, Pallas kernels for 32% -> 29%
where the time goes in v5:
time: 118 us; the launch traced here: 119 us
  waiting for transfers between devices  44.9 us (38%)
  Pallas kernels  36.6 us (31%)
  starting transfers between devices  35 us (30%)
  local copies, waits for them, and re-layouts  1.31 us (1%)
    ppermute x16, waiting for transfers between devices, to_z(): return lax.ppermute(value, 'col', [(i, i ^ k) for i in range(count)])  31 us
    ppermute x11, starting transfers between devices, to_core(): return lax.ppermute(value, 'row', [(i, i ^ 1) for i in range(2 * near)])  19.6 us
    ppermute x16, starting transfers between devices, to_z(): return lax.ppermute(value, 'col', [(i, i ^ k) for i in range(count)])  13.1 us
    pallas_call x6, Pallas kernels, forward(): call(functools.partial(forward_kernel, grid_cols, near, first, last, tota...  10.6 us
    ppermute x6, waiting for transfers between devices, to_x(): return lax.ppermute(value, 'row', [(i, i ^ 2 * k) for i in range(2 * near)])  8.1 us
    pallas_call x2, Pallas kernels, load(): pl.pallas_call(functools.partial(load_kernel, second), out_shape=loaded,...  5.87 us
    pallas_call x4, Pallas kernels, back(): call(functools.partial(back_kernel, grid_cols), (shape(size, cols + TAIL,...  5.76 us
    ppermute x2, waiting for transfers between devices, update(): steps[b] = (lax.ppermute(msg, ('row', 'col'), to_holder), to_core(msg))  4.4 us
  transfers between devices with their start and end apart: 35, of which 19 were waited for; matrix products, arithmetic and copies ran while one was open for 0% of the time, Pallas kernels for 29%

profile of v5, /device:TPU:5, one launch (start us, length us, event | category | flops | bytes accessed | tf_op | source)
XLA Modules:
  0.0 119.1 jit_solution(7234879009425466134)
XLA Ops:
  1.4 3.1 %first_product.1 = (f32[128,2048]{1,0:T(8,128)S(1)}, f32[72,2048]{1,0:T(8,128)S(1)}, f32[64,2048]{1,0:T(8,128)S(1)}, f32[8,2048]{1,0:T(8,128)S(1)}, f32[64,128]{1,0:T(8,128)S(1)}, /*index=5*/f32[64,128]{1,0:T(8,128)S(1)}) custom-call(s32[2,4]{1,0:T(2,128)} %tile_map.5, s32[2]{0:T(128)S(1)} %pad_add_fusion.place, bf16[1024,2048]{1,0:T(8,128)(2,1)} %source.1, ...), custom_call_target="tpu_custom_call" | custom-call | tf_op jit(solution)/shard_map/first_product/pallas_call | solution.py:422
  5.4 2.2 %turn_primal.1 = (f32[64,2048]{1,0:T(8,128)S(1)}, f32[64,2048]{1,0:T(8,128)S(1)}) custom-call(s32[2]{0:T(128)S(1)} %pad_add_fusion.place, f32[2048,256]{1,0:T(8,128)} %value.1, f32[64,128]{1,0:T(8,128)S(1)} %get-tuple-element.64.after.refs_4_), custom_call_target="tpu_custom_call" | custom-call | tf_op jit(solution)/shard_map/turn_primal/pallas_call | solution.py:553
  11.5 2.6 %load_blocks.2 = (bf16[16,512,512]{2,1,0:T(8,128)(2,1)S(1)}, bf16[16,512,512]{2,1,0:T(8,128)(2,1)S(1)}, s32[17]{0:T(128)}) custom-call(s32[2,4]{1,0:T(2,128)} %tile_map.5, bf16[1024,2048]{1,0:T(8,128)(2,1)} %source.1, bf16[64,2048]{1,0:T(8,128)(2,1)S(1)} %first_pack.2.refs_0_.refs_6_), custom_call_target="tpu_custom_call" | custom-call | tf_op jit(solution)/shard_map/load_blocks/pallas_call | solution.py:539
  14.1 3.3 %load_blocks.3 = (bf16[16,512,512]{2,1,0:T(8,128)(2,1)S(1)}, bf16[16,512,512]{2,1,0:T(8,128)(2,1)S(1)}, s32[17]{0:T(128)S(1)}) custom-call(s32[2,4]{1,0:T(2,128)} %tile_map.5, bf16[1024,2048]{1,0:T(8,128)(2,1)} %collective-permute-done.source, f32[72,2048]{1,0:T(8,128)S(1)} %collective-permute-done.1.other.refs_0_, ...), custom_call_target="tpu_custom_call", output_to_operand_aliasing={{0}: (3, {}), {1}: (4, {})} | custom-call | tf_op jit(solution)/shard_map/load_blocks/pallas_call | solution.py:539
  20.9 3.2 %collective-permute-done.3.got = bf16[64,1024]{1,0:T(8,128)(2,1)S(1)} collective-permute-done((bf16[64,1024]{1,0:T(8,128)(2,1)S(1)}, bf16[64,1024]{1,0:T(8,128)(2,1)S(1)}, u32[]{:S(2)}, u32[]{:S(2)}) %collective-permute-start.3) | collective-permute-done | bytes 131104 | tf_op jit(solution)/shard_map/ppermute | solution.py:403
  24.3 3.9 %collective-permute-done.8.refs_1_ = bf16[64,2048]{1,0:T(8,128)(2,1)S(1)} collective-permute-done((bf16[64,2048]{1,0:T(8,128)(2,1)S(1)}, bf16[64,2048]{1,0:T(8,128)(2,1)S(1)}, u32[]{:S(2)}, u32[]{:S(2)}) %collective-permute-start.8) | collective-permute-done | bytes 262176 | tf_op jit(solution)/shard_map/ppermute | solution.py:400
  31.3 2.2 %turn_rows.1 = (f32[1,1024]{1,0:T(1,128)S(1)}, f32[64,1024]{1,0:T(8,128)S(1)}, f32[64,1024]{1,0:T(8,128)S(1)}, f32[64,1024]{1,0:T(8,128)S(1)}, f32[64,1024]{1,0:T(8,128)S(1)}) custom-call(s32[2]{0:T(128)S(1)} %pad_add_fusion.place, f32[1024,256]{1,0:T(8,128)} %dual.3, f32[1024,256]{1,0:T(8,128)} %right.1, f32[1024,256]{1,0:T(8,128)} %copy-done.2, ...), custom_call_target="tpu_custom_call" | custom-call | tf_op jit(solution)/shard_map/turn_rows/pallas_call | solution.py:570
  39.8 5.4 %collective-permute-done.12.got = bf16[64,1152]{1,0:T(8,128)(2,1)S(1)} collective-permute-done((bf16[64,1152]{1,0:T(8,128)(2,1)S(1)}, bf16[64,1152]{1,0:T(8,128)(2,1)S(1)}, u32[]{:S(2)}, u32[]{:S(2)}) %collective-permute-start.12) | collective-permute-done | bytes 147488 | tf_op jit(solution)/shard_map/ppermute | solution.py:403
  45.5 1.8 %forward_product.8 = (f32[64,2048]{1,0:T(8,128)S(1)}, f32[64,1024]{1,0:T(8,128)S(1)}, bf16[64,1024]{1,0:T(8,128)(2,1)S(1)}, f32[64,128]{1,0:T(8,128)S(1)}) custom-call(s32[17]{0:T(128)S(1)} %get-tuple-element.68.order, s32[2]{0:T(128)S(1)} %pad_add_fusion.place, bf16[64,2176]{1,0:T(8,128)(2,1)S(1)} %back_product.4.before_ref.after_ref.refs_0_, ...), custom_call_target="tpu_custom_call" | custom-call | flops 4000000000 | tf_op jit(solution)/shard_map/forward_product/pallas_call | solution.py:482
  51.0 1.8 %collective-permute-done.13.got = bf16[64,1024]{1,0:T(8,128)(2,1)S(1)} collective-permute-done((bf16[64,1024]{1,0:T(8,128)(2,1)S(1)}, bf16[64,1024]{1,0:T(8,128)(2,1)S(1)}, u32[]{:S(2)}, u32[]{:S(2)}) %collective-permute-start.13) | collective-permute-done | bytes 131104 | tf_op jit(solution)/shard_map/ppermute | solution.py:403
  53.0 3.4 %collective-permute-done.16.refs_1_ = bf16[64,2176]{1,0:T(8,128)(2,1)S(1)} collective-permute-done((bf16[64,2176]{1,0:T(8,128)(2,1)S(1)}, bf16[64,2176]{1,0:T(8,128)(2,1)S(1)}, u32[]{:S(2)}, u32[]{:S(2)}) %collective-permute-start.16) | collective-permute-done | bytes 278560 | tf_op jit(solution)/shard_map/ppermute | solution.py:400
  56.4 1.8 %forward_product.9 = (f32[64,2048]{1,0:T(8,128)S(1)}, f32[64,1024]{1,0:T(8,128)S(1)}, bf16[64,1024]{1,0:T(8,128)(2,1)S(1)}, f32[64,128]{1,0:T(8,128)S(1)}) custom-call(s32[17]{0:T(128)S(1)} %get-tuple-element.68.order, s32[2]{0:T(128)S(1)} %pad_add_fusion.place, bf16[64,2176]{1,0:T(8,128)(2,1)S(1)} %back_product.5.after.refs_0_, ...), custom_call_target="tpu_custom_call" | custom-call | flops 4000000000 | tf_op jit(solution)/shard_map/forward_product/pallas_call | solution.py:482
  60.1 3.6 %collective-permute-done.18.got = bf16[64,1024]{1,0:T(8,128)(2,1)S(1)} collective-permute-done((bf16[64,1024]{1,0:T(8,128)(2,1)S(1)}, bf16[64,1024]{1,0:T(8,128)(2,1)S(1)}, u32[]{:S(2)}, u32[]{:S(2)}) %collective-permute-start.18) | collective-permute-done | bytes 131104 | tf_op jit(solution)/shard_map/ppermute | solution.py:403
  66.8 3.1 %collective-permute-done.20.got = bf16[64,1152]{1,0:T(8,128)(2,1)S(1)} collective-permute-done((bf16[64,1152]{1,0:T(8,128)(2,1)S(1)}, bf16[64,1152]{1,0:T(8,128)(2,1)S(1)}, u32[]{:S(2)}, u32[]{:S(2)}) %collective-permute-start.20) | collective-permute-done | bytes 147488 | tf_op jit(solution)/shard_map/ppermute | solution.py:403
  72.2 1.9 %forward_product.10 = (f32[64,2048]{1,0:T(8,128)S(1)}, f32[64,1024]{1,0:T(8,128)S(1)}, bf16[64,1024]{1,0:T(8,128)(2,1)S(1)}, f32[64,128]{1,0:T(8,128)S(1)}) custom-call(s32[17]{0:T(128)S(1)} %get-tuple-element.68.order, s32[2]{0:T(128)S(1)} %pad_add_fusion.place, bf16[64,2176]{1,0:T(8,128)(2,1)S(1)} %get-tuple-element.98.before_ref.after_ref.refs_0_, ...), custom_call_target="tpu_custom_call" | custom-call | flops 4000000000 | tf_op jit(solution)/shard_map/forward_product/pallas_call | solution.py:482
  76.7 13.0 %collective-permute-start.24 = (f32[64,2048]{1,0:T(8,128)S(1)}, f32[64,2048]{1,0:T(8,128)S(1)}, u32[]{:S(2)}, u32[]{:S(2)}) collective-permute-start(f32[64,2048]{1,0:T(8,128)S(1)} %get-tuple-element.102.refs_0_), channel_id=1, source_target_pairs={{0,4},{4,0},{8,12},{12,8},{1,5},{5,1},{9,13},{13,9},{2,6},{6,2},{1... | collective-permute-start | bytes 1572872 | tf_op jit(solution)/shard_map/ppermute | solution.py:397
  89.8 3.5 %collective-permute-start.27 = (bf16[64,1024]{1,0:T(8,128)(2,1)S(1)}, bf16[64,1024]{1,0:T(8,128)(2,1)S(1)}, u32[]{:S(2)}, u32[]{:S(2)}) collective-permute-start(bf16[64,1024]{1,0:T(8,128)(2,1)S(1)} %pair_sum.10.refs_6_.own), channel_id=1, source_target_pairs={{0,2},{1,3},{2,0},{3,1},{4,6},{5,7},{6,4},{7,5},{8,10},{9,11},{10,... | collective-permute-start | bytes 393224 | tf_op jit(solution)/shard_map/ppermute | solution.py:403
  93.2 1.7 %forward_product.11 = (f32[64,2048]{1,0:T(8,128)S(1)}, f32[64,1024]{1,0:T(8,128)S(1)}, bf16[64,1024]{1,0:T(8,128)(2,1)S(1)}, f32[64,128]{1,0:T(8,128)S(1)}) custom-call(s32[17]{0:T(128)S(1)} %get-tuple-element.68.order, s32[2]{0:T(128)S(1)} %pad_add_fusion.place, bf16[64,2176]{1,0:T(8,128)(2,1)S(1)} %get-tuple-element.104.after.refs_0_, ...), custom_call_target="tpu_custom_call" | custom-call | flops 4000000000 | tf_op jit(solution)/shard_map/forward_product/pallas_call | solution.py:482
  96.5 3.5 %collective-permute-done.27.got = bf16[64,1024]{1,0:T(8,128)(2,1)S(1)} collective-permute-done((bf16[64,1024]{1,0:T(8,128)(2,1)S(1)}, bf16[64,1024]{1,0:T(8,128)(2,1)S(1)}, u32[]{:S(2)}, u32[]{:S(2)}) %collective-permute-start.27) | collective-permute-done | bytes 131104 | tf_op jit(solution)/shard_map/ppermute | solution.py:403
  100.1 2.7 %collective-permute-done.26.got = bf16[64,1024]{1,0:T(8,128)(2,1)S(1)} collective-permute-done((bf16[64,1024]{1,0:T(8,128)(2,1)S(1)}, bf16[64,1024]{1,0:T(8,128)(2,1)S(1)}, u32[]{:S(2)}, u32[]{:S(2)}) %collective-permute-start.26) | collective-permute-done | bytes 131104 | tf_op jit(solution)/shard_map/ppermute | solution.py:403
  105.8 2.5 %primal_out.1 = (f32[2048,256]{1,0:T(8,128)}, f32[8,128]{1,0:T(8,128)S(1)}) custom-call(s32[2]{0:T(128)S(1)} %pad_add_fusion.place, f32[64,2048]{1,0:T(8,128)S(1)} %get-tuple-element.102.refs_0_, f32[64,2048]{1,0:T(8,128)S(1)} %get-tuple-element.108.refs_1_, f32[64,2048]{1,0:T(8,128)S(1)} %collective-permute-done.24.refs_2_, ...), custom_call_target="tpu_custom_call" | custom-call | tf_op jit(solution)/shard_map/primal_out/pallas_call | solution.py:579
  108.3 2.8 %collective-permute-done.28.got = bf16[64,1024]{1,0:T(8,128)(2,1)S(1)} collective-permute-done((bf16[64,1024]{1,0:T(8,128)(2,1)S(1)}, bf16[64,1024]{1,0:T(8,128)(2,1)S(1)}, u32[]{:S(2)}, u32[]{:S(2)}) %collective-permute-start.28) | collective-permute-done | bytes 131104 | tf_op jit(solution)/shard_map/ppermute | solution.py:403
  113.6 3.5 %collective-permute-done.29.refs_1_ = bf16[64,1024]{1,0:T(8,128)(2,1)S(1)} collective-permute-done((bf16[64,1024]{1,0:T(8,128)(2,1)S(1)}, bf16[64,1024]{1,0:T(8,128)(2,1)S(1)}, u32[]{:S(2)}, u32[]{:S(2)}) %collective-permute-start.29) | collective-permute-done | bytes 131104 | tf_op jit(solution)/shard_map/ppermute | solution.py:517
  117.1 1.8 %dual_out.1 = f32[1024,256]{1,0:T(8,128)} custom-call(s32[2]{0:T(128)S(1)} %pad_add_fusion.place, f32[64,1024]{1,0:T(8,128)S(1)} %get-tuple-element.117.refs_0_, bf16[64,1024]{1,0:T(8,128)(2,1)S(1)} %collective-permute-done.29.refs_1_, bf16[64,1024]{1,0:T(8,128)(2,1)S(1)} %collective-permute-done.30.refs_2_, ...), custom_call_target="tpu_custom_call" | custom-call | tf_op jit(solution)/shard_map/dual_out/pallas_call | solution.py:592
  (87 shorter events, 39.7 us)
Async XLA Ops:
  0.6 13.5 %collective-permute-start = (bf16[1024,2048]{1,0:T(8,128)(2,1)}, bf16[1024,2048]{1,0:T(8,128)(2,1)}, u32[]{:S(2)}, u32[]{:S(2)}) collective-permute-start(bf16[1024,2048]{1,0:T(8,128)(2,1)} %source.1), channel_id=1, source_target_pairs={{0,4},{4,0},{8,12},{12,8},{1,5},{5,1},{9,13},{13,9},{2,6},{6,2},{1... | collective-permute-start | bytes 12582920 | tf_op jit(solution)/shard_map/ppermute | solution.py:397
  9.1 8.3 %collective-permute-start.2 = (bf16[64,2048]{1,0:T(8,128)(2,1)S(1)}, bf16[64,2048]{1,0:T(8,128)(2,1)S(1)}, u32[]{:S(2)}, u32[]{:S(2)}) collective-permute-start(bf16[64,2048]{1,0:T(8,128)(2,1)S(1)} %first_pack.2.refs_0_.refs_6_), channel_id=1, source_target_pairs={{0,8},{4,12},{8,0},{12,4},{1,9},{5,13},{9,1},{13,5},{2,10},{6,14},... | collective-permute-start | bytes 786440 | tf_op jit(solution)/shard_map/ppermute | solution.py:400
  10.4 10.4 %collective-permute-start.4 = (f32[64,2048]{1,0:T(8,128)S(1)}, f32[64,2048]{1,0:T(8,128)S(1)}, u32[]{:S(2)}, u32[]{:S(2)}) collective-permute-start(f32[64,2048]{1,0:T(8,128)S(1)} %get-tuple-element.74), channel_id=1, source_target_pairs={{0,4},{4,0},{8,12},{12,8},{1,5},{5,1},{9,13},{13,9},{2,6},{6,2},{1... | collective-permute-start | bytes 1572872 | tf_op jit(solution)/shard_map/ppermute | solution.py:397
  11.0 19.0 %collective-permute-start.6 = (f32[1024,256]{1,0:T(8,128)S(1)}, f32[1024,256]{1,0:T(8,128)S(1)}, u32[]{:S(2)}, u32[]{:S(2)}) collective-permute-start(f32[1024,256]{1,0:T(8,128)S(1)} %copy-done), channel_id=1, source_target_pairs={{0,4},{4,0},{8,12},{12,8},{1,5},{5,1},{9,13},{13,9},{2,6},{6,2},{1... | collective-permute-start | bytes 3145736 | tf_op jit(solution)/shard_map/ppermute | solution.py:397
  11.0 19.0 %collective-permute-start.7 = (f32[1024,256]{1,0:T(8,128)S(1)}, f32[1024,256]{1,0:T(8,128)S(1)}, u32[]{:S(2)}, u32[]{:S(2)}) collective-permute-start(f32[1024,256]{1,0:T(8,128)S(1)} %copy-done.1), channel_id=1, source_target_pairs={{0,4},{4,0},{8,12},{12,8},{1,5},{5,1},{9,13},{13,9},{2,6},{6,2},{1... | collective-permute-start | bytes 3145736 | tf_op jit(solution)/shard_map/ppermute | solution.py:397
  20.8 7.4 %collective-permute-start.8 = (bf16[64,2048]{1,0:T(8,128)(2,1)S(1)}, bf16[64,2048]{1,0:T(8,128)(2,1)S(1)}, u32[]{:S(2)}, u32[]{:S(2)}) collective-permute-start(bf16[64,2048]{1,0:T(8,128)(2,1)S(1)} %first_pack.3.after.refs_0_), channel_id=1, source_target_pairs={{0,8},{4,12},{8,0},{12,4},{1,9},{5,13},{9,1},{13,5},{2,10},{6,14},... | collective-permute-start | bytes 786440 | tf_op jit(solution)/shard_map/ppermute | solution.py:400
  24.2 9.4 %collective-permute-start.5 = (bf16[64,1152]{1,0:T(8,128)(2,1)S(1)}, bf16[64,1152]{1,0:T(8,128)(2,1)S(1)}, u32[]{:S(2)}, u32[]{:S(2)}) collective-permute-start(bf16[64,1152]{1,0:T(8,128)(2,1)S(1)} %pair_sum.6.refs_6_.own), channel_id=1, source_target_pairs={{0,2},{1,3},{2,0},{3,1},{4,6},{5,7},{6,4},{7,5},{8,10},{9,11},{10,... | collective-permute-start | bytes 442376 | tf_op jit(solution)/shard_map/ppermute | solution.py:403
  29.9 6.6 %collective-permute-start.10 = (bf16[64,1024]{1,0:T(8,128)(2,1)S(1)}, bf16[64,1024]{1,0:T(8,128)(2,1)S(1)}, u32[]{:S(2)}, u32[]{:S(2)}) collective-permute-start(bf16[64,1024]{1,0:T(8,128)(2,1)S(1)} %get-tuple-element.84), channel_id=1, source_target_pairs={{0,1},{1,0},{2,3},{3,2},{4,5},{5,4},{6,7},{7,6},{8,9},{9,8},{10,11... | collective-permute-start | bytes 393224 | tf_op jit(solution)/shard_map/ppermute | solution.py:403
  36.6 8.6 %collective-permute-start.12 = (bf16[64,1152]{1,0:T(8,128)(2,1)S(1)}, bf16[64,1152]{1,0:T(8,128)(2,1)S(1)}, u32[]{:S(2)}, u32[]{:S(2)}) collective-permute-start(bf16[64,1152]{1,0:T(8,128)(2,1)S(1)} %pair_sum.7.after.own), channel_id=1, source_target_pairs={{0,2},{1,3},{2,0},{3,1},{4,6},{5,7},{6,4},{7,5},{8,10},{9,11},{10,... | collective-permute-start | bytes 442376 | tf_op jit(solution)/shard_map/ppermute | solution.py:403
  39.7 5.8 %collective-permute-start.11 = (bf16[64,2176]{1,0:T(8,128)(2,1)S(1)}, bf16[64,2176]{1,0:T(8,128)(2,1)S(1)}, u32[]{:S(2)}, u32[]{:S(2)}) collective-permute-start(bf16[64,2176]{1,0:T(8,128)(2,1)S(1)} %back_product.4.before_ref.after_ref.refs_0_), channel_id=1, source_target_pairs={{0,8},{4,12},{8,0},{12,4},{1,9},{5,13},{9,1},{13,5},{2,10},{6,14},... | collective-permute-start | bytes 835592 | tf_op jit(solution)/shard_map/ppermute | solution.py:400
  52.9 6.4 %collective-permute-start.15 = (bf16[64,1152]{1,0:T(8,128)(2,1)S(1)}, bf16[64,1152]{1,0:T(8,128)(2,1)S(1)}, u32[]{:S(2)}, u32[]{:S(2)}) collective-permute-start(bf16[64,1152]{1,0:T(8,128)(2,1)S(1)} %pair_sum.8.refs_6_.own), channel_id=1, source_target_pairs={{0,2},{1,3},{2,0},{3,1},{4,6},{5,7},{6,4},{7,5},{8,10},{9,11},{10,... | collective-permute-start | bytes 442376 | tf_op jit(solution)/shard_map/ppermute | solution.py:403
  63.8 6.1 %collective-permute-start.20 = (bf16[64,1152]{1,0:T(8,128)(2,1)S(1)}, bf16[64,1152]{1,0:T(8,128)(2,1)S(1)}, u32[]{:S(2)}, u32[]{:S(2)}) collective-permute-start(bf16[64,1152]{1,0:T(8,128)(2,1)S(1)} %pair_sum.9.after.own), channel_id=1, source_target_pairs={{0,2},{1,3},{2,0},{3,1},{4,6},{5,7},{6,4},{7,5},{8,10},{9,11},{10,... | collective-permute-start | bytes 442376 | tf_op jit(solution)/shard_map/ppermute | solution.py:403
  74.1 15.6 %collective-permute-start.23 = (bf16[64,1024]{1,0:T(8,128)(2,1)S(1)}, bf16[64,1024]{1,0:T(8,128)(2,1)S(1)}, u32[]{:S(2)}, u32[]{:S(2)}) collective-permute-start(bf16[64,1024]{1,0:T(8,128)(2,1)S(1)} %get-tuple-element.107), channel_id=1, source_target_pairs={{0,1},{1,0},{2,3},{3,2},{4,5},{5,4},{6,7},{7,6},{8,9},{9,8},{10,11... | collective-permute-start | bytes 393224 | tf_op jit(solution)/shard_map/ppermute | solution.py:403
  76.6 16.6 %collective-permute-start.22 = (bf16[64,2176]{1,0:T(8,128)(2,1)S(1)}, bf16[64,2176]{1,0:T(8,128)(2,1)S(1)}, u32[]{:S(2)}, u32[]{:S(2)}) collective-permute-start(bf16[64,2176]{1,0:T(8,128)(2,1)S(1)} %get-tuple-element.104.after.refs_0_), channel_id=1, source_target_pairs={{0,8},{4,12},{8,0},{12,4},{1,9},{5,13},{9,1},{13,5},{2,10},{6,14},... | collective-permute-start | bytes 835592 | tf_op jit(solution)/shard_map/ppermute | solution.py:400
  76.7 27.7 %collective-permute-start.24 = (f32[64,2048]{1,0:T(8,128)S(1)}, f32[64,2048]{1,0:T(8,128)S(1)}, u32[]{:S(2)}, u32[]{:S(2)}) collective-permute-start(f32[64,2048]{1,0:T(8,128)S(1)} %get-tuple-element.102.refs_0_), channel_id=1, source_target_pairs={{0,4},{4,0},{8,12},{12,8},{1,5},{5,1},{9,13},{13,9},{2,6},{6,2},{1... | collective-permute-start | bytes 1572872 | tf_op jit(solution)/shard_map/ppermute | solution.py:397
  89.8 10.2 %collective-permute-start.27 = (bf16[64,1024]{1,0:T(8,128)(2,1)S(1)}, bf16[64,1024]{1,0:T(8,128)(2,1)S(1)}, u32[]{:S(2)}, u32[]{:S(2)}) collective-permute-start(bf16[64,1024]{1,0:T(8,128)(2,1)S(1)} %pair_sum.10.refs_6_.own), channel_id=1, source_target_pairs={{0,2},{1,3},{2,0},{3,1},{4,6},{5,7},{6,4},{7,5},{8,10},{9,11},{10,... | collective-permute-start | bytes 393224 | tf_op jit(solution)/shard_map/ppermute | solution.py:403
  95.0 7.8 %collective-permute-start.26 = (bf16[64,1024]{1,0:T(8,128)(2,1)S(1)}, bf16[64,1024]{1,0:T(8,128)(2,1)S(1)}, u32[]{:S(2)}, u32[]{:S(2)}) collective-permute-start(bf16[64,1024]{1,0:T(8,128)(2,1)S(1)} %get-tuple-element.111), channel_id=1, source_target_pairs={{0,1},{1,0},{2,3},{3,2},{4,5},{5,4},{6,7},{7,6},{8,9},{9,8},{10,11... | collective-permute-start | bytes 393224 | tf_op jit(solution)/shard_map/ppermute | solution.py:403
  95.5 9.5 %collective-permute-start.25 = (f32[64,2048]{1,0:T(8,128)S(1)}, f32[64,2048]{1,0:T(8,128)S(1)}, u32[]{:S(2)}, u32[]{:S(2)}) collective-permute-start(f32[64,2048]{1,0:T(8,128)S(1)} %get-tuple-element.108.refs_1_), channel_id=1, source_target_pairs={{0,4},{4,0},{8,12},{12,8},{1,5},{5,1},{9,13},{13,9},{2,6},{6,2},{1... | collective-permute-start | bytes 1572872 | tf_op jit(solution)/shard_map/ppermute | solution.py:397
  102.8 8.2 %collective-permute-start.28 = (bf16[64,1024]{1,0:T(8,128)(2,1)S(1)}, bf16[64,1024]{1,0:T(8,128)(2,1)S(1)}, u32[]{:S(2)}, u32[]{:S(2)}) collective-permute-start(bf16[64,1024]{1,0:T(8,128)(2,1)S(1)} %pair_sum.11.refs_4_.own), channel_id=1, source_target_pairs={{0,2},{1,3},{2,0},{3,1},{4,6},{5,7},{6,4},{7,5},{8,10},{9,11},{10,... | collective-permute-start | bytes 393224 | tf_op jit(solution)/shard_map/ppermute | solution.py:403
  102.9 8.4 %collective-permute-start.34 = (bf16[64,1024]{1,0:T(8,128)(2,1)S(1)}, bf16[64,1024]{1,0:T(8,128)(2,1)S(1)}, u32[]{:S(2)}, u32[]{:S(2)}) collective-permute-start(bf16[64,1024]{1,0:T(8,128)(2,1)S(1)} %get-tuple-element.121), channel_id=1, source_target_pairs={{0,4},{4,0},{8,12},{12,8},{1,5},{5,1},{9,13},{13,9},{2,6},{6,2},{1... | collective-permute-start | bytes 393224 | tf_op jit(solution)/shard_map/ppermute | solution.py:397
  104.4 9.2 %collective-permute-start.31 = (bf16[64,1024]{1,0:T(8,128)(2,1)S(1)}, bf16[64,1024]{1,0:T(8,128)(2,1)S(1)}, u32[]{:S(2)}, u32[]{:S(2)}) collective-permute-start(bf16[64,1024]{1,0:T(8,128)(2,1)S(1)} %get-tuple-element.119), channel_id=1, source_target_pairs={{0,4},{4,0},{8,12},{12,8},{1,5},{5,1},{9,13},{13,9},{2,6},{6,2},{1... | collective-permute-start | bytes 393224 | tf_op jit(solution)/shard_map/ppermute | solution.py:397
  104.4 8.4 %collective-permute-start.32 = (bf16[64,1024]{1,0:T(8,128)(2,1)S(1)}, bf16[64,1024]{1,0:T(8,128)(2,1)S(1)}, u32[]{:S(2)}, u32[]{:S(2)}) collective-permute-start(bf16[64,1024]{1,0:T(8,128)(2,1)S(1)} %get-tuple-element.113.after), channel_id=1, source_target_pairs={{0,1},{1,4},{2,3},{3,6},{4,5},{5,0},{6,7},{7,2},{8,9},{9,12},{10,1... | collective-permute-start | bytes 393224 | tf_op jit(solution)/shard_map/ppermute | solution.py:517
  105.0 7.8 %collective-permute-start.33 = (bf16[64,1024]{1,0:T(8,128)(2,1)S(1)}, bf16[64,1024]{1,0:T(8,128)(2,1)S(1)}, u32[]{:S(2)}, u32[]{:S(2)}) collective-permute-start(bf16[64,1024]{1,0:T(8,128)(2,1)S(1)} %get-tuple-element.113.after), channel_id=1, source_target_pairs={{0,4},{4,0},{8,12},{12,8},{1,5},{5,1},{9,13},{13,9},{2,6},{6,2},{1... | collective-permute-start | bytes 393224 | tf_op jit(solution)/shard_map/ppermute | solution.py:397
  111.2 5.9 %collective-permute-start.29 = (bf16[64,1024]{1,0:T(8,128)(2,1)S(1)}, bf16[64,1024]{1,0:T(8,128)(2,1)S(1)}, u32[]{:S(2)}, u32[]{:S(2)}) collective-permute-start(bf16[64,1024]{1,0:T(8,128)(2,1)S(1)} %get-tuple-element.118.refs_5_), channel_id=1, source_target_pairs={{0,1},{1,4},{2,3},{3,6},{4,5},{5,0},{6,7},{7,2},{8,9},{9,12},{10,1... | collective-permute-start | bytes 393224 | tf_op jit(solution)/shard_map/ppermute | solution.py:517
  (15 other events, 69.9 us)
